TPU v7x, 128 devices: a whole 4x4x4 slice. The times are simulated.
128 devices in a mesh: ctx: 16 (over y, x), cmp: 8 (over z, core).
Axes of the slice: x: 4, y: 4, z: 4, core: 2. Of those that a mesh axis runs over, the one named last changes fastest.
Arguments:
- hidden_in: bfloat16 [2, 16384, 4096], P(None, 'ctx', 'cmp'), may hold values from -6 to 6
- route_index: int32 [2, 16, 128], P(None, 'ctx'), may hold values from 0 to 1023, as said below
- norm_gain: float32 [4096], replicated, may hold values from 0.1 to 1.9
- w_qkv: bfloat16 [4096, 32, 3, 128], P(None, 'ctx')
- w_out: bfloat16 [32, 128, 4096], P('ctx'), may hold values from -0.09375 to 0.09375
- cotangent: bfloat16 [2, 16384, 4096], P(None, 'ctx', 'cmp'), may hold values from -6 to 6
Outputs:
- hidden_out: bfloat16 [2, 16384, 4096], P(None, 'ctx', 'cmp')
- grad_in: bfloat16 [2, 16384, 4096], P(None, 'ctx', 'cmp')
- grad_gain: float32 [4096], replicated
- grad_w_qkv: bfloat16 [4096, 32, 3, 128], P('cmp', 'ctx')
- grad_w_out: bfloat16 [32, 128, 4096], P('ctx', None, 'cmp')
Inputs may be any that keep to these rules, and one draw needn't show every extreme that they name: `route_index`: in each slab and block the 128 offsets are distinct and increasing; the first block of every slab holds offsets 0 and 1023.
All inputs are finite; a program needn't handle non-finite values.
Results may differ from a plain program's by a relative error of at most 0.025.
Values may be sent and summed in bfloat16 or wider, within the bound.
No kernel may reach another device: no remote copies, remote signals or barrier semaphores. Data moves between devices by JAX's collectives and lax.ppermute only.
A program may use at most 192 MiB of HBM per device.

v0:
```python
import jax
import jax.numpy as jnp
import numpy as np
from jax import lax
from jax.experimental import pallas as pl
from jax.experimental.pallas import tpu as pltpu
from jax.sharding import PartitionSpec as P

THETA = 500000.0
EPS = 1e-05
BOTH = ("ctx", "cmp")
EXTRA = 128
BF = jnp.bfloat16
F32 = jnp.float32


def ring_pairs(second, shift):
    pairs = []
    for y in range(4):
        for x in range(4):
            for z in range(4):
                for c in range(2):
                    along_x = (c == 0) != second
                    ty, tx = (y, (x - shift) % 4) if along_x else ((y - shift) % 4, x)
                    pairs.append(((y * 4 + x) * 8 + z * 2 + c, (ty * 4 + tx) * 8 + z * 2 + c))
    return pairs


def ring(values, second, shift):
    return lax.ppermute(values, BOTH, ring_pairs(second, shift))


def send_z(values, shift):
    return lax.ppermute(
        values, "cmp", [(z * 2 + c, ((z + shift) % 4) * 2 + c) for z in range(4) for c in range(2)]
    )


def swap_core(values):
    return lax.ppermute(values, "cmp", [(k, k ^ 1) for k in range(8)])


def swap_chip(values):
    return lax.ppermute(values, "cmp", [(k, k ^ 2) for k in range(8)])


def dyn(values, index, axis=0):
    return lax.dynamic_index_in_dim(values, index, axis, keepdims=False)


WHOLE = pl.BlockSpec(memory_space=pltpu.VMEM)
SMEM = pl.BlockSpec(memory_space=pltpu.SMEM)
ANY = pl.BlockSpec(memory_space=pl.ANY)
WIDE = 4096 + EXTRA
LAST = (((1,), (1,)), ((), ()))
ROWS = (((0,), (0,)), ((), ()))


def shape(*dims, dtype=BF):
    return jax.ShapeDtypeStruct(dims, dtype)


ORDER = []


def call(kernel, name, out_shape, room=8, after=(), **options):
    def invoke(*operands):
        tokens = ORDER[-1:] + list(after)
        count, skip = len(operands), len(tokens)

        def body(*refs):
            kernel(*refs[:count], *refs[count + skip :])

        out = pl.pallas_call(
            body,
            out_shape=out_shape,
            compiler_params=pltpu.CompilerParams(vmem_limit_bytes=room * 2**20),
            cost_estimate=pl.CostEstimate(flops=1, bytes_accessed=1, transcendentals=0),
            name=name,
            **{**options, "in_specs": options["in_specs"] + [ANY] * skip},
        )(*operands, *tokens)
        results = out if isinstance(out, (list, tuple)) else [out]
        ORDER.append(min(results, key=lambda r: r.size))
        return out

    return invoke


def unpack_kernel(w, out):
    row = lax.broadcasted_iota(jnp.int32, (192, 192), 0)
    column = lax.broadcasted_iota(jnp.int32, (192, 192), 1)
    hot = (column == lax.rem(row, 32) * 6 + lax.div(row, 32)).astype(F32).astype(BF)
    rows = jnp.concatenate([w[k * 192 : k * 192 + 192] for k in range(32)], 1)
    moved = jnp.dot(hot, rows, preferred_element_type=F32).astype(BF)
    for k in range(32):
        for p in range(6):
            out[k * 32 : k * 32 + 32, p * 128 : p * 128 + 128] = moved[
                p * 32 : p * 32 + 32, k * 128 : k * 128 + 128
            ]


def unpack_weights(w):
    return call(
        unpack_kernel,
        "unpack_weights",
        shape(4096, 768),
        room=12,
        grid=(4,),
        in_specs=[pl.BlockSpec((6144, 128), lambda i: (i, 0))],
        out_specs=pl.BlockSpec((1024, 768), lambda i: (i, 0)),
    )(w)


def pick_kernel(where, index, hidden, cotangent, o0, o1, o2, o3, picked):
    s = pl.program_id(0)
    token = lax.broadcasted_iota(jnp.int32, (1024, 128), 0)
    hot = (token == index[0]).astype(F32).astype(BF)
    for i, source in enumerate((hidden, cotangent)):
        rows = lax.dot_general(hot, source[0], ROWS, preferred_element_type=F32).astype(BF)
        picked[2 * s, :, i] = rows[:64].reshape(2, 32, 512)
        picked[2 * s + 1, :, i] = rows[64:].reshape(2, 32, 512)

    @pl.when(s == 1)
    def _():
        for d, out in enumerate((o0, o1, o2, o3)):
            out[...] = picked[lax.rem(where[0] + d, 4)]


def pick_rows(where, index, hidden, cotangent):
    block = pl.BlockSpec((1, 1024, 512), lambda s: (s, 0, 0))
    return call(
        pick_kernel,
        "pick_rows",
        [shape(2, 2, 32, 512)] * 4,
        room=12,
        grid=(2,),
        in_specs=[SMEM, pl.BlockSpec((1, 1, 128), lambda s: (s, 0, 0)), block, block],
        out_specs=[pl.BlockSpec((2, 2, 32, 512), lambda s: (0, 0, 0, 0))] * 4,
        scratch_shapes=[pltpu.VMEM((4, 2, 2, 32, 512), BF)],
    )(where, index, hidden, cotangent)


def other_core_kernel(where, p0, p1, p2, p3, out):
    for d, piece in enumerate((p0, p1, p2, p3)):
        out[d] = piece[1 - where[1]]


def norm_kernel(where, p0, p1, p2, p3, other, gain, places, both, rows):
    z, core = where[0], where[1]
    for d, piece in enumerate((p0, p1, p2, p3)):
        chip = lax.rem(z - d + 4, 4) * 2
        for source, index, part in ((piece, core, core), (other, d, 1 - core)):
            at = pl.multiple_of((chip + part) * 512, 512)
            rows[:, pl.ds(at, 512)] = source[index, 0]
            both[:, pl.ds(WIDE + at, 512)] = source[index, 1]
    x = rows[...].astype(F32)
    inverse = lax.rsqrt(jnp.mean(x * x, -1, keepdims=True) + EPS)
    both[:, :4096] = (x * inverse * gain[...]).astype(BF)
    both[:, 4096:WIDE] = places[...]


def own_rows(where, pieces, gain, places):
    other = swap_core(
        call(
            other_core_kernel,
            "rows_of_other_core",
            shape(4, 2, 32, 512),
            in_specs=[SMEM] + [WHOLE] * 4,
            out_specs=WHOLE,
        )(where, *pieces)
    )
    return call(
        norm_kernel,
        "norm_rows",
        [shape(32, WIDE + 4096), shape(32, 4096)],
        in_specs=[SMEM] + [WHOLE] * 7,
        out_specs=[WHOLE] * 2,
    )(where, *pieces, other, gain, places)


def stack_x_kernel(p0, p1, p2, p3, low, high):
    for i, piece in enumerate((p0, p1, p2, p3)):
        out = low if i < 2 else high
        out[i % 2 * 32 : i % 2 * 32 + 32] = piece[:, :WIDE]


def stack_g_kernel(p0, p1, p2, p3, out):
    for i, piece in enumerate((p0, p1, p2, p3)):
        out[i * 32 : i * 32 + 32] = piece[:, WIDE:]


def halves_kernel(plus, minus, first, second):
    first[...] = plus[:64]
    second[...] = minus[64:]


def gather_first(own):
    return [own] + [ring(own, False, shift) for shift in (1, 2, 3)]


def gather_x(pieces):
    low, high = call(
        stack_x_kernel,
        "stack_x",
        [shape(64, WIDE)] * 2,
        in_specs=[WHOLE] * 4,
        out_specs=[WHOLE] * 2,
    )(*pieces)
    plus_low, minus_high = ring(low, True, 1), ring(high, True, 3)
    plus_high, minus_low = ring(high, True, 1), ring(low, True, 3)
    far_low, far_high = ring(plus_low, True, 1), ring(minus_high, True, 3)
    return [low, high, plus_low, plus_high, far_low, far_high, minus_low, minus_high]


def gather_g(pieces, after):
    column = call(
        stack_g_kernel,
        "stack_g",
        shape(128, 4096),
        after=after,
        in_specs=[WHOLE] * 4,
        out_specs=WHOLE,
    )(*pieces)
    return column, ring(column, True, 1), ring(column, True, 3)


def gather_g_far(column, plus, minus):
    first, second = call(
        halves_kernel,
        "halves_g",
        [shape(64, 4096)] * 2,
        in_specs=[WHOLE] * 2,
        out_specs=[WHOLE] * 2,
    )(plus, minus)
    return [column, plus, ring(first, True, 1), ring(second, True, 3), minus]


def add_kernel(a, ta, b, tb, out_a, out_b):
    out_a[...] = a[...] + ta[...]
    out_b[...] = b[...] + tb[...]


def sum_column_kernel(own, u_low, u_high, v_low, v_high, *outs):
    for half, u, v in ((0, u_low, v_low), (64, u_high, v_high)):
        for i in range(2):
            rows = slice(i * 32, i * 32 + 32)
            first = own[half + i * 32 : half + i * 32 + 32].astype(F32)
            total = first + u[rows].astype(F32) + v[rows].astype(F32)
            outs[half // 32 + i][...] = total.astype(BF)


def reduce_start(parts):
    own, plus_low, plus_high, far_low, far_high, minus_low, minus_high = parts
    to_plus, to_minus = ring(far_low, True, 3), ring(far_high, True, 1)
    u_high, v_low = ring(plus_high, True, 3), ring(minus_low, True, 1)
    return own, plus_low, to_plus, minus_high, to_minus, u_high, v_low


def reduce_add(state, name):
    own, plus_low, to_plus, minus_high, to_minus, u_high, v_low = state
    plus, minus = call(
        add_kernel,
        name + "_add",
        [shape(*plus_low.shape)] * 2,
        in_specs=[WHOLE] * 4,
        out_specs=[WHOLE] * 2,
    )(plus_low, to_plus, minus_high, to_minus)
    return own, ring(plus, True, 3), u_high, v_low, ring(minus, True, 1)


def reduce_column(terms, name):
    width = terms[0].shape[1]
    parts = call(
        sum_column_kernel,
        name + "_column",
        [shape(32, width)] * 4,
        in_specs=[WHOLE] * 5,
        out_specs=[WHOLE] * 4,
    )(*terms)
    return [parts[0]] + [ring(parts[i], False, 4 - i) for i in (1, 2, 3)]


X_PIECES = (64,) * 8
G_PIECES = (128, 128, 64, 64, 128)
PARTS = (128, 64, 64, 64, 64, 64, 64)


def joined(refs, columns=slice(None)):
    return jnp.concatenate([r[:, columns] for r in refs], 0)


def tile(index, size):
    return pl.ds(pl.multiple_of(index * size, size), size)


def spread(outs, values, columns=slice(None)):
    row = 0
    for out in outs:
        count = out.shape[0]
        out[:, columns] = values[row : row + count]
        row += count


def turn_tables():
    frequency = THETA ** (-2.0 * np.arange(64) / 128)
    out = np.zeros((128, 3, 3, 128))
    for part, (first, count, step) in enumerate(((0, 32, 32), (32, 32, 1), (64, 16, 1024))):
        angles = np.arange(count)[:, None] * step * frequency
        rest = np.concatenate([np.cos(angles), np.sin(angles)], 1)
        for term in range(3):
            low = rest.astype(BF).astype(np.float64)
            out[first : first + count, part, term] = low
            rest = rest - low
    return out.reshape(128, 9 * 128).astype(BF)


def place_weights():
    out = np.zeros((8, 128))
    out[0, :32] = np.arange(32) * 32
    out[0, 32:64] = np.arange(32)
    out[0, 64:80] = np.arange(16) * 1024
    return out.astype(BF)


def project_kernel(*refs):
    x, (w, turns, weights, q, kv, table, total) = refs[:8], refs[8:]
    total[...] = jnp.zeros_like(total)

    @pl.loop(0, 4)
    def _(i):
        columns = tile(i, 1024)
        total[...] += jnp.dot(joined(x, columns), w[columns, :], preferred_element_type=F32)

    code = joined(x, slice(4096, WIDE))
    turned = jnp.dot(code, turns[...], preferred_element_type=F32)
    parts = []
    for part in range(3):
        at = part * 384
        both = turned[:, at : at + 128] + turned[:, at + 128 : at + 256] + turned[:, at + 256 : at + 384]
        parts.append((both[:, :64], both[:, 64:]))
    (ca, sa), (cb, sb), (cc, sc) = parts
    ca, sa = ca * cb - sa * sb, sa * cb + ca * sb
    ca, sa = ca * cc - sa * sc, sa * cc + ca * sc
    cosine, sine = jnp.concatenate([ca, ca], 1), jnp.concatenate([-sa, sa], 1)
    table[:, :128] = cosine
    table[:, 128:256] = sine
    place = lax.dot_general(code, weights[...], LAST, preferred_element_type=F32)
    table[:, 256:] = jnp.broadcast_to(place[:, :1], (512, 128))
    row = lax.dot_general(weights[...], code, LAST, preferred_element_type=F32)[:1]
    high = jnp.floor(row * (1.0 / 128)) * 128.0
    kv[512:, :] = jnp.concatenate([high, row - high, jnp.zeros((14, 512), F32)], 0).astype(BF)
    for h in range(2):
        u = total[:, h * 128 : h * 128 + 128]
        q[:, h * 128 : h * 128 + 128] = (u * cosine + pltpu.roll(u, 64, 1) * sine).astype(BF)
        u = total[:, 256 + h * 128 : 384 + h * 128]
        kv[:512, h * 256 : h * 256 + 128] = (u * cosine + pltpu.roll(u, 64, 1) * sine).astype(BF)
        kv[:512, h * 256 + 128 : h * 256 + 256] = total[:, 512 + h * 128 : 640 + h * 128].astype(BF)


def project(x, w):
    return call(
        project_kernel,
        "project",
        [shape(512, 256), shape(528, 512), shape(512, 384, dtype=F32)],
        room=24,
        in_specs=[WHOLE] * 11,
        out_specs=[WHOLE] * 3,
        scratch_shapes=[pltpu.VMEM((512, 768), F32)],
    )(*x, w, jnp.asarray(turn_tables()), jnp.asarray(place_weights()))


def output_kernel(att, w, *outs):
    @pl.loop(0, 8)
    def _(i):
        columns = tile(i, 512)
        part = jnp.dot(att[...], w[:, columns], preferred_element_type=F32).astype(BF)
        spread(outs, part, columns)


def output_parts(att, w):
    return call(
        output_kernel,
        "output_parts",
        [shape(n, 4096) for n in PARTS],
        room=12,
        in_specs=[WHOLE] * 2,
        out_specs=[WHOLE] * 7,
    )(att, w)


def grad_attended_kernel(g0, g1, g2, g3, g4, w, out, total):
    total[...] = jnp.zeros_like(total)

    @pl.loop(0, 4)
    def _(i):
        columns = tile(i, 1024)
        total[...] += lax.dot_general(
            joined((g0, g1, g2, g3, g4), columns), w[:, columns], LAST, preferred_element_type=F32
        )

    out[...] = total[...].astype(BF)


def attended_grad(g, w):
    return call(
        grad_attended_kernel,
        "grad_attended",
        shape(512, 256),
        room=12,
        in_specs=[WHOLE] * 6,
        out_specs=WHOLE,
        scratch_shapes=[pltpu.VMEM((512, 256), F32)],
    )(*g, w)


def forward_kernel(q, kv0, kv1, kv2, kv3, table, out, probs):
    factor = 128 ** (-0.5) * 1.4426950408889634
    key_places = [kv[512:513, :].astype(F32) + kv[513:514, :].astype(F32) for kv in (kv0, kv1, kv2, kv3)]

    @pl.loop(0, 4)
    def _(step):
        rows = tile(step, 128)
        place = table[rows, 256:257]
        for h in range(2):
            query = q[rows, h * 128 : h * 128 + 128]
            scores = []
            for i, kv in enumerate((kv0, kv1, kv2, kv3)):
                key = kv[:512, h * 256 : h * 256 + 128]
                s = lax.dot_general(query, key, LAST, preferred_element_type=F32)
                scores.append(jnp.where(place >= key_places[i], s, -jnp.inf))
            top = jnp.maximum(jnp.maximum(scores[0], scores[1]), jnp.maximum(scores[2], scores[3]))
            top = jnp.max(top, -1, keepdims=True)
            exps = [jnp.exp2((s - top) * factor) for s in scores]
            inverse = 1.0 / jnp.sum((exps[0] + exps[1]) + (exps[2] + exps[3]), -1, keepdims=True)
            total = None
            for i, kv in enumerate((kv0, kv1, kv2, kv3)):
                p = (exps[i] * inverse).astype(BF)
                probs[h, rows, i * 512 : (i + 1) * 512] = p
                value = kv[:512, h * 256 + 128 : h * 256 + 256]
                part = jnp.dot(p, value, preferred_element_type=F32)
                total = part if total is None else total + part
            out[rows, h * 128 : h * 128 + 128] = total.astype(BF)


def attend(q, pieces, table):
    return call(
        forward_kernel,
        "attention_forward",
        [shape(512, 256), shape(2, 512, 2048)],
        room=16,
        in_specs=[WHOLE] * 6,
        out_specs=[WHOLE] * 2,
    )(q, *pieces, table)


def backward_kernel(q, kv0, kv1, kv2, kv3, probs, grad, att, table, gq, near, mid, sent):
    scale = 128 ** (-0.5)
    places = ((near, 0), (sent, 512), (mid, 0), (sent, 0))
    for h in range(2):
        head = slice(h * 128, h * 128 + 128)
        g = grad[:, head]
        delta = jnp.sum(g.astype(F32) * att[:, head].astype(F32), -1, keepdims=True)
        total = None
        for i, kv in enumerate((kv0, kv1, kv2, kv3)):
            p = probs[h, :, i * 512 : (i + 1) * 512]
            key, value = kv[:512, h * 256 : h * 256 + 128], kv[:512, h * 256 + 128 : h * 256 + 256]
            dp = lax.dot_general(g, value, LAST, preferred_element_type=F32)
            ds = (p.astype(F32) * (dp - delta)).astype(BF)
            part = jnp.dot(ds, key, preferred_element_type=F32)
            total = part if total is None else total + part
            dk = lax.dot_general(ds, q[:, head], ROWS, preferred_element_type=F32) * scale
            dv = lax.dot_general(p, g, ROWS, preferred_element_type=F32)
            out, row = places[i]
            out[row : row + 512, h * 256 : h * 256 + 128] = dk.astype(BF)
            out[row : row + 512, h * 256 + 128 : h * 256 + 256] = dv.astype(BF)
        u = total * scale
        gq[:, head] = (u * table[:, :128] - pltpu.roll(u, 64, 1) * table[:, 128:256]).astype(BF)


def attend_back(q, pieces, probs, grad, att, table):
    return call(
        backward_kernel,
        "attention_backward",
        [shape(512, 256), shape(512, 512), shape(512, 512), shape(1024, 512)],
        room=20,
        in_specs=[WHOLE] * 9,
        out_specs=[WHOLE] * 4,
    )(q, *pieces, probs, grad, att, table)


def chip_sum_kernel(mid, recv, out):
    out[...] = mid[...] + recv[:512]


def chip_sum(mid, recv):
    return call(
        chip_sum_kernel,
        "chip_sum",
        shape(512, 512),
        in_specs=[WHOLE] * 2,
        out_specs=WHOLE,
    )(mid, recv)


def feature_kernel(near, recv, chip, gq, table, *refs):
    x, w, gain, gp, gp_kv, parts, ride = refs[:8], refs[8], refs[9], refs[10], refs[11], refs[12:19], refs[19]
    own = near[...].astype(F32) + recv[512:].astype(F32) + chip[...].astype(F32)
    gp[:, :256] = gq[...]
    for h in range(2):
        u = own[:, h * 256 : h * 256 + 128]
        u = u * table[:, :128] - pltpu.roll(u, 64, 1) * table[:, 128:256]
        gp[:, 256 + h * 128 : 384 + h * 128] = u.astype(BF)
        gp[:, 512 + h * 128 : 640 + h * 128] = own[:, h * 256 + 128 : h * 256 + 256].astype(BF)
    gp_kv[...] = gp[:, 256:].T

    @pl.loop(0, 8)
    def _(step):
        columns = tile(step, 512)
        values = lax.dot_general(gp[...], w[columns, :], LAST, preferred_element_type=F32)
        weight = jnp.sum(values * joined(x, columns).astype(F32), 0, keepdims=True) / gain[:, columns]
        for j in range(4):
            ride[pl.ds(step * 4 + j, 1), :] = weight[:, j * 128 : (j + 1) * 128]
        spread(parts, values.astype(BF), columns)

    for part in parts:
        for r in range(0, part.shape[0], 32):
            part[r : r + 32, 4096:] = ride[...].astype(BF)


def feature_parts(near, recv, chip, gq, table, x, w, gain):
    out = call(
        feature_kernel,
        "feature_parts",
        [shape(512, 768), shape(512, 512)] + [shape(n, WIDE) for n in PARTS],
        room=26,
        in_specs=[WHOLE] * 15,
        out_specs=[WHOLE] * 9,
        scratch_shapes=[pltpu.VMEM((32, 128), F32)],
    )(near, recv, chip, gq, table, *x, w, gain)
    return out[1], out[2:]


def query_weight_kernel(where, *refs):
    x, g, (gq, att, kept, sent, left) = refs[:8], refs[8:13], refs[13:]
    left[:256] = gq[...].T
    left[256:] = att[...].T

    @pl.loop(0, 8)
    def _(i):
        slot = lax.rem(i, 4)
        core = jnp.where(i < 4, 1 - where[1], where[1])
        columns = tile(lax.rem(where[0] + slot, 4) * 2 + core, 512)
        a = jnp.dot(left[:256], joined(x, columns), preferred_element_type=F32)
        b = jnp.dot(left[256:], joined(g, columns), preferred_element_type=F32)

        @pl.when(i < 4)
        def _():
            sent[slot, :256] = a.astype(BF)
            sent[slot, 256:] = b.astype(BF)

        @pl.when(i >= 4)
        def _():
            kept[slot, :256] = a.astype(BF)
            kept[slot, 256:] = b.astype(BF)


def query_weights(where, x, g, gq, att):
    return call(
        query_weight_kernel,
        "query_weights",
        [shape(4, 512, 512)] * 2,
        room=20,
        in_specs=[SMEM] + [WHOLE] * 15,
        out_specs=[WHOLE] * 2,
        scratch_shapes=[pltpu.VMEM((512, 512), BF)],
    )(where, *x, *g, gq, att)


def key_weight_kernel(where, *refs):
    x, (left, kept, sent) = refs[:8], refs[8:]

    @pl.loop(0, 8)
    def _(i):
        slot = lax.rem(i, 4)
        core = jnp.where(i < 4, 1 - where[1], where[1])
        columns = tile(lax.rem(where[0] + slot, 4) * 2 + core, 512)
        a = jnp.dot(left[...], joined(x, columns), preferred_element_type=F32).astype(BF)

        @pl.when(i < 4)
        def _():
            sent[slot] = a

        @pl.when(i >= 4)
        def _():
            kept[slot] = a


def key_weights(where, x, left):
    return call(
        key_weight_kernel,
        "key_weights",
        [shape(4, 512, 512)] * 2,
        room=16,
        in_specs=[SMEM] + [WHOLE] * 9,
        out_specs=[WHOLE] * 2,
    )(where, *x, left)


def sum_cores_kernel(a, b, own, plus_low, plus_high, far_low, far_high, minus_low, minus_high):
    own[...] = a[0] + b[0]
    outs = ((plus_low, plus_high), (far_low, far_high), (minus_low, minus_high))
    for d, (low, high) in enumerate(outs):
        low[...] = a[d + 1, :256] + b[d + 1, :256]
        high[...] = a[d + 1, 256:] + b[d + 1, 256:]


def sum_cores(keep, recv, name):
    parts = call(
        sum_cores_kernel,
        name + "_cores",
        [shape(n, 512) for n in (512,) + (256,) * 6],
        in_specs=[WHOLE] * 2,
        out_specs=[WHOLE] * 7,
    )(keep, recv)
    return parts, send_z(parts[3], 1), send_z(parts[4], 3)


def join_kernel(plus_low, to_plus, plus_high, minus_low, minus_high, to_minus, out_a, out_b):
    out_a[:256] = plus_low[...] + to_plus[...]
    out_a[256:] = plus_high[...]
    out_b[:256] = minus_low[...]
    out_b[256:] = minus_high[...] + to_minus[...]


def sum_near(state, name):
    parts, to_plus, to_minus = state
    plus, minus = call(
        join_kernel,
        name + "_near",
        [shape(512, 512)] * 2,
        in_specs=[WHOLE] * 6,
        out_specs=[WHOLE] * 2,
    )(parts[1], to_plus, parts[2], parts[5], parts[6], to_minus)
    return parts[0], send_z(plus, 1), send_z(minus, 3)


def sum_weights_kernel(a0, a1, a2, b0, b1, b2, in_grad, out_grad):
    a = a0[...].astype(F32) + a1[...].astype(F32) + a2[...].astype(F32)
    b = b0[...].astype(F32) + b1[...].astype(F32) + b2[...].astype(F32)
    in_grad[:, :256] = a[:256].astype(BF).T
    in_grad[:, 256:] = b.astype(BF).T
    out_grad[...] = a[256:].astype(BF)


def sum_weights(a, b):
    return call(
        sum_weights_kernel,
        "sum_weights",
        [shape(512, 768), shape(256, 512)],
        room=12,
        in_specs=[WHOLE] * 6,
        out_specs=[WHOLE] * 2,
    )(*a, *b)


def grad_rows_kernel(where, own, u, t, v, rows, gain, o0, o1, o2, o3, total):
    x = rows[...].astype(F32)
    inverse = lax.rsqrt(jnp.mean(x * x, -1, keepdims=True) + EPS)
    unit = x * inverse
    s = (own[...].astype(F32) + u[...].astype(F32)) + (t[...].astype(F32) + v[...].astype(F32))
    scaled = s[:, :4096] * gain[...]
    total[...] = (inverse * (scaled - unit * jnp.mean(scaled * unit, -1, keepdims=True))).astype(BF)
    for d, out in enumerate((o0, o1, o2, o3)):
        start = pl.multiple_of(lax.rem(where[0] + d, 4) * 1024, 1024)
        out[:, :1024] = total[:, pl.ds(start, 1024)]
        out[:, 1024:] = s[:, 4096:].astype(BF)


def out_rows_kernel(where, own, u, t, v, o0, o1, o2, o3, total):
    s = (own[...].astype(F32) + u[...].astype(F32)) + (t[...].astype(F32) + v[...].astype(F32))
    total[...] = s.astype(BF)
    for d, out in enumerate((o0, o1, o2, o3)):
        start = pl.multiple_of(lax.rem(where[0] + d, 4) * 1024, 1024)
        out[...] = total[:, pl.ds(start, 1024)]


def split_rows(kernel, name, where, operands, width):
    parts = call(
        kernel,
        name,
        [shape(32, width)] * 4,
        in_specs=[SMEM] + [WHOLE] * len(operands),
        out_specs=[WHOLE] * 4,
        scratch_shapes=[pltpu.VMEM((32, 4096), BF)],
    )(where, *operands)
    return [parts[0]] + [send_z(parts[d], d) for d in (1, 2, 3)]


def columns_kernel(where, p0, p1, p2, p3, out, *gain):
    start = pl.multiple_of((1 - where[1]) * 512, 512)
    pieces = (p0, p1, p2, p3)
    for d, piece in enumerate(pieces):
        out[d, :, :512] = piece[:, pl.ds(start, 512)]
    if gain:
        total = (p0[:, 1024:].astype(F32) + p1[:, 1024:].astype(F32)) + (
            p2[:, 1024:].astype(F32) + p3[:, 1024:].astype(F32)
        )
        high = total.astype(BF)
        out[0, :, 512:] = high
        out[1, :, 512:] = (total - high.astype(F32)).astype(BF)
        out[2, :, 512:] = high
        out[3, :, 512:] = high
        gain[0][...] = total


def place_kernel(where, base, places, p0, p1, p2, p3, other, out, rows):
    step = pl.program_id(0)

    @pl.when(step == 0)
    def _():
        start = pl.multiple_of(where[1] * 512, 512)
        for d, piece in enumerate((p0, p1, p2, p3)):
            rows[d * 32 : d * 32 + 32] = piece[:, pl.ds(start, 512)]
            rows[128 + d * 32 : 160 + d * 32] = other[d, :, :512]

    token = step * 512 + lax.broadcasted_iota(jnp.int32, (512, 256), 0)
    hot = (token == places[...]).astype(F32).astype(BF)
    added = jnp.dot(hot, rows[...], preferred_element_type=F32)
    out[...] = (base[...].astype(F32) + added).astype(BF)


def other_columns(where, pieces, name):
    riding = pieces[0].shape[1] > 1024
    width = 512 + (128 if riding else 0)
    sent = call(
        columns_kernel,
        name + "_columns",
        [shape(4, 32, width)] + ([shape(32, 128, dtype=F32)] if riding else []),
        in_specs=[SMEM] + [WHOLE] * 4,
        out_specs=[WHOLE] * (2 if riding else 1),
    )(where, *pieces)
    return swap_core(sent[0]), sent[1:]


def place_rows(where, base, places, pieces, other, name):
    block = pl.BlockSpec((512, 512), lambda i: (i, 0))
    fixed = lambda i: (0, 0)
    return call(
        place_kernel,
        name + "_placed",
        shape(2048, 512),
        grid=(4,),
        in_specs=[SMEM, block, pl.BlockSpec((1, 256), fixed)]
        + [pl.BlockSpec(pieces[0].shape, fixed)] * 4
        + [pl.BlockSpec(other.shape, lambda i: (0, 0, 0))],
        out_specs=block,
        scratch_shapes=[pltpu.VMEM((256, 512), BF)],
    )(where, base, places, *pieces, other)


def shards(hidden_in, route_index, norm_gain, w_qkv, w_out, cotangent):
    ORDER.clear()
    context = lax.axis_index("ctx")
    device = lax.axis_index("cmp")
    z, core = device // 2, device % 2
    slab, quarter = z // 2, device % 4
    where = jnp.stack([z, core])
    local_index = route_index[:, 0, :]
    gain = norm_gain[None, :]
    w_back = w_out.reshape(256, 4096)

    own_index = dyn(dyn(local_index, slab).reshape(4, 32), quarter)[:, None]
    lane = jnp.arange(EXTRA, dtype=jnp.int32)[None, :]
    code = (lane == own_index // 32) | (lane == own_index % 32 + 32) | (lane == context + 64)
    code = code.astype(F32).astype(BF)

    picked = pick_rows(where, route_index, hidden_in, cotangent)
    picked = [picked[0]] + [send_z(picked[d], d) for d in (1, 2, 3)]
    w_in = unpack_weights(w_qkv.transpose(0, 2, 1, 3).reshape(24576, 128))
    both_own, rows_own = own_rows(where, picked, gain, code)
    column = gather_first(both_own)
    x = gather_x(column)
    g_near = gather_g(column, (x[4], x[5]))

    queries, own_pair, table = project(x, w_in)
    chip_pair = swap_chip(own_pair)
    core_pair = swap_core(own_pair)
    far_pair = swap_core(chip_pair)
    pieces = [own_pair, core_pair, chip_pair, far_pair]
    g = gather_g_far(*g_near)
    attended, probs = attend(queries, pieces, table)

    out_state = reduce_start(output_parts(attended, w_back))
    grad_attended = attended_grad(g, w_back)
    grad_q, near, mid, sent = attend_back(queries, pieces, probs, grad_attended, attended, table)
    recv = swap_core(sent)
    out_terms = reduce_add(out_state, "out")
    chip_part = swap_chip(chip_sum(mid, recv))
    kept_a, sent_a = query_weights(where, x, g, grad_q, attended)
    recv_a = swap_core(sent_a)
    out_column = reduce_column(out_terms, "out")

    gp_kv, parts = feature_parts(near, recv, chip_part, grad_q, table, x, w_in, gain)
    grad_state = reduce_start(parts)
    state_a = sum_cores(kept_a, recv_a, "query")
    out_split = split_rows(out_rows_kernel, "out_rows", where, out_column, 1024)
    grad_terms = reduce_add(grad_state, "grad")
    kept_b, sent_b = key_weights(where, x, gp_kv)
    recv_b = swap_core(sent_b)
    terms_a = sum_near(state_a, "query")
    grad_column = reduce_column(grad_terms, "grad")
    state_b = sum_cores(kept_b, recv_b, "key")
    out_other, _ = other_columns(where, out_split, "out")
    grad_split = split_rows(
        grad_rows_kernel, "grad_rows", where, [*grad_column, rows_own, gain], 1024 + EXTRA
    )

    chips = (z - jnp.arange(4)) % 4
    by_chip = (local_index + jnp.arange(2, dtype=jnp.int32)[:, None] * 1024).reshape(4, 2, 32)
    by_core = jnp.stack([dyn(by_chip, core, 1), dyn(by_chip, 1 - core, 1)])
    places = jnp.stack([dyn(by_core, chips[d], 1) for d in range(4)], 1).reshape(1, 256)
    hidden_out = place_rows(where, hidden_in.reshape(2048, 512), places, out_split, out_other, "out")
    terms_b = sum_near(state_b, "key")
    grad_other, (gain_part,) = other_columns(where, grad_split, "grad")
    grad_in = place_rows(where, cotangent.reshape(2048, 512), places, grad_split, grad_other, "grad")
    grad_gain = gain_part + grad_other[0, :, 512:].astype(F32) + grad_other[1, :, 512:].astype(F32)
    grad_w_qkv, grad_w_out = sum_weights(terms_a, terms_b)
    return (
        hidden_out.reshape(2, 1024, 512),
        grad_in.reshape(2, 1024, 512),
        grad_gain.reshape(4096),
        grad_w_qkv.reshape(512, 3, 2, 128).transpose(0, 2, 1, 3),
        grad_w_out.reshape(2, 128, 512),
    )


def solution(mesh):
    in_specs = (
        P(None, "ctx", "cmp"),
        P(None, "ctx", None),
        P(),
        P(None, "ctx", None, None),
        P("ctx", None, None),
        P(None, "ctx", "cmp"),
    )
    out_specs = (
        P(None, "ctx", "cmp"),
        P(None, "ctx", "cmp"),
        P(),
        P("cmp", "ctx", None, None),
        P("ctx", None, "cmp"),
    )
    return jax.shard_map(shards, mesh=mesh, in_specs=in_specs, out_specs=out_specs, check_vma=False)
```

profile of v0, /device:TPU:1, one launch (start us, length us, event | category | flops | bytes accessed | tf_op | source)
XLA Modules:
  0.0 286.3 jit_solution(16129489511294038265)
XLA Ops:
  27.2 4.7 %collective-permute-done.6.refs_3_ = bf16[32,8320]{1,0:T(8,128)(2,1)S(1)} collective-permute-done((bf16[32,8320]{1,0:T(8,128)(2,1)S(1)}, bf16[32,8320]{1,0:T(8,128)(2,1)S(1)}, u32[]{:S(2)}, u32[]{:S(2)}) %collective-permute-start.6) | collective-permute-done | bytes 532512 | tf_op jit(solution)/shard_map/ppermute | solution.py:30
  31.9 6.9 %collective-permute-done.5.refs_2_ = bf16[32,8320]{1,0:T(8,128)(2,1)S(1)} collective-permute-done((bf16[32,8320]{1,0:T(8,128)(2,1)S(1)}, bf16[32,8320]{1,0:T(8,128)(2,1)S(1)}, u32[]{:S(2)}, u32[]{:S(2)}) %collective-permute-start.5) | collective-permute-done | bytes 532512 | tf_op jit(solution)/shard_map/ppermute | solution.py:30
  41.6 7.0 %collective-permute-done.10.refs_7_.refs_8_.refs_12_ = bf16[64,4224]{1,0:T(8,128)(2,1)S(1)} collective-permute-done((bf16[64,4224]{1,0:T(8,128)(2,1)S(1)}, bf16[64,4224]{1,0:T(8,128)(2,1)S(1)}, u32[]{:S(2)}, u32[]{:S(2)}) %collective-permute-start.10) | collective-permute-done | bytes 540704 | tf_op jit(solution)/shard_map/ppermute | solution.py:30
  52.7 5.6 %collective-permute-done.11.refs_6_.refs_5_.refs_10_ = bf16[64,4224]{1,0:T(8,128)(2,1)S(1)} collective-permute-done((bf16[64,4224]{1,0:T(8,128)(2,1)S(1)}, bf16[64,4224]{1,0:T(8,128)(2,1)S(1)}, u32[]{:S(2)}, u32[]{:S(2)}) %collective-permute-start.11) | collective-permute-done | bytes 540704 | tf_op jit(solution)/shard_map/ppermute | solution.py:30
  64.1 5.3 %project.1 = (bf16[512,256]{1,0:T(8,128)(2,1)S(1)}, bf16[528,512]{1,0:T(8,128)(2,1)S(1)}, f32[512,384]{1,0:T(8,128)S(1)}) custom-call(bf16[64,4224]{1,0:T(8,128)(2,1)S(1)} %get-tuple-element.91.refs_4_.refs_0_.refs_1_.refs_5_, bf16[64,4224]{1,0:T(8,128)(2,1)S(1)} %get-tuple-element.92.refs_1_.refs_2_.refs_6_, ...), custom_call_target="tpu_custom_call" | custom-call | flops 1 | bytes 1 | tf_op jit(solution)/shard_map/project/pallas_call | solution.py:74
  73.2 7.4 %collective-permute-done.14.refs_3_ = bf16[528,512]{1,0:T(8,128)(2,1)S(1)} collective-permute-done((bf16[528,512]{1,0:T(8,128)(2,1)S(1)}, bf16[528,512]{1,0:T(8,128)(2,1)S(1)}, u32[]{:S(2)}, u32[]{:S(2)}) %collective-permute-start.14) | collective-permute-done | bytes 540704 | tf_op jit(solution)/shard_map/ppermute | solution.py:44
  80.5 3.6 %collective-permute-start.15 = (bf16[528,512]{1,0:T(8,128)(2,1)S(1)}, bf16[528,512]{1,0:T(8,128)(2,1)S(1)}, u32[]{:S(2)}, u32[]{:S(2)}) collective-permute-start(bf16[528,512]{1,0:T(8,128)(2,1)S(1)} %collective-permute-done.14.refs_3_), channel_id=1, source_target_pairs={{0,1},{1,0},{2,3},{3,2},{4,5},{5,4},{6,7},{7,6},{8,9},{9,8},{10,11... | collective-permute-start | bytes 1622024 | tf_op jit(solution)/shard_map/ppermute | solution.py:40
  87.4 6.2 %attention_forward.1 = (bf16[512,256]{1,0:T(8,128)(2,1)S(1)}, bf16[2,512,2048]{2,1,0:T(8,128)(2,1)S(1)}) custom-call(bf16[512,256]{1,0:T(8,128)(2,1)S(1)} %get-tuple-element.93.refs_2_.refs_0_, bf16[528,512]{1,0:T(8,128)(2,1)S(1)} %get-tuple-element.94.refs_1_, bf16[528,512]{1,0:T(8,128)(2,1)S(1)} %collective-permute-done.13.refs_2_, ...), custom_call_target="tpu_custom_call" | custom-call | flops 1 | bytes 1 | tf_op jit(solution)/shard_map/attention_forward/pallas_call | solution.py:74
  97.9 5.1 %attention_backward.1 = (bf16[512,256]{1,0:T(8,128)(2,1)S(1)}, bf16[512,512]{1,0:T(8,128)(2,1)S(1)}, bf16[512,512]{1,0:T(8,128)(2,1)S(1)}, bf16[1024,512]{1,0:T(8,128)(2,1)S(1)}) custom-call(bf16[512,256]{1,0:T(8,128)(2,1)S(1)} %get-tuple-element.93.refs_2_.refs_0_, bf16[528,512]{1,0:T(8,128)(2,1)S(1)} %get-tuple-element.94.refs_1_, ...), custom_call_target="tpu_custom_call" | custom-call | flops 1 | bytes 1 | tf_op jit(solution)/shard_map/attention_backward/pallas_call | solution.py:74
  106.2 6.9 %collective-permute-done.18.refs_1_ = bf16[64,4096]{1,0:T(8,128)(2,1)S(1)} collective-permute-done((bf16[64,4096]{1,0:T(8,128)(2,1)S(1)}, bf16[64,4096]{1,0:T(8,128)(2,1)S(1)}, u32[]{:S(2)}, u32[]{:S(2)}) %collective-permute-start.18) | collective-permute-done | bytes 524320 | tf_op jit(solution)/shard_map/ppermute | solution.py:30
  113.3 4.7 %query_weights.1 = (bf16[4,512,512]{2,1,0:T(8,128)(2,1)S(1)}, bf16[4,512,512]{2,1,0:T(8,128)(2,1)S(1)}) custom-call(s32[2]{0:T(128)S(1)} %pad_add_fusion.1.refs_0_, bf16[64,4224]{1,0:T(8,128)(2,1)S(1)} %get-tuple-element.91.refs_4_.refs_0_.refs_1_.refs_5_, bf16[64,4224]{1,0:T(8,128)(2,1)S(1)} %get-tuple-element.92.refs_1_.refs_2_.refs_6_, ...), custom_call_target="tpu_custom_call" | custom-call | flops 1 | bytes 1 | tf_op jit(solution)/shard_map/query_weights/pallas_call | solution.py:74
  123.2 5.4 %collective-permute-done.23.refs_2_ = bf16[64,4096]{1,0:T(8,128)(2,1)S(1)} collective-permute-done((bf16[64,4096]{1,0:T(8,128)(2,1)S(1)}, bf16[64,4096]{1,0:T(8,128)(2,1)S(1)}, u32[]{:S(2)}, u32[]{:S(2)}) %collective-permute-start.23) | collective-permute-done | bytes 524320 | tf_op jit(solution)/shard_map/ppermute | solution.py:30
  129.3 4.1 %collective-permute-done.25.refs_4_ = bf16[64,4096]{1,0:T(8,128)(2,1)S(1)} collective-permute-done((bf16[64,4096]{1,0:T(8,128)(2,1)S(1)}, bf16[64,4096]{1,0:T(8,128)(2,1)S(1)}, u32[]{:S(2)}, u32[]{:S(2)}) %collective-permute-start.25) | collective-permute-done | bytes 524320 | tf_op jit(solution)/shard_map/ppermute | solution.py:30
  134.6 6.5 %collective-permute-done.31.refs_2_ = bf16[512,512]{1,0:T(8,128)(2,1)S(1)} collective-permute-done((bf16[512,512]{1,0:T(8,128)(2,1)S(1)}, bf16[512,512]{1,0:T(8,128)(2,1)S(1)}, u32[]{:S(2)}, u32[]{:S(2)}) %collective-permute-start.31) | collective-permute-done | bytes 524320 | tf_op jit(solution)/shard_map/ppermute | solution.py:44
  141.1 6.6 %feature_parts.1 = (bf16[512,768]{1,0:T(8,128)(2,1)}, bf16[512,512]{1,0:T(8,128)(2,1)S(1)}, bf16[128,4224]{1,0:T(8,128)(2,1)S(1)}, bf16[64,4224]{1,0:T(8,128)(2,...) custom-call(bf16[512,512]{1,0:T(8,128)(2,1)S(1)} %get-tuple-element., ...), custom_call_target="tpu_custom_call" | custom-call | flops 1 | bytes 1 | tf_op jit(solution)/shard_map/feature_parts/pallas_call | solution.py:74
  147.7 9.8 %collective-permute-start.35 = (bf16[64,4224]{1,0:T(8,128)(2,1)S(1)}, bf16[64,4224]{1,0:T(8,128)(2,1)S(1)}, u32[]{:S(2)}, u32[]{:S(2)}) collective-permute-start(bf16[64,4224]{1,0:T(8,128)(2,1)S(1)} %get-tuple-element.126), channel_id=1, source_target_pairs={{0,32},{1,9},{2,34},{3,11},{4,36},{5,13},{6,38},{7,15},{8,40},{9,1... | collective-permute-start | bytes 1622024 | tf_op jit(solution)/shard_map/ppermute | solution.py:30
  161.3 4.3 %collective-permute-start.28 = (bf16[32,4096]{1,0:T(8,128)(2,1)S(1)}, bf16[32,4096]{1,0:T(8,128)(2,1)S(1)}, u32[]{:S(2)}, u32[]{:S(2)}) collective-permute-start(bf16[32,4096]{1,0:T(8,128)(2,1)S(1)} %get-tuple-element.115), channel_id=1, source_target_pairs={{0,16},{1,65},{2,18},{3,67},{4,20},{5,69},{6,22},{7,71},{8,24},{9,... | collective-permute-start | bytes 786440 | tf_op jit(solution)/shard_map/ppermute | solution.py:30
  166.5 4.8 %collective-permute-done.27.refs_2_ = bf16[32,4096]{1,0:T(8,128)(2,1)S(1)} collective-permute-done((bf16[32,4096]{1,0:T(8,128)(2,1)S(1)}, bf16[32,4096]{1,0:T(8,128)(2,1)S(1)}, u32[]{:S(2)}, u32[]{:S(2)}) %collective-permute-start.27) | collective-permute-done | bytes 262176 | tf_op jit(solution)/shard_map/ppermute | solution.py:30
  171.3 5.0 %collective-permute-done.28.refs_3_ = bf16[32,4096]{1,0:T(8,128)(2,1)S(1)} collective-permute-done((bf16[32,4096]{1,0:T(8,128)(2,1)S(1)}, bf16[32,4096]{1,0:T(8,128)(2,1)S(1)}, u32[]{:S(2)}, u32[]{:S(2)}) %collective-permute-start.28) | collective-permute-done | bytes 262176 | tf_op jit(solution)/shard_map/ppermute | solution.py:30
  178.8 5.8 %key_weights.1 = (bf16[4,512,512]{2,1,0:T(8,128)(2,1)S(1)}, bf16[4,512,512]{2,1,0:T(8,128)(2,1)}) custom-call(s32[2]{0:T(128)S(1)} %pad_add_fusion.1.refs_0_, bf16[64,4224]{1,0:T(8,128)(2,1)S(1)} %get-tuple-element.91.refs_4_.refs_0_.refs_1_.refs_5_, bf16[64,4224]{1,0:T(8,128)(2,1)S(1)} %get-tuple-element.92.refs_1_.refs_2_.refs_6_, ...), custom_call_target="tpu_custom_call" | custom-call | flops 1 | bytes 1 | tf_op jit(solution)/shard_map/key_weights/pallas_call | solution.py:74
  211.5 3.8 %collective-permute-start.46 = (bf16[32,4224]{1,0:T(8,128)(2,1)}, bf16[32,4224]{1,0:T(8,128)(2,1)}, u32[]{:S(2)}, u32[]{:S(2)}) collective-permute-start(bf16[32,4224]{1,0:T(8,128)(2,1)} %get-tuple-element.145), channel_id=1, source_target_pairs={{0,16},{1,65},{2,18},{3,67},{4,20},{5,69},{6,22},{7,71},{8,24},{9,... | collective-permute-start | bytes 811016 | tf_op jit(solution)/shard_map/ppermute | solution.py:30
  232.7 3.8 %collective-permute-start.44 = (bf16[4,32,512]{2,1,0:T(8,128)(2,1)}, bf16[4,32,512]{2,1,0:T(8,128)(2,1)}, u32[]{:S(2)}, u32[]{:S(2)}) collective-permute-start(bf16[4,32,512]{2,1,0:T(8,128)(2,1)} %out_columns.1.refs_7_), channel_id=1, source_target_pairs={{0,1},{1,0},{2,3},{3,2},{4,5},{5,4},{6,7},{7,6},{8,9},{9,8},{10,11... | collective-permute-start | bytes 393224 | tf_op jit(solution)/shard_map/ppermute | solution.py:40
  245.3 3.6 %out_placed.1.refs_6_ = bf16[2048,512]{1,0:T(8,128)(2,1)} custom-call(s32[2]{0:T(128)S(1)} %pad_add_fusion.1.refs_0_, bf16[2048,512]{1,0:T(8,128)(2,1)S(1)} %bitcast.42, s32[1,256]{1,0:T(1,128)S(1)} %reshape.156.refs_2_, bf16[32,1024]{1,0:T(8,128)(2,1)S(1)} %get-tuple-element.121.refs_4_.refs_1_.refs_3_, bf16[32,1024]{1,0:T(8,128)(2,1)S(1)} %copy-done.18, ...), custom_call_target="tpu_custom_call" | custom-call | flops 1 | bytes 1 | tf_op jit(solution)/shard_map/out_placed/pallas_call | solution.py:74
  255.5 18.9 %collective-permute-done.50.refs_4_.refs_6_ = bf16[32,1152]{1,0:T(8,128)(2,1)S(1)} collective-permute-done((bf16[32,1152]{1,0:T(8,128)(2,1)S(1)}, bf16[32,1152]{1,0:T(8,128)(2,1)S(1)}, u32[]{:S(2)}, u32[]{:S(2)}) %collective-permute-start.50) | collective-permute-done | bytes 73760 | tf_op jit(solution)/shard_map/ppermute | solution.py:34
  (243 shorter events, 132.0 us)
Async XLA Ops:
  23.5 15.3 %collective-permute-start.5 = (bf16[32,8320]{1,0:T(8,128)(2,1)S(1)}, bf16[32,8320]{1,0:T(8,128)(2,1)S(1)}, u32[]{:S(2)}, u32[]{:S(2)}) collective-permute-start(bf16[32,8320]{1,0:T(8,128)(2,1)S(1)} %get-tuple-element.89.refs_0_), channel_id=1, source_target_pairs={{0,16},{1,65},{2,18},{3,67},{4,20},{5,69},{6,22},{7,71},{8,24},{9,... | collective-permute-start | bytes 1597448 | tf_op jit(solution)/shard_map/ppermute | solution.py:30
  51.3 12.8 %collective-permute-start.12 = (bf16[64,4224]{1,0:T(8,128)(2,1)S(1)}, bf16[64,4224]{1,0:T(8,128)(2,1)S(1)}, u32[]{:S(2)}, u32[]{:S(2)}) collective-permute-start(bf16[64,4224]{1,0:T(8,128)(2,1)S(1)} %get-tuple-element.91.refs_4_.refs_0_.refs_1_.refs_5_), channel_id=1, source_target_pairs={{0,32},{1,9},{2,34},{3,11},{4,36},{5,13},{6,38},{7,15},{8,40},{9,1... | collective-permute-start | bytes 1622024 | tf_op jit(solution)/shard_map/ppermute | solution.py:30
  58.4 25.8 %collective-permute-start.17 = (bf16[128,4096]{1,0:T(8,128)(2,1)S(1)}, bf16[128,4096]{1,0:T(8,128)(2,1)S(1)}, u32[]{:S(2)}, u32[]{:S(2)}) collective-permute-start(bf16[128,4096]{1,0:T(8,128)(2,1)S(1)} %stack_g.1.refs_11_.refs_0_.refs_9_), channel_id=1, source_target_pairs={{0,32},{1,9},{2,34},{3,11},{4,36},{5,13},{6,38},{7,15},{8,40},{9,1... | collective-permute-start | bytes 3145736 | tf_op jit(solution)/shard_map/ppermute | solution.py:30
  58.5 25.7 %collective-permute-start.16 = (bf16[128,4096]{1,0:T(8,128)(2,1)S(1)}, bf16[128,4096]{1,0:T(8,128)(2,1)S(1)}, u32[]{:S(2)}, u32[]{:S(2)}) collective-permute-start(bf16[128,4096]{1,0:T(8,128)(2,1)S(1)} %stack_g.1.refs_11_.refs_0_.refs_9_), channel_id=1, source_target_pairs={{0,96},{1,25},{2,98},{3,27},{4,100},{5,29},{6,102},{7,31},{8,104},... | collective-permute-start | bytes 3145736 | tf_op jit(solution)/shard_map/ppermute | solution.py:30
  70.2 17.1 %collective-permute-start.13 = (bf16[528,512]{1,0:T(8,128)(2,1)S(1)}, bf16[528,512]{1,0:T(8,128)(2,1)S(1)}, u32[]{:S(2)}, u32[]{:S(2)}) collective-permute-start(bf16[528,512]{1,0:T(8,128)(2,1)S(1)} %get-tuple-element.94.refs_1_), channel_id=1, source_target_pairs={{0,1},{1,0},{2,3},{3,2},{4,5},{5,4},{6,7},{7,6},{8,9},{9,8},{10,11... | collective-permute-start | bytes 1622024 | tf_op jit(solution)/shard_map/ppermute | solution.py:40
  118.0 47.5 %collective-permute-start.30 = (bf16[4,512,512]{2,1,0:T(8,128)(2,1)S(1)}, bf16[4,512,512]{2,1,0:T(8,128)(2,1)S(1)}, u32[]{:S(2)}, u32[]{:S(2)}) collective-permute-start(bf16[4,512,512]{2,1,0:T(8,128)(2,1)S(1)} %get-tuple-element.117), channel_id=1, source_target_pairs={{0,1},{1,0},{2,3},{3,2},{4,5},{5,4},{6,7},{7,6},{8,9},{9,8},{10,11... | collective-permute-start | bytes 6291464 | tf_op jit(solution)/shard_map/ppermute | solution.py:40
  147.7 30.0 %collective-permute-start.35 = (bf16[64,4224]{1,0:T(8,128)(2,1)S(1)}, bf16[64,4224]{1,0:T(8,128)(2,1)S(1)}, u32[]{:S(2)}, u32[]{:S(2)}) collective-permute-start(bf16[64,4224]{1,0:T(8,128)(2,1)S(1)} %get-tuple-element.126), channel_id=1, source_target_pairs={{0,32},{1,9},{2,34},{3,11},{4,36},{5,13},{6,38},{7,15},{8,40},{9,1... | collective-permute-start | bytes 1622024 | tf_op jit(solution)/shard_map/ppermute | solution.py:30
  157.5 20.2 %collective-permute-start.36 = (bf16[64,4224]{1,0:T(8,128)(2,1)S(1)}, bf16[64,4224]{1,0:T(8,128)(2,1)S(1)}, u32[]{:S(2)}, u32[]{:S(2)}) collective-permute-start(bf16[64,4224]{1,0:T(8,128)(2,1)S(1)} %get-tuple-element.128), channel_id=1, source_target_pairs={{0,96},{1,25},{2,98},{3,27},{4,100},{5,29},{6,102},{7,31},{8,104},... | collective-permute-start | bytes 1622024 | tf_op jit(solution)/shard_map/ppermute | solution.py:30
  161.3 15.0 %collective-permute-start.28 = (bf16[32,4096]{1,0:T(8,128)(2,1)S(1)}, bf16[32,4096]{1,0:T(8,128)(2,1)S(1)}, u32[]{:S(2)}, u32[]{:S(2)}) collective-permute-start(bf16[32,4096]{1,0:T(8,128)(2,1)S(1)} %get-tuple-element.115), channel_id=1, source_target_pairs={{0,16},{1,65},{2,18},{3,67},{4,20},{5,69},{6,22},{7,71},{8,24},{9,... | collective-permute-start | bytes 786440 | tf_op jit(solution)/shard_map/ppermute | solution.py:30
  184.7 30.5 %collective-permute-start.37 = (bf16[4,512,512]{2,1,0:T(8,128)(2,1)}, bf16[4,512,512]{2,1,0:T(8,128)(2,1)}, u32[]{:S(2)}, u32[]{:S(2)}) collective-permute-start(bf16[4,512,512]{2,1,0:T(8,128)(2,1)} %get-tuple-element.131), channel_id=1, source_target_pairs={{0,1},{1,0},{2,3},{3,2},{4,5},{5,4},{6,7},{7,6},{8,9},{9,8},{10,11... | collective-permute-start | bytes 6291464 | tf_op jit(solution)/shard_map/ppermute | solution.py:40
  187.4 16.1 %collective-permute-start.39 = (bf16[64,4224]{1,0:T(8,128)(2,1)}, bf16[64,4224]{1,0:T(8,128)(2,1)}, u32[]{:S(2)}, u32[]{:S(2)}) collective-permute-start(bf16[64,4224]{1,0:T(8,128)(2,1)} %get-tuple-element.133), channel_id=1, source_target_pairs={{0,32},{1,9},{2,34},{3,11},{4,36},{5,13},{6,38},{7,15},{8,40},{9,1... | collective-permute-start | bytes 1622024 | tf_op jit(solution)/shard_map/ppermute | solution.py:30
  187.4 16.2 %collective-permute-start.40 = (bf16[64,4224]{1,0:T(8,128)(2,1)}, bf16[64,4224]{1,0:T(8,128)(2,1)}, u32[]{:S(2)}, u32[]{:S(2)}) collective-permute-start(bf16[64,4224]{1,0:T(8,128)(2,1)} %get-tuple-element.134), channel_id=1, source_target_pairs={{0,96},{1,25},{2,98},{3,27},{4,100},{5,29},{6,102},{7,31},{8,104},... | collective-permute-start | bytes 1622024 | tf_op jit(solution)/shard_map/ppermute | solution.py:30
  208.8 23.9 %collective-permute-start.45 = (bf16[32,4224]{1,0:T(8,128)(2,1)}, bf16[32,4224]{1,0:T(8,128)(2,1)}, u32[]{:S(2)}, u32[]{:S(2)}) collective-permute-start(bf16[32,4224]{1,0:T(8,128)(2,1)} %get-tuple-element.144), channel_id=1, source_target_pairs={{0,8},{1,33},{2,10},{3,35},{4,12},{5,37},{6,14},{7,39},{8,16},{9,4... | collective-permute-start | bytes 811016 | tf_op jit(solution)/shard_map/ppermute | solution.py:30
  211.5 25.0 %collective-permute-start.46 = (bf16[32,4224]{1,0:T(8,128)(2,1)}, bf16[32,4224]{1,0:T(8,128)(2,1)}, u32[]{:S(2)}, u32[]{:S(2)}) collective-permute-start(bf16[32,4224]{1,0:T(8,128)(2,1)} %get-tuple-element.145), channel_id=1, source_target_pairs={{0,16},{1,65},{2,18},{3,67},{4,20},{5,69},{6,22},{7,71},{8,24},{9,... | collective-permute-start | bytes 811016 | tf_op jit(solution)/shard_map/ppermute | solution.py:30
  215.2 21.3 %collective-permute-start.47 = (bf16[32,4224]{1,0:T(8,128)(2,1)}, bf16[32,4224]{1,0:T(8,128)(2,1)}, u32[]{:S(2)}, u32[]{:S(2)}) collective-permute-start(bf16[32,4224]{1,0:T(8,128)(2,1)} %get-tuple-element.146), channel_id=1, source_target_pairs={{0,24},{1,97},{2,26},{3,99},{4,28},{5,101},{6,30},{7,103},{8,0},{9... | collective-permute-start | bytes 811016 | tf_op jit(solution)/shard_map/ppermute | solution.py:30
  221.4 27.5 %collective-permute-start.51 = (bf16[256,512]{1,0:T(8,128)(2,1)}, bf16[256,512]{1,0:T(8,128)(2,1)}, u32[]{:S(2)}, u32[]{:S(2)}) collective-permute-start(bf16[256,512]{1,0:T(8,128)(2,1)} %get-tuple-element.151), channel_id=1, source_target_pairs={{0,2},{1,3},{2,4},{3,5},{4,6},{5,7},{6,0},{7,1},{8,10},{9,11},{10,... | collective-permute-start | bytes 786440 | tf_op jit(solution)/shard_map/ppermute | solution.py:34
  221.4 28.2 %collective-permute-start.52 = (bf16[256,512]{1,0:T(8,128)(2,1)}, bf16[256,512]{1,0:T(8,128)(2,1)}, u32[]{:S(2)}, u32[]{:S(2)}) collective-permute-start(bf16[256,512]{1,0:T(8,128)(2,1)} %get-tuple-element.155), channel_id=1, source_target_pairs={{0,6},{1,7},{2,0},{3,1},{4,2},{5,3},{6,4},{7,5},{8,14},{9,15},{10,... | collective-permute-start | bytes 786440 | tf_op jit(solution)/shard_map/ppermute | solution.py:34
  239.4 13.3 %collective-permute-start.48 = (bf16[32,1152]{1,0:T(8,128)(2,1)}, bf16[32,1152]{1,0:T(8,128)(2,1)S(1)}, u32[]{:S(2)}, u32[]{:S(2)}) collective-permute-start(bf16[32,1152]{1,0:T(8,128)(2,1)} %get-tuple-element.148), channel_id=1, source_target_pairs={{0,2},{1,3},{2,4},{3,5},{4,6},{5,7},{6,0},{7,1},{8,10},{9,11},{10,... | collective-permute-start | bytes 221192 | tf_op jit(solution)/shard_map/ppermute | solution.py:34
  239.4 14.7 %collective-permute-start.49 = (bf16[32,1152]{1,0:T(8,128)(2,1)}, bf16[32,1152]{1,0:T(8,128)(2,1)}, u32[]{:S(2)}, u32[]{:S(2)}) collective-permute-start(bf16[32,1152]{1,0:T(8,128)(2,1)} %get-tuple-element.149), channel_id=1, source_target_pairs={{0,4},{1,5},{2,6},{3,7},{4,0},{5,1},{6,2},{7,3},{8,12},{9,13},{10,... | collective-permute-start | bytes 221192 | tf_op jit(solution)/shard_map/ppermute | solution.py:34
  240.8 41.4 %collective-permute-start.54 = (bf16[512,512]{1,0:T(8,128)(2,1)}, bf16[512,512]{1,0:T(8,128)(2,1)S(1)}, u32[]{:S(2)}, u32[]{:S(2)}) collective-permute-start(bf16[512,512]{1,0:T(8,128)(2,1)} %copy-done.12), channel_id=1, source_target_pairs={{0,2},{1,3},{2,4},{3,5},{4,6},{5,7},{6,0},{7,1},{8,10},{9,11},{10,... | collective-permute-start | bytes 1572872 | tf_op jit(solution)/shard_map/ppermute | solution.py:34
  248.9 33.3 %collective-permute-start.55 = (bf16[512,512]{1,0:T(8,128)(2,1)S(1)}, bf16[512,512]{1,0:T(8,128)(2,1)S(1)}, u32[]{:S(2)}, u32[]{:S(2)}) collective-permute-start(bf16[512,512]{1,0:T(8,128)(2,1)S(1)} %copy-done.44), channel_id=1, source_target_pairs={{0,6},{1,7},{2,0},{3,1},{4,2},{5,3},{6,4},{7,5},{8,14},{9,15},{10,... | collective-permute-start | bytes 1572872 | tf_op jit(solution)/shard_map/ppermute | solution.py:34
  252.5 29.7 %collective-permute-start.57 = (bf16[512,512]{1,0:T(8,128)(2,1)S(1)}, bf16[512,512]{1,0:T(8,128)(2,1)S(1)}, u32[]{:S(2)}, u32[]{:S(2)}) collective-permute-start(bf16[512,512]{1,0:T(8,128)(2,1)S(1)} %get-tuple-element.162), channel_id=1, source_target_pairs={{0,6},{1,7},{2,0},{3,1},{4,2},{5,3},{6,4},{7,5},{8,14},{9,15},{10,... | collective-permute-start | bytes 1572872 | tf_op jit(solution)/shard_map/ppermute | solution.py:34
  252.8 29.5 %collective-permute-start.56 = (bf16[512,512]{1,0:T(8,128)(2,1)S(1)}, bf16[512,512]{1,0:T(8,128)(2,1)S(1)}, u32[]{:S(2)}, u32[]{:S(2)}) collective-permute-start(bf16[512,512]{1,0:T(8,128)(2,1)S(1)} %get-tuple-element.156.refs_5_), channel_id=1, source_target_pairs={{0,2},{1,3},{2,4},{3,5},{4,6},{5,7},{6,0},{7,1},{8,10},{9,11},{10,... | collective-permute-start | bytes 1572872 | tf_op jit(solution)/shard_map/ppermute | solution.py:34
  254.1 20.3 %collective-permute-start.50 = (bf16[32,1152]{1,0:T(8,128)(2,1)S(1)}, bf16[32,1152]{1,0:T(8,128)(2,1)S(1)}, u32[]{:S(2)}, u32[]{:S(2)}) collective-permute-start(bf16[32,1152]{1,0:T(8,128)(2,1)S(1)} %copy-done.46), channel_id=1, source_target_pairs={{0,6},{1,7},{2,0},{3,1},{4,2},{5,3},{6,4},{7,5},{8,14},{9,15},{10,... | collective-permute-start | bytes 221192 | tf_op jit(solution)/shard_map/ppermute | solution.py:34
  (83 other events, 643.3 us)
where the time goes:
time: 290 us; the launch traced here: 286 us
  waiting for transfers between devices  95 us (33%)
  starting transfers between devices  88.2 us (30%)
  Pallas kernels  65.9 us (23%)
  local copies, waits for them, and re-layouts  27 us (9%)
  between operations  8.73 us (3%)
    pallas_call x31, Pallas kernels, invoke(): pl.pallas_call(body, out_shape=out_shape, compiler_params=pltpu.CompilerP...  65.9 us
    ppermute x31, waiting for transfers between devices, ring(): return lax.ppermute(values, BOTH, ring_pairs(second, shift))  56.7 us
    ppermute x31, starting transfers between devices, ring(): return lax.ppermute(values, BOTH, ring_pairs(second, shift))  50.5 us
    unnamed x99, local copies, waits for them, and re-layouts  24.8 us
    ppermute x17, waiting for transfers between devices, send_z(): lax.ppermute(values, 'cmp', [(z * 2 + c, (z + shift) % 4 * 2 + c) for z i...  22.2 us
    ppermute x17, starting transfers between devices, send_z(): lax.ppermute(values, 'cmp', [(z * 2 + c, (z + shift) % 4 * 2 + c) for z i...  20.9 us
    ppermute x8, starting transfers between devices, swap_core(): return lax.ppermute(values, 'cmp', [(k, k ^ 1) for k in range(8)])  15.3 us
    ppermute x2, waiting for transfers between devices, swap_chip(): return lax.ppermute(values, 'cmp', [(k, k ^ 2) for k in range(8)])  13.9 us
  transfers between devices with their start and end apart: 58, of which 19 were waited for; matrix products, arithmetic and copies ran while one was open for 1% of the time, Pallas kernels for 15%

commit v1 on v0

--- a/solution.py
+++ b/solution.py
@@ -26,22 +26,25 @@
     return pairs
 
 
-def ring(values, second, shift):
-    return lax.ppermute(values, BOTH, ring_pairs(second, shift))
-
-
-def send_z(values, shift):
-    return lax.ppermute(
-        values, "cmp", [(z * 2 + c, ((z + shift) % 4) * 2 + c) for z in range(4) for c in range(2)]
-    )
-
-
-def swap_core(values):
-    return lax.ppermute(values, "cmp", [(k, k ^ 1) for k in range(8)])
-
-
-def swap_chip(values):
-    return lax.ppermute(values, "cmp", [(k, k ^ 2) for k in range(8)])
+def ring(values, second, shift, name="rows"):
+    with jax.named_scope(f"{name}_{'second' if second else 'first'}_{shift}"):
+        return lax.ppermute(values, BOTH, ring_pairs(second, shift))
+
+
+def send_z(values, shift, name="rows"):
+    pairs = [(z * 2 + c, ((z + shift) % 4) * 2 + c) for z in range(4) for c in range(2)]
+    with jax.named_scope(f"{name}_z_{shift}"):
+        return lax.ppermute(values, "cmp", pairs)
+
+
+def swap_core(values, name="rows"):
+    with jax.named_scope(name + "_core"):
+        return lax.ppermute(values, "cmp", [(k, k ^ 1) for k in range(8)])
+
+
+def swap_chip(values, name="rows"):
+    with jax.named_scope(name + "_chip"):
+        return lax.ppermute(values, "cmp", [(k, k ^ 2) for k in range(8)])
 
 
 def dyn(values, index, axis=0):
@@ -61,9 +64,10 @@
 
 
 ORDER = []
-
-
-def call(kernel, name, out_shape, room=8, after=(), **options):
+COSTS = {"out_add": 20, "feature_parts": 30, "sum_column": 30, "query_weights_near": 20}
+
+
+def call(kernel, name, out_shape, room=8, after=(), cost=0, **options):
     def invoke(*operands):
         tokens = ORDER[-1:] + list(after)
         count, skip = len(operands), len(tokens)
@@ -75,7 +79,7 @@
             body,
             out_shape=out_shape,
             compiler_params=pltpu.CompilerParams(vmem_limit_bytes=room * 2**20),
-            cost_estimate=pl.CostEstimate(flops=1, bytes_accessed=1, transcendentals=0),
+            cost_estimate=pl.CostEstimate(flops=1 + COSTS.get(name, 0) * 10**9, bytes_accessed=1, transcendentals=0),
             name=name,
             **{**options, "in_specs": options["in_specs"] + [ANY] * skip},
         )(*operands, *tokens)
@@ -236,53 +240,51 @@
 
 
 def add_kernel(a, ta, b, tb, out_a, out_b):
-    out_a[...] = a[...] + ta[...]
-    out_b[...] = b[...] + tb[...]
-
-
-def sum_column_kernel(own, u_low, u_high, v_low, v_high, *outs):
-    for half, u, v in ((0, u_low, v_low), (64, u_high, v_high)):
-        for i in range(2):
-            rows = slice(i * 32, i * 32 + 32)
-            first = own[half + i * 32 : half + i * 32 + 32].astype(F32)
-            total = first + u[rows].astype(F32) + v[rows].astype(F32)
-            outs[half // 32 + i][...] = total.astype(BF)
-
-
-def reduce_start(parts):
-    own, plus_low, plus_high, far_low, far_high, minus_low, minus_high = parts
-    to_plus, to_minus = ring(far_low, True, 3), ring(far_high, True, 1)
-    u_high, v_low = ring(plus_high, True, 3), ring(minus_low, True, 1)
-    return own, plus_low, to_plus, minus_high, to_minus, u_high, v_low
+    out_a[:64] = a[:64] + ta[...]
+    out_a[64:] = a[64:]
+    out_b[:64] = b[:64]
+    out_b[64:] = b[64:] + tb[...]
+
+
+def sum_column_kernel(og, ug, vg, oo, uo, vo, *outs):
+    for i, out in enumerate(outs):
+        rows = slice(i * 32, i * 32 + 32)
+        for own, u, v, at in ((oo, uo, vo, slice(0, 4096)), (og, ug, vg, slice(4096, 4096 + WIDE))):
+            total = own[rows].astype(F32) + u[rows].astype(F32) + v[rows].astype(F32)
+            out[:, at] = total.astype(BF)
+
+
+def reduce_start(parts, name):
+    own, plus, far_low, far_high, minus = parts
+    return own, plus, ring(far_low, True, 3, name), minus, ring(far_high, True, 1, name)
 
 
 def reduce_add(state, name):
-    own, plus_low, to_plus, minus_high, to_minus, u_high, v_low = state
+    own, plus, to_plus, minus, to_minus = state
     plus, minus = call(
         add_kernel,
         name + "_add",
-        [shape(*plus_low.shape)] * 2,
+        [shape(*plus.shape)] * 2,
         in_specs=[WHOLE] * 4,
         out_specs=[WHOLE] * 2,
-    )(plus_low, to_plus, minus_high, to_minus)
-    return own, ring(plus, True, 3), u_high, v_low, ring(minus, True, 1)
-
-
-def reduce_column(terms, name):
-    width = terms[0].shape[1]
+    )(plus, to_plus, minus, to_minus)
+    return own, ring(plus, True, 3, name), ring(minus, True, 1, name)
+
+
+def reduce_column(grad_terms, out_terms, after):
     parts = call(
         sum_column_kernel,
-        name + "_column",
-        [shape(32, width)] * 4,
-        in_specs=[WHOLE] * 5,
+        "sum_column",
+        [shape(32, 4096 + WIDE)] * 4,
+        after=after,
+        in_specs=[WHOLE] * 6,
         out_specs=[WHOLE] * 4,
-    )(*terms)
-    return [parts[0]] + [ring(parts[i], False, 4 - i) for i in (1, 2, 3)]
+    )(*grad_terms, *out_terms)
+    return [parts[0]] + [ring(parts[i], False, 4 - i, "sum") for i in (1, 2, 3)]
 
 
 X_PIECES = (64,) * 8
 G_PIECES = (128, 128, 64, 64, 128)
-PARTS = (128, 64, 64, 64, 64, 64, 64)
 
 
 def joined(refs, columns=slice(None)):
@@ -381,10 +383,10 @@
     return call(
         output_kernel,
         "output_parts",
-        [shape(n, 4096) for n in PARTS],
+        [shape(n, 4096) for n in G_PIECES],
         room=12,
         in_specs=[WHOLE] * 2,
-        out_specs=[WHOLE] * 7,
+        out_specs=[WHOLE] * 5,
     )(att, w)
 
 
@@ -503,7 +505,7 @@
 
 
 def feature_kernel(near, recv, chip, gq, table, *refs):
-    x, w, gain, gp, gp_kv, parts, ride = refs[:8], refs[8], refs[9], refs[10], refs[11], refs[12:19], refs[19]
+    x, w, gain, gp, gp_kv, parts, ride = refs[:8], refs[8], refs[9], refs[10], refs[11], refs[12:17], refs[17]
     own = near[...].astype(F32) + recv[512:].astype(F32) + chip[...].astype(F32)
     gp[:, :256] = gq[...]
     for h in range(2):
@@ -527,14 +529,15 @@
             part[r : r + 32, 4096:] = ride[...].astype(BF)
 
 
-def feature_parts(near, recv, chip, gq, table, x, w, gain):
+def feature_parts(near, recv, chip, gq, table, x, w, gain, after):
     out = call(
         feature_kernel,
         "feature_parts",
-        [shape(512, 768), shape(512, 512)] + [shape(n, WIDE) for n in PARTS],
+        [shape(512, 768), shape(512, 512)] + [shape(n, WIDE) for n in G_PIECES],
         room=26,
+        after=after,
         in_specs=[WHOLE] * 15,
-        out_specs=[WHOLE] * 9,
+        out_specs=[WHOLE] * 7,
         scratch_shapes=[pltpu.VMEM((32, 128), F32)],
     )(near, recv, chip, gq, table, *x, w, gain)
     return out[1], out[2:]
@@ -622,7 +625,7 @@
         in_specs=[WHOLE] * 2,
         out_specs=[WHOLE] * 7,
     )(keep, recv)
-    return parts, send_z(parts[3], 1), send_z(parts[4], 3)
+    return parts, send_z(parts[3], 1, name), send_z(parts[4], 3, name)
 
 
 def join_kernel(plus_low, to_plus, plus_high, minus_low, minus_high, to_minus, out_a, out_b):
@@ -641,7 +644,7 @@
         in_specs=[WHOLE] * 6,
         out_specs=[WHOLE] * 2,
     )(parts[1], to_plus, parts[2], parts[5], parts[6], to_minus)
-    return parts[0], send_z(plus, 1), send_z(minus, 3)
+    return parts[0], send_z(plus, 1, name), send_z(minus, 3, name)
 
 
 def sum_weights_kernel(a0, a1, a2, b0, b1, b2, in_grad, out_grad):
@@ -663,90 +666,84 @@
     )(*a, *b)
 
 
-def grad_rows_kernel(where, own, u, t, v, rows, gain, o0, o1, o2, o3, total):
+def final_rows_kernel(where, own, u, t, v, rows, gain, o0, o1, o2, o3, total):
     x = rows[...].astype(F32)
     inverse = lax.rsqrt(jnp.mean(x * x, -1, keepdims=True) + EPS)
     unit = x * inverse
-    s = (own[...].astype(F32) + u[...].astype(F32)) + (t[...].astype(F32) + v[...].astype(F32))
-    scaled = s[:, :4096] * gain[...]
-    total[...] = (inverse * (scaled - unit * jnp.mean(scaled * unit, -1, keepdims=True))).astype(BF)
+
+    def summed(at):
+        first = own[:, at].astype(F32) + u[:, at].astype(F32)
+        return first + (t[:, at].astype(F32) + v[:, at].astype(F32))
+
+    total[:, :4096] = summed(slice(0, 4096)).astype(BF)
+    scaled = summed(slice(4096, 8192)) * gain[...]
+    grads = inverse * (scaled - unit * jnp.mean(scaled * unit, -1, keepdims=True))
+    total[:, 4096:] = grads.astype(BF)
+    riding = summed(slice(8192, 8192 + EXTRA)).astype(BF)
     for d, out in enumerate((o0, o1, o2, o3)):
-        start = pl.multiple_of(lax.rem(where[0] + d, 4) * 1024, 1024)
-        out[:, :1024] = total[:, pl.ds(start, 1024)]
-        out[:, 1024:] = s[:, 4096:].astype(BF)
-
-
-def out_rows_kernel(where, own, u, t, v, o0, o1, o2, o3, total):
-    s = (own[...].astype(F32) + u[...].astype(F32)) + (t[...].astype(F32) + v[...].astype(F32))
-    total[...] = s.astype(BF)
-    for d, out in enumerate((o0, o1, o2, o3)):
-        start = pl.multiple_of(lax.rem(where[0] + d, 4) * 1024, 1024)
-        out[...] = total[:, pl.ds(start, 1024)]
-
-
-def split_rows(kernel, name, where, operands, width):
+        start = lax.rem(where[0] + d, 4) * 1024
+        out[:, :1024] = total[:, pl.ds(pl.multiple_of(start, 1024), 1024)]
+        out[:, 1024:2048] = total[:, pl.ds(pl.multiple_of(start + 4096, 1024), 1024)]
+        out[:, 2048:] = riding
+
+
+def final_rows(where, *operands):
     parts = call(
-        kernel,
-        name,
-        [shape(32, width)] * 4,
+        final_rows_kernel,
+        "final_rows",
+        [shape(32, 2048 + EXTRA)] * 4,
         in_specs=[SMEM] + [WHOLE] * len(operands),
         out_specs=[WHOLE] * 4,
-        scratch_shapes=[pltpu.VMEM((32, 4096), BF)],
+        scratch_shapes=[pltpu.VMEM((32, 8192), BF)],
     )(where, *operands)
-    return [parts[0]] + [send_z(parts[d], d) for d in (1, 2, 3)]
-
-
-def columns_kernel(where, p0, p1, p2, p3, out, *gain):
-    start = pl.multiple_of((1 - where[1]) * 512, 512)
-    pieces = (p0, p1, p2, p3)
-    for d, piece in enumerate(pieces):
-        out[d, :, :512] = piece[:, pl.ds(start, 512)]
-    if gain:
-        total = (p0[:, 1024:].astype(F32) + p1[:, 1024:].astype(F32)) + (
-            p2[:, 1024:].astype(F32) + p3[:, 1024:].astype(F32)
-        )
-        high = total.astype(BF)
-        out[0, :, 512:] = high
-        out[1, :, 512:] = (total - high.astype(F32)).astype(BF)
-        out[2, :, 512:] = high
-        out[3, :, 512:] = high
-        gain[0][...] = total
-
-
-def place_kernel(where, base, places, p0, p1, p2, p3, other, out, rows):
-    step = pl.program_id(0)
-
-    @pl.when(step == 0)
-    def _():
-        start = pl.multiple_of(where[1] * 512, 512)
-        for d, piece in enumerate((p0, p1, p2, p3)):
-            rows[d * 32 : d * 32 + 32] = piece[:, pl.ds(start, 512)]
-            rows[128 + d * 32 : 160 + d * 32] = other[d, :, :512]
-
-    token = step * 512 + lax.broadcasted_iota(jnp.int32, (512, 256), 0)
-    hot = (token == places[...]).astype(F32).astype(BF)
-    added = jnp.dot(hot, rows[...], preferred_element_type=F32)
-    out[...] = (base[...].astype(F32) + added).astype(BF)
-
-
-def other_columns(where, pieces, name):
-    riding = pieces[0].shape[1] > 1024
-    width = 512 + (128 if riding else 0)
-    sent = call(
+    return [parts[0]] + [send_z(parts[d], d, "final") for d in (1, 2, 3)]
+
+
+def columns_kernel(where, p0, p1, p2, p3, out, gain):
+    total = jnp.zeros((32, EXTRA), F32)
+    for d, piece in enumerate((p0, p1, p2, p3)):
+        for half in range(2):
+            start = pl.multiple_of(half * 1024 + (1 - where[1]) * 512, 512)
+            out[d, :, half * 512 : half * 512 + 512] = piece[:, pl.ds(start, 512)]
+        total += piece[:, 2048:].astype(F32)
+    high = total.astype(BF)
+    low = (total - high.astype(F32)).astype(BF)
+    for d in range(4):
+        out[d, :, 1024:] = low if d == 1 else high
+    gain[...] = total
+
+
+def other_columns(where, pieces):
+    sent, gain = call(
         columns_kernel,
-        name + "_columns",
-        [shape(4, 32, width)] + ([shape(32, 128, dtype=F32)] if riding else []),
+        "columns",
+        [shape(4, 32, 1024 + EXTRA), shape(32, EXTRA, dtype=F32)],
         in_specs=[SMEM] + [WHOLE] * 4,
-        out_specs=[WHOLE] * (2 if riding else 1),
+        out_specs=[WHOLE] * 2,
     )(where, *pieces)
-    return swap_core(sent[0]), sent[1:]
-
-
-def place_rows(where, base, places, pieces, other, name):
+    return swap_core(sent, "final"), gain
+
+
+def place_rows(where, base, places, pieces, other, half, name):
+    def kernel(where, base, places, p0, p1, p2, p3, other, out, rows):
+        step = pl.program_id(0)
+
+        @pl.when(step == 0)
+        def _():
+            start = pl.multiple_of(half * 1024 + where[1] * 512, 512)
+            for d, piece in enumerate((p0, p1, p2, p3)):
+                rows[d * 32 : d * 32 + 32] = piece[:, pl.ds(start, 512)]
+                rows[128 + d * 32 : 160 + d * 32] = other[d, :, half * 512 : half * 512 + 512]
+
+        token = step * 512 + lax.broadcasted_iota(jnp.int32, (512, 256), 0)
+        hot = (token == places[...]).astype(F32).astype(BF)
+        added = jnp.dot(hot, rows[...], preferred_element_type=F32)
+        out[...] = (base[...].astype(F32) + added).astype(BF)
+
     block = pl.BlockSpec((512, 512), lambda i: (i, 0))
     fixed = lambda i: (0, 0)
     return call(
-        place_kernel,
+        kernel,
         name + "_placed",
         shape(2048, 512),
         grid=(4,),
@@ -783,47 +780,46 @@
     g_near = gather_g(column, (x[4], x[5]))
 
     queries, own_pair, table = project(x, w_in)
-    chip_pair = swap_chip(own_pair)
-    core_pair = swap_core(own_pair)
-    far_pair = swap_core(chip_pair)
+    chip_pair = swap_chip(own_pair, "pair")
+    core_pair = swap_core(own_pair, "pair")
+    far_pair = swap_core(chip_pair, "far_pair")
     pieces = [own_pair, core_pair, chip_pair, far_pair]
     g = gather_g_far(*g_near)
     attended, probs = attend(queries, pieces, table)
 
-    out_state = reduce_start(output_parts(attended, w_back))
+    out_state = reduce_start(output_parts(attended, w_back), "out")
     grad_attended = attended_grad(g, w_back)
     grad_q, near, mid, sent = attend_back(queries, pieces, probs, grad_attended, attended, table)
-    recv = swap_core(sent)
+    recv = swap_core(sent, "key_grads")
     out_terms = reduce_add(out_state, "out")
-    chip_part = swap_chip(chip_sum(mid, recv))
+    chip_part = swap_chip(chip_sum(mid, recv), "key_grads")
     kept_a, sent_a = query_weights(where, x, g, grad_q, attended)
-    recv_a = swap_core(sent_a)
-    out_column = reduce_column(out_terms, "out")
-
-    gp_kv, parts = feature_parts(near, recv, chip_part, grad_q, table, x, w_in, gain)
-    grad_state = reduce_start(parts)
-    state_a = sum_cores(kept_a, recv_a, "query")
-    out_split = split_rows(out_rows_kernel, "out_rows", where, out_column, 1024)
+    recv_a = swap_core(sent_a, "query_weights")
+
+    gp_kv, parts = feature_parts(
+        near, recv, chip_part, grad_q, table, x, w_in, gain, out_terms[1:]
+    )
+    grad_state = reduce_start(parts, "grad")
+    state_a = sum_cores(kept_a, recv_a, "query_weights")
     grad_terms = reduce_add(grad_state, "grad")
+    terms_a = sum_near(state_a, "query_weights")
     kept_b, sent_b = key_weights(where, x, gp_kv)
-    recv_b = swap_core(sent_b)
-    terms_a = sum_near(state_a, "query")
-    grad_column = reduce_column(grad_terms, "grad")
-    state_b = sum_cores(kept_b, recv_b, "key")
-    out_other, _ = other_columns(where, out_split, "out")
-    grad_split = split_rows(
-        grad_rows_kernel, "grad_rows", where, [*grad_column, rows_own, gain], 1024 + EXTRA
-    )
+    recv_b = swap_core(sent_b, "key_weights")
+    column = reduce_column(grad_terms, out_terms, terms_a[1:])
+    state_b = sum_cores(kept_b, recv_b, "key_weights")
+    final = final_rows(where, *column, rows_own, gain)
+    terms_b = sum_near(state_b, "key_weights")
+    other, gain_part = other_columns(where, final)
 
     chips = (z - jnp.arange(4)) % 4
     by_chip = (local_index + jnp.arange(2, dtype=jnp.int32)[:, None] * 1024).reshape(4, 2, 32)
     by_core = jnp.stack([dyn(by_chip, core, 1), dyn(by_chip, 1 - core, 1)])
     places = jnp.stack([dyn(by_core, chips[d], 1) for d in range(4)], 1).reshape(1, 256)
-    hidden_out = place_rows(where, hidden_in.reshape(2048, 512), places, out_split, out_other, "out")
-    terms_b = sum_near(state_b, "key")
-    grad_other, (gain_part,) = other_columns(where, grad_split, "grad")
-    grad_in = place_rows(where, cotangent.reshape(2048, 512), places, grad_split, grad_other, "grad")
-    grad_gain = gain_part + grad_other[0, :, 512:].astype(F32) + grad_other[1, :, 512:].astype(F32)
+    hidden = hidden_in.reshape(2048, 512)
+    grad_base = cotangent.reshape(2048, 512)
+    grad_in = place_rows(where, grad_base, places, final, other, 1, "grad")
+    hidden_out = place_rows(where, hidden, places, final, other, 0, "out")
+    grad_gain = gain_part + other[0, :, 1024:].astype(F32) + other[1, :, 1024:].astype(F32)
     grad_w_qkv, grad_w_out = sum_weights(terms_a, terms_b)
     return (
         hidden_out.reshape(2, 1024, 512),

time: 290 us -> 223 us (0.77); the launches traced: 286 us -> 222 us
  waiting for transfers between devices: 95 us -> 56.8 us
  local copies, waits for them, and re-layouts: 27 us -> 15.7 us
  Pallas kernels: 65.9 us -> 58.2 us
  starting transfers between devices: 88.2 us -> 81.7 us
    ppermute x31 -> x24, starting transfers between devices: 50.5 us -> 30.5 us  [ring(): return lax.ppermute(values, BOTH, ring_pairs(second, shift))]
    ppermute x8 -> x7, starting transfers between devices: 15.3 us -> 30.8 us  [swap_core(): return lax.ppermute(values, 'cmp', [(k, k ^ 1) for k in range(8)])]
    ppermute x17 -> x14, waiting for transfers between devices: 22.2 us -> 7.37 us  [send_z(): return lax.ppermute(values, 'cmp', pairs)]
    ppermute x31 -> x24, waiting for transfers between devices: 56.7 us -> 44.2 us  [ring(): return lax.ppermute(values, BOTH, ring_pairs(second, shift))]
    unnamed x99 -> x63, local copies, waits for them, and re-layouts: 24.8 us -> 13.6 us
    ppermute x2, waiting for transfers between devices: 13.9 us -> 4.15 us  [swap_chip(): return lax.ppermute(values, 'cmp', [(k, k ^ 2) for k in range(8)])]
    pallas_call x31 -> x28, Pallas kernels: 65.9 us -> 58.2 us  [invoke(): pl.pallas_call(body, out_shape=out_shape, compiler_params=pltpu.CompilerP...]
    ppermute x17 -> x14, starting transfers between devices: 20.9 us -> 18.7 us  [send_z(): return lax.ppermute(values, 'cmp', pairs)]
  transfers between devices with their start and end apart: 58 -> 47, of which waited for: 19 -> 18; matrix products, arithmetic and copies ran while one was open for 1% -> 1% of each run, Pallas kernels for 15% -> 22%
where the time goes in v1:
time: 223 us; the launch traced here: 222 us
  starting transfers between devices  81.7 us (37%)
  Pallas kernels  58.2 us (26%)
  waiting for transfers between devices  56.8 us (25%)
  local copies, waits for them, and re-layouts  15.7 us (7%)
  between operations  8.54 us (4%)
    pallas_call x28, Pallas kernels, invoke(): pl.pallas_call(body, out_shape=out_shape, compiler_params=pltpu.CompilerP...  58.2 us
    ppermute x24, waiting for transfers between devices, ring(): return lax.ppermute(values, BOTH, ring_pairs(second, shift))  44.2 us
    ppermute x7, starting transfers between devices, swap_core(): return lax.ppermute(values, 'cmp', [(k, k ^ 1) for k in range(8)])  30.8 us
    ppermute x24, starting transfers between devices, ring(): return lax.ppermute(values, BOTH, ring_pairs(second, shift))  30.5 us
    ppermute x14, starting transfers between devices, send_z(): return lax.ppermute(values, 'cmp', pairs)  18.7 us
    unnamed x63, local copies, waits for them, and re-layouts  13.6 us
    ppermute x14, waiting for transfers between devices, send_z(): return lax.ppermute(values, 'cmp', pairs)  7.37 us
  transfers between devices with their start and end apart: 47, of which 18 were waited for; matrix products, arithmetic and copies ran while one was open for 1% of the time, Pallas kernels for 22%

profile of v1, /device:TPU:1, one launch (start us, length us, event | category | flops | bytes accessed | tf_op | source)
XLA Modules:
  0.0 222.5 jit_solution(3243457623393781992)
XLA Ops:
  8.7 3.3 %collective-permute-start.1 = (bf16[2,2,32,512]{3,2,1,0:T(8,128)(2,1)S(1)}, bf16[2,2,32,512]{3,2,1,0:T(8,128)(2,1)S(1)}, u32[]{:S(2)}, u32[]{:S(2)}) collective-permute-start(bf16[2,2,32,512]{3,2,1,0:T(8,128)(2,1)S(1)} %get-tuple-element.75), channel_id=1, source_target_pairs={{0,4},{1,5},{2,6},{3,7},{4,0},{5,1},{6,2},{7,3},{8,12},{9,13},{10,... | collective-permute-start | bytes 393224 | tf_op jit(solution)/shard_map/rows_z_2/ppermute | solution.py:37
  27.1 4.7 %collective-permute-done.6.refs_3_ = bf16[32,8320]{1,0:T(8,128)(2,1)S(1)} collective-permute-done((bf16[32,8320]{1,0:T(8,128)(2,1)S(1)}, bf16[32,8320]{1,0:T(8,128)(2,1)S(1)}, u32[]{:S(2)}, u32[]{:S(2)}) %collective-permute-start.6) | collective-permute-done | bytes 532512 | tf_op jit(solution)/shard_map/rows_first_3/ppermute | solution.py:31
  31.8 6.9 %collective-permute-done.5.refs_2_ = bf16[32,8320]{1,0:T(8,128)(2,1)S(1)} collective-permute-done((bf16[32,8320]{1,0:T(8,128)(2,1)S(1)}, bf16[32,8320]{1,0:T(8,128)(2,1)S(1)}, u32[]{:S(2)}, u32[]{:S(2)}) %collective-permute-start.5) | collective-permute-done | bytes 532512 | tf_op jit(solution)/shard_map/rows_first_2/ppermute | solution.py:31
  41.6 7.0 %collective-permute-done.10.refs_7_.refs_8_.refs_12_ = bf16[64,4224]{1,0:T(8,128)(2,1)S(1)} collective-permute-done((bf16[64,4224]{1,0:T(8,128)(2,1)S(1)}, bf16[64,4224]{1,0:T(8,128)(2,1)S(1)}, u32[]{:S(2)}, u32[]{:S(2)}) %collective-permute-start.10) | collective-permute-done | bytes 540704 | tf_op jit(solution)/shard_map/rows_second_3/ppermute | solution.py:31
  52.7 5.6 %collective-permute-done.11.refs_6_.refs_5_.refs_10_ = bf16[64,4224]{1,0:T(8,128)(2,1)S(1)} collective-permute-done((bf16[64,4224]{1,0:T(8,128)(2,1)S(1)}, bf16[64,4224]{1,0:T(8,128)(2,1)S(1)}, u32[]{:S(2)}, u32[]{:S(2)}) %collective-permute-start.11) | collective-permute-done | bytes 540704 | tf_op jit(solution)/shard_map/rows_second_3/ppermute | solution.py:31
  58.4 5.0 %collective-permute-done.8.refs_3_.refs_4_.refs_8_ = bf16[64,4224]{1,0:T(8,128)(2,1)S(1)} collective-permute-done((bf16[64,4224]{1,0:T(8,128)(2,1)S(1)}, bf16[64,4224]{1,0:T(8,128)(2,1)S(1)}, u32[]{:S(2)}, u32[]{:S(2)}) %collective-permute-start.8) | collective-permute-done | bytes 540704 | tf_op jit(solution)/shard_map/rows_second_1/ppermute | solution.py:31
  64.1 5.3 %project.1 = (bf16[512,256]{1,0:T(8,128)(2,1)S(1)}, bf16[528,512]{1,0:T(8,128)(2,1)S(1)}, f32[512,384]{1,0:T(8,128)S(1)}) custom-call(bf16[64,4224]{1,0:T(8,128)(2,1)S(1)} %get-tuple-element.79.refs_4_.refs_0_.refs_1_.refs_5_, bf16[64,4224]{1,0:T(8,128)(2,1)S(1)} %get-tuple-element.80.refs_1_.refs_2_.refs_6_, ...), custom_call_target="tpu_custom_call" | custom-call | flops 1 | bytes 1 | tf_op jit(solution)/shard_map/project/pallas_call | solution.py:78
  72.9 3.5 %collective-permute-start.13 = (bf16[528,512]{1,0:T(8,128)(2,1)S(1)}, bf16[528,512]{1,0:T(8,128)(2,1)S(1)}, u32[]{:S(2)}, u32[]{:S(2)}) collective-permute-start(bf16[528,512]{1,0:T(8,128)(2,1)S(1)} %get-tuple-element.82.refs_1_), channel_id=1, source_target_pairs={{0,1},{1,0},{2,3},{3,2},{4,5},{5,4},{6,7},{7,6},{8,9},{9,8},{10,11... | collective-permute-start | bytes 1622024 | tf_op jit(solution)/shard_map/pair_core/ppermute | solution.py:42
  76.4 4.1 %collective-permute-done.14.refs_3_ = bf16[528,512]{1,0:T(8,128)(2,1)S(1)} collective-permute-done((bf16[528,512]{1,0:T(8,128)(2,1)S(1)}, bf16[528,512]{1,0:T(8,128)(2,1)S(1)}, u32[]{:S(2)}, u32[]{:S(2)}) %collective-permute-start.14) | collective-permute-done | bytes 540704 | tf_op jit(solution)/shard_map/pair_chip/ppermute | solution.py:47
  80.6 3.6 %collective-permute-start.15 = (bf16[528,512]{1,0:T(8,128)(2,1)S(1)}, bf16[528,512]{1,0:T(8,128)(2,1)S(1)}, u32[]{:S(2)}, u32[]{:S(2)}) collective-permute-start(bf16[528,512]{1,0:T(8,128)(2,1)S(1)} %collective-permute-done.14.refs_3_), channel_id=1, source_target_pairs={{0,1},{1,0},{2,3},{3,2},{4,5},{5,4},{6,7},{7,6},{8,9},{9,8},{10,11... | collective-permute-start | bytes 1622024 | tf_op jit(solution)/shard_map/far_pair_core/ppermute | solution.py:42
  88.5 6.2 %attention_forward.1 = (bf16[512,256]{1,0:T(8,128)(2,1)S(1)}, bf16[2,512,2048]{2,1,0:T(8,128)(2,1)S(1)}) custom-call(bf16[512,256]{1,0:T(8,128)(2,1)S(1)} %get-tuple-element.81.refs_2_.refs_0_, bf16[528,512]{1,0:T(8,128)(2,1)S(1)} %get-tuple-element.82.refs_1_, bf16[528,512]{1,0:T(8,128)(2,1)S(1)} %collective-permute-done.13.refs_2_, ...), custom_call_target="tpu_custom_call" | custom-call | flops 1 | bytes 1 | tf_op jit(solution)/shard_map/attention_forward/pallas_call | solution.py:78
  100.6 5.2 %attention_backward.1 = (bf16[512,256]{1,0:T(8,128)(2,1)S(1)}, bf16[512,512]{1,0:T(8,128)(2,1)S(1)}, bf16[512,512]{1,0:T(8,128)(2,1)S(1)}, bf16[1024,512]{1,0:T(8,128)(2,1)S(1)}) custom-call(bf16[512,256]{1,0:T(8,128)(2,1)S(1)} %get-tuple-element.81.refs_2_.refs_0_, bf16[528,512]{1,0:T(8,128)(2,1)S(1)} %get-tuple-element.82.refs_1_, ...), custom_call_target="tpu_custom_call" | custom-call | flops 1 | bytes 1 | tf_op jit(solution)/shard_map/attention_backward/pallas_call | solution.py:78
  105.8 5.0 %collective-permute-start.20 = (bf16[1024,512]{1,0:T(8,128)(2,1)S(1)}, bf16[1024,512]{1,0:T(8,128)(2,1)S(1)}, u32[]{:S(2)}, u32[]{:S(2)}) collective-permute-start(bf16[1024,512]{1,0:T(8,128)(2,1)S(1)} %get-tuple-element.90), channel_id=1, source_target_pairs={{0,1},{1,0},{2,3},{3,2},{4,5},{5,4},{6,7},{7,6},{8,9},{9,8},{10,11... | collective-permute-start | bytes 3145736 | tf_op jit(solution)/shard_map/key_grads_core/ppermute | solution.py:42
  114.3 4.7 %query_weights.1 = (bf16[4,512,512]{2,1,0:T(8,128)(2,1)S(1)}, bf16[4,512,512]{2,1,0:T(8,128)(2,1)S(1)}) custom-call(s32[2]{0:T(128)S(1)} %pad_add_fusion.1.refs_0_, bf16[64,4224]{1,0:T(8,128)(2,1)S(1)} %get-tuple-element.79.refs_4_.refs_0_.refs_1_.refs_5_, bf16[64,4224]{1,0:T(8,128)(2,1)S(1)} %get-tuple-element.80.refs_1_.refs_2_.refs_6_, ...), custom_call_target="tpu_custom_call" | custom-call | flops 1 | bytes 1 | tf_op jit(solution)/shard_map/query_weights/pallas_call | solution.py:78
  122.0 3.2 %collective-permute-done.25.refs_17_.refs_5_ = bf16[128,4096]{1,0:T(8,128)(2,1)S(1)} collective-permute-done((bf16[128,4096]{1,0:T(8,128)(2,1)S(1)}, bf16[128,4096]{1,0:T(8,128)(2,1)S(1)}, u32[]{:S(2)}, u32[]{:S(2)}) %collective-permute-start.25) | collective-permute-done | bytes 1048608 | tf_op jit(solution)/shard_map/out_second_1/ppermute | solution.py:31
  125.2 3.3 %collective-permute-done.24.refs_16_.refs_4_ = bf16[128,4096]{1,0:T(8,128)(2,1)S(1)} collective-permute-done((bf16[128,4096]{1,0:T(8,128)(2,1)S(1)}, bf16[128,4096]{1,0:T(8,128)(2,1)S(1)}, u32[]{:S(2)}, u32[]{:S(2)}) %collective-permute-start.24) | collective-permute-done | bytes 1048608 | tf_op jit(solution)/shard_map/out_second_3/ppermute | solution.py:31
  128.5 6.2 %feature_parts.1 = (bf16[512,768]{1,0:T(8,128)(2,1)}, bf16[512,512]{1,0:T(8,128)(2,1)S(1)}, bf16[128,4224]{1,0:T(8,128)(2,1)S(1)}, bf16[128,4224]{1,0:T(8,128)(2...) custom-call(bf16[512,512]{1,0:T(8,128)(2,1)S(1)} %get-tuple-element.89.refs_0_, ...), custom_call_target="tpu_custom_call" | custom-call | flops 30000001024 | bytes 1 | tf_op jit(solution)/shard_map/feature_parts/pallas_call | solution.py:78
  140.6 3.8 %collective-permute-done.26.refs_1_ = bf16[64,4224]{1,0:T(8,128)(2,1)S(1)} collective-permute-done((bf16[64,4224]{1,0:T(8,128)(2,1)S(1)}, bf16[64,4224]{1,0:T(8,128)(2,1)S(1)}, u32[]{:S(2)}, u32[]{:S(2)}) %collective-permute-start.26) | collective-permute-done | bytes 540704 | tf_op jit(solution)/shard_map/grad_second_3/ppermute | solution.py:31
  149.1 4.5 %key_weights.1 = (bf16[4,512,512]{2,1,0:T(8,128)(2,1)S(1)}, bf16[4,512,512]{2,1,0:T(8,128)(2,1)S(1)}) custom-call(s32[2]{0:T(128)S(1)} %pad_add_fusion.1.refs_0_, bf16[64,4224]{1,0:T(8,128)(2,1)S(1)} %get-tuple-element.79.refs_4_.refs_0_.refs_1_.refs_5_, bf16[64,4224]{1,0:T(8,128)(2,1)S(1)} %get-tuple-element.80.refs_1_.refs_2_.refs_6_, ...), custom_call_target="tpu_custom_call" | custom-call | flops 1 | bytes 1 | tf_op jit(solution)/shard_map/key_weights/pallas_call | solution.py:78
  153.6 3.7 %collective-permute-start.38 = (bf16[4,512,512]{2,1,0:T(8,128)(2,1)S(1)}, bf16[4,512,512]{2,1,0:T(8,128)(2,1)S(1)}, u32[]{:S(2)}, u32[]{:S(2)}) collective-permute-start(bf16[4,512,512]{2,1,0:T(8,128)(2,1)S(1)} %get-tuple-element.122), channel_id=1, source_target_pairs={{0,1},{1,0},{2,3},{3,2},{4,5},{5,4},{6,7},{7,6},{8,9},{9,8},{10,11... | collective-permute-start | bytes 6291464 | tf_op jit(solution)/shard_map/key_weights_core/ppermute | solution.py:42
  164.6 3.6 %collective-permute-start.36 = (bf16[32,8320]{1,0:T(8,128)(2,1)}, bf16[32,8320]{1,0:T(8,128)(2,1)S(1)}, u32[]{:S(2)}, u32[]{:S(2)}) collective-permute-start(bf16[32,8320]{1,0:T(8,128)(2,1)} %get-tuple-element.120), channel_id=1, source_target_pairs={{0,16},{1,65},{2,18},{3,67},{4,20},{5,69},{6,22},{7,71},{8,24},{9,... | collective-permute-start | bytes 1597448 | tf_op jit(solution)/shard_map/sum_first_2/ppermute | solution.py:31
  193.4 10.3 %collective-permute-start.44 = (bf16[4,32,1152]{2,1,0:T(8,128)(2,1)}, bf16[4,32,1152]{2,1,0:T(8,128)(2,1)S(1)}, u32[]{:S(2)}, u32[]{:S(2)}) collective-permute-start(bf16[4,32,1152]{2,1,0:T(8,128)(2,1)} %get-tuple-element.134), channel_id=1, source_target_pairs={{0,1},{1,0},{2,3},{3,2},{4,5},{5,4},{6,7},{7,6},{8,9},{9,8},{10,11... | collective-permute-start | bytes 884744 | tf_op jit(solution)/shard_map/final_core/ppermute | solution.py:42
  205.5 3.1 %grad_placed.1.refs_8_ = bf16[2048,512]{1,0:T(8,128)(2,1)} custom-call(s32[2]{0:T(128)S(1)} %pad_add_fusion.1.refs_0_, bf16[2048,512]{1,0:T(8,128)(2,1)S(1)} %bitcast.42, s32[1,256]{1,0:T(1,128)S(1)} %reshape.156.refs_2_, bf16[32,2176]{1,0:T(8,128)(2,1)S(1)} %get-tuple-element.124.refs_6_.refs_1_.refs_3_, ...), custom_call_target="tpu_custom_call" | custom-call | flops 1 | bytes 1 | tf_op jit(solution)/shard_map/grad_placed/pallas_call | solution.py:78
  214.0 3.6 %collective-permute-done.46.refs_5_ = bf16[512,512]{1,0:T(8,128)(2,1)} collective-permute-done((bf16[512,512]{1,0:T(8,128)(2,1)}, bf16[512,512]{1,0:T(8,128)(2,1)}, u32[]{:S(2)}, u32[]{:S(2)}) %collective-permute-start.46) | collective-permute-done | bytes 524320 | tf_op jit(solution)/shard_map/key_weights_z_3/ppermute | solution.py:37
  (182 shorter events, 98.4 us)
Async XLA Ops:
  23.5 15.3 %collective-permute-start.5 = (bf16[32,8320]{1,0:T(8,128)(2,1)S(1)}, bf16[32,8320]{1,0:T(8,128)(2,1)S(1)}, u32[]{:S(2)}, u32[]{:S(2)}) collective-permute-start(bf16[32,8320]{1,0:T(8,128)(2,1)S(1)} %get-tuple-element.77.refs_0_), channel_id=1, source_target_pairs={{0,16},{1,65},{2,18},{3,67},{4,20},{5,69},{6,22},{7,71},{8,24},{9,... | collective-permute-start | bytes 1597448 | tf_op jit(solution)/shard_map/rows_first_2/ppermute | solution.py:31
  26.1 12.7 %collective-permute-start.4 = (bf16[32,8320]{1,0:T(8,128)(2,1)S(1)}, bf16[32,8320]{1,0:T(8,128)(2,1)S(1)}, u32[]{:S(2)}, u32[]{:S(2)}) collective-permute-start(bf16[32,8320]{1,0:T(8,128)(2,1)S(1)} %get-tuple-element.77.refs_0_), channel_id=1, source_target_pairs={{0,24},{1,97},{2,26},{3,99},{4,28},{5,101},{6,30},{7,103},{8,0},{9... | collective-permute-start | bytes 1597448 | tf_op jit(solution)/shard_map/rows_first_1/ppermute | solution.py:31
  51.3 12.8 %collective-permute-start.12 = (bf16[64,4224]{1,0:T(8,128)(2,1)S(1)}, bf16[64,4224]{1,0:T(8,128)(2,1)S(1)}, u32[]{:S(2)}, u32[]{:S(2)}) collective-permute-start(bf16[64,4224]{1,0:T(8,128)(2,1)S(1)} %get-tuple-element.79.refs_4_.refs_0_.refs_1_.refs_5_), channel_id=1, source_target_pairs={{0,32},{1,9},{2,34},{3,11},{4,36},{5,13},{6,38},{7,15},{8,40},{9,1... | collective-permute-start | bytes 1622024 | tf_op jit(solution)/shard_map/rows_second_3/ppermute | solution.py:31
  70.2 15.2 %collective-permute-start.17 = (bf16[128,4096]{1,0:T(8,128)(2,1)S(1)}, bf16[128,4096]{1,0:T(8,128)(2,1)S(1)}, u32[]{:S(2)}, u32[]{:S(2)}) collective-permute-start(bf16[128,4096]{1,0:T(8,128)(2,1)S(1)} %stack_g.1.refs_11_.refs_0_.refs_9_), channel_id=1, source_target_pairs={{0,32},{1,9},{2,34},{3,11},{4,36},{5,13},{6,38},{7,15},{8,40},{9,1... | collective-permute-start | bytes 3145736 | tf_op jit(solution)/shard_map/rows_second_3/ppermute | solution.py:31
  70.2 15.2 %collective-permute-start.16 = (bf16[128,4096]{1,0:T(8,128)(2,1)S(1)}, bf16[128,4096]{1,0:T(8,128)(2,1)S(1)}, u32[]{:S(2)}, u32[]{:S(2)}) collective-permute-start(bf16[128,4096]{1,0:T(8,128)(2,1)S(1)} %stack_g.1.refs_11_.refs_0_.refs_9_), channel_id=1, source_target_pairs={{0,96},{1,25},{2,98},{3,27},{4,100},{5,29},{6,102},{7,31},{8,104},... | collective-permute-start | bytes 3145736 | tf_op jit(solution)/shard_map/rows_second_1/ppermute | solution.py:31
  72.9 15.6 %collective-permute-start.13 = (bf16[528,512]{1,0:T(8,128)(2,1)S(1)}, bf16[528,512]{1,0:T(8,128)(2,1)S(1)}, u32[]{:S(2)}, u32[]{:S(2)}) collective-permute-start(bf16[528,512]{1,0:T(8,128)(2,1)S(1)} %get-tuple-element.82.refs_1_), channel_id=1, source_target_pairs={{0,1},{1,0},{2,3},{3,2},{4,5},{5,4},{6,7},{7,6},{8,9},{9,8},{10,11... | collective-permute-start | bytes 1622024 | tf_op jit(solution)/shard_map/pair_core/ppermute | solution.py:42
  85.5 13.2 %collective-permute-start.19 = (bf16[64,4096]{1,0:T(8,128)(2,1)S(1)}, bf16[64,4096]{1,0:T(8,128)(2,1)S(1)}, u32[]{:S(2)}, u32[]{:S(2)}) collective-permute-start(bf16[64,4096]{1,0:T(8,128)(2,1)S(1)} %get-tuple-element.86), channel_id=1, source_target_pairs={{0,32},{1,9},{2,34},{3,11},{4,36},{5,13},{6,38},{7,15},{8,40},{9,1... | collective-permute-start | bytes 1572872 | tf_op jit(solution)/shard_map/rows_second_3/ppermute | solution.py:31
  86.4 12.3 %collective-permute-start.18 = (bf16[64,4096]{1,0:T(8,128)(2,1)S(1)}, bf16[64,4096]{1,0:T(8,128)(2,1)S(1)}, u32[]{:S(2)}, u32[]{:S(2)}) collective-permute-start(bf16[64,4096]{1,0:T(8,128)(2,1)S(1)} %get-tuple-element.84.refs_6_), channel_id=1, source_target_pairs={{0,96},{1,25},{2,98},{3,27},{4,100},{5,29},{6,102},{7,31},{8,104},... | collective-permute-start | bytes 1572872 | tf_op jit(solution)/shard_map/rows_second_1/ppermute | solution.py:31
  97.1 13.7 %collective-permute-start.22 = (bf16[64,4096]{1,0:T(8,128)(2,1)S(1)}, bf16[64,4096]{1,0:T(8,128)(2,1)S(1)}, u32[]{:S(2)}, u32[]{:S(2)}) collective-permute-start(bf16[64,4096]{1,0:T(8,128)(2,1)S(1)} %get-tuple-element.94), channel_id=1, source_target_pairs={{0,96},{1,25},{2,98},{3,27},{4,100},{5,29},{6,102},{7,31},{8,104},... | collective-permute-start | bytes 1572872 | tf_op jit(solution)/shard_map/out_second_1/ppermute | solution.py:31
  98.4 12.4 %collective-permute-start.21 = (bf16[64,4096]{1,0:T(8,128)(2,1)S(1)}, bf16[64,4096]{1,0:T(8,128)(2,1)S(1)}, u32[]{:S(2)}, u32[]{:S(2)}) collective-permute-start(bf16[64,4096]{1,0:T(8,128)(2,1)S(1)} %get-tuple-element.88.refs_6_), channel_id=1, source_target_pairs={{0,32},{1,9},{2,34},{3,11},{4,36},{5,13},{6,38},{7,15},{8,40},{9,1... | collective-permute-start | bytes 1572872 | tf_op jit(solution)/shard_map/out_second_3/ppermute | solution.py:31
  111.0 14.1 %collective-permute-start.25 = (bf16[128,4096]{1,0:T(8,128)(2,1)S(1)}, bf16[128,4096]{1,0:T(8,128)(2,1)S(1)}, u32[]{:S(2)}, u32[]{:S(2)}) collective-permute-start(bf16[128,4096]{1,0:T(8,128)(2,1)S(1)} %get-tuple-element.98), channel_id=1, source_target_pairs={{0,96},{1,25},{2,98},{3,27},{4,100},{5,29},{6,102},{7,31},{8,104},... | collective-permute-start | bytes 3145736 | tf_op jit(solution)/shard_map/out_second_1/ppermute | solution.py:31
  113.4 15.2 %collective-permute-start.24 = (bf16[128,4096]{1,0:T(8,128)(2,1)S(1)}, bf16[128,4096]{1,0:T(8,128)(2,1)S(1)}, u32[]{:S(2)}, u32[]{:S(2)}) collective-permute-start(bf16[128,4096]{1,0:T(8,128)(2,1)S(1)} %get-tuple-element.96.refs_2_), channel_id=1, source_target_pairs={{0,32},{1,9},{2,34},{3,11},{4,36},{5,13},{6,38},{7,15},{8,40},{9,1... | collective-permute-start | bytes 3145736 | tf_op jit(solution)/shard_map/out_second_3/ppermute | solution.py:31
  113.4 15.1 %collective-permute-start.23 = (bf16[512,512]{1,0:T(8,128)(2,1)S(1)}, bf16[512,512]{1,0:T(8,128)(2,1)S(1)}, u32[]{:S(2)}, u32[]{:S(2)}) collective-permute-start(bf16[512,512]{1,0:T(8,128)(2,1)S(1)} %chip_sum.1.refs_16_), channel_id=1, source_target_pairs={{0,2},{1,3},{2,0},{3,1},{4,6},{5,7},{6,4},{7,5},{8,10},{9,11},{10,... | collective-permute-start | bytes 1572872 | tf_op jit(solution)/shard_map/key_grads_chip/ppermute | solution.py:47
  119.0 18.5 %collective-permute-start.28 = (bf16[4,512,512]{2,1,0:T(8,128)(2,1)S(1)}, bf16[4,512,512]{2,1,0:T(8,128)(2,1)S(1)}, u32[]{:S(2)}, u32[]{:S(2)}) collective-permute-start(bf16[4,512,512]{2,1,0:T(8,128)(2,1)S(1)} %get-tuple-element.104), channel_id=1, source_target_pairs={{0,1},{1,0},{2,3},{3,2},{4,5},{5,4},{6,7},{7,6},{8,9},{9,8},{10,11... | collective-permute-start | bytes 6291464 | tf_op jit(solution)/shard_map/query_weights_core/ppermute | solution.py:42
  144.7 15.5 %collective-permute-start.30 = (bf16[128,4224]{1,0:T(8,128)(2,1)S(1)}, bf16[128,4224]{1,0:T(8,128)(2,1)S(1)}, u32[]{:S(2)}, u32[]{:S(2)}) collective-permute-start(bf16[128,4224]{1,0:T(8,128)(2,1)S(1)} %get-tuple-element.108), channel_id=1, source_target_pairs={{0,96},{1,25},{2,98},{3,27},{4,100},{5,29},{6,102},{7,31},{8,104},... | collective-permute-start | bytes 3244040 | tf_op jit(solution)/shard_map/grad_second_1/ppermute | solution.py:31
  147.4 15.5 %collective-permute-start.29 = (bf16[128,4224]{1,0:T(8,128)(2,1)S(1)}, bf16[128,4224]{1,0:T(8,128)(2,1)S(1)}, u32[]{:S(2)}, u32[]{:S(2)}) collective-permute-start(bf16[128,4224]{1,0:T(8,128)(2,1)S(1)} %get-tuple-element.107.refs_6_), channel_id=1, source_target_pairs={{0,32},{1,9},{2,34},{3,11},{4,36},{5,13},{6,38},{7,15},{8,40},{9,1... | collective-permute-start | bytes 3244040 | tf_op jit(solution)/shard_map/grad_second_3/ppermute | solution.py:31
  153.6 15.3 %collective-permute-start.38 = (bf16[4,512,512]{2,1,0:T(8,128)(2,1)S(1)}, bf16[4,512,512]{2,1,0:T(8,128)(2,1)S(1)}, u32[]{:S(2)}, u32[]{:S(2)}) collective-permute-start(bf16[4,512,512]{2,1,0:T(8,128)(2,1)S(1)} %get-tuple-element.122), channel_id=1, source_target_pairs={{0,1},{1,0},{2,3},{3,2},{4,5},{5,4},{6,7},{7,6},{8,9},{9,8},{10,11... | collective-permute-start | bytes 6291464 | tf_op jit(solution)/shard_map/key_weights_core/ppermute | solution.py:42
  164.6 19.0 %collective-permute-start.35 = (bf16[32,8320]{1,0:T(8,128)(2,1)}, bf16[32,8320]{1,0:T(8,128)(2,1)S(1)}, u32[]{:S(2)}, u32[]{:S(2)}) collective-permute-start(bf16[32,8320]{1,0:T(8,128)(2,1)} %get-tuple-element.119), channel_id=1, source_target_pairs={{0,8},{1,33},{2,10},{3,35},{4,12},{5,37},{6,14},{7,39},{8,16},{9,4... | collective-permute-start | bytes 1597448 | tf_op jit(solution)/shard_map/sum_first_3/ppermute | solution.py:31
  164.6 19.0 %collective-permute-start.36 = (bf16[32,8320]{1,0:T(8,128)(2,1)}, bf16[32,8320]{1,0:T(8,128)(2,1)S(1)}, u32[]{:S(2)}, u32[]{:S(2)}) collective-permute-start(bf16[32,8320]{1,0:T(8,128)(2,1)} %get-tuple-element.120), channel_id=1, source_target_pairs={{0,16},{1,65},{2,18},{3,67},{4,20},{5,69},{6,22},{7,71},{8,24},{9,... | collective-permute-start | bytes 1597448 | tf_op jit(solution)/shard_map/sum_first_2/ppermute | solution.py:31
  168.2 15.4 %collective-permute-start.37 = (bf16[32,8320]{1,0:T(8,128)(2,1)}, bf16[32,8320]{1,0:T(8,128)(2,1)S(1)}, u32[]{:S(2)}, u32[]{:S(2)}) collective-permute-start(bf16[32,8320]{1,0:T(8,128)(2,1)} %get-tuple-element.121), channel_id=1, source_target_pairs={{0,24},{1,97},{2,26},{3,99},{4,28},{5,101},{6,30},{7,103},{8,0},{9... | collective-permute-start | bytes 1597448 | tf_op jit(solution)/shard_map/sum_first_1/ppermute | solution.py:31
  172.0 15.9 %collective-permute-start.42 = (bf16[256,512]{1,0:T(8,128)(2,1)}, bf16[256,512]{1,0:T(8,128)(2,1)}, u32[]{:S(2)}, u32[]{:S(2)}) collective-permute-start(bf16[256,512]{1,0:T(8,128)(2,1)} %get-tuple-element.128), channel_id=1, source_target_pairs={{0,2},{1,3},{2,4},{3,5},{4,6},{5,7},{6,0},{7,1},{8,10},{9,11},{10,... | collective-permute-start | bytes 786440 | tf_op jit(solution)/shard_map/key_weights_z_1/ppermute | solution.py:37
  172.8 15.1 %collective-permute-start.43 = (bf16[256,512]{1,0:T(8,128)(2,1)}, bf16[256,512]{1,0:T(8,128)(2,1)}, u32[]{:S(2)}, u32[]{:S(2)}) collective-permute-start(bf16[256,512]{1,0:T(8,128)(2,1)} %get-tuple-element.132), channel_id=1, source_target_pairs={{0,6},{1,7},{2,0},{3,1},{4,2},{5,3},{6,4},{7,5},{8,14},{9,15},{10,... | collective-permute-start | bytes 786440 | tf_op jit(solution)/shard_map/key_weights_z_3/ppermute | solution.py:37
  190.9 26.7 %collective-permute-start.45 = (bf16[512,512]{1,0:T(8,128)(2,1)}, bf16[512,512]{1,0:T(8,128)(2,1)S(1)}, u32[]{:S(2)}, u32[]{:S(2)}) collective-permute-start(bf16[512,512]{1,0:T(8,128)(2,1)} %get-tuple-element.133.refs_5_), channel_id=1, source_target_pairs={{0,2},{1,3},{2,4},{3,5},{4,6},{5,7},{6,0},{7,1},{8,10},{9,11},{10,... | collective-permute-start | bytes 1572872 | tf_op jit(solution)/shard_map/key_weights_z_1/ppermute | solution.py:37
  203.7 13.9 %collective-permute-start.46 = (bf16[512,512]{1,0:T(8,128)(2,1)}, bf16[512,512]{1,0:T(8,128)(2,1)}, u32[]{:S(2)}, u32[]{:S(2)}) collective-permute-start(bf16[512,512]{1,0:T(8,128)(2,1)} %get-tuple-element.138), channel_id=1, source_target_pairs={{0,6},{1,7},{2,0},{3,1},{4,2},{5,3},{6,4},{7,5},{8,14},{9,15},{10,... | collective-permute-start | bytes 1572872 | tf_op jit(solution)/shard_map/key_weights_z_3/ppermute | solution.py:37
  (54 other events, 426.8 us)

commit v2 on v1

--- a/solution.py
+++ b/solution.py
@@ -64,7 +64,7 @@
 
 
 ORDER = []
-COSTS = {"out_add": 20, "feature_parts": 30, "sum_column": 30, "query_weights_near": 20}
+COSTS = {"out_add": 20, "feature_parts": 30, "sum_column": 30, "query_weights_near": 20, "stack_g": 20, "halves_g": 5}
 
 
 def call(kernel, name, out_shape, room=8, after=(), cost=0, **options):
@@ -136,7 +136,7 @@
         pick_kernel,
         "pick_rows",
         [shape(2, 2, 32, 512)] * 4,
-        room=12,
+        room=56,
         grid=(2,),
         in_specs=[SMEM, pl.BlockSpec((1, 1, 128), lambda s: (s, 0, 0)), block, block],
         out_specs=[pl.BlockSpec((2, 2, 32, 512), lambda s: (0, 0, 0, 0))] * 4,
@@ -210,9 +210,9 @@
         in_specs=[WHOLE] * 4,
         out_specs=[WHOLE] * 2,
     )(*pieces)
-    plus_low, minus_high = ring(low, True, 1), ring(high, True, 3)
-    plus_high, minus_low = ring(high, True, 1), ring(low, True, 3)
-    far_low, far_high = ring(plus_low, True, 1), ring(minus_high, True, 3)
+    plus_low, minus_high = ring(low, True, 1, "x_1"), ring(high, True, 3, "x_1")
+    plus_high, minus_low = ring(high, True, 1, "x_2"), ring(low, True, 3, "x_2")
+    far_low, far_high = ring(plus_low, True, 1, "x_far"), ring(minus_high, True, 3, "x_far")
     return [low, high, plus_low, plus_high, far_low, far_high, minus_low, minus_high]
 
 
@@ -225,7 +225,7 @@
         in_specs=[WHOLE] * 4,
         out_specs=WHOLE,
     )(*pieces)
-    return column, ring(column, True, 1), ring(column, True, 3)
+    return column, ring(column, True, 1, "g"), ring(column, True, 3, "g")
 
 
 def gather_g_far(column, plus, minus):
@@ -236,7 +236,7 @@
         in_specs=[WHOLE] * 2,
         out_specs=[WHOLE] * 2,
     )(plus, minus)
-    return [column, plus, ring(first, True, 1), ring(second, True, 3), minus]
+    return [column, plus, ring(first, True, 1, "g_far"), ring(second, True, 3, "g_far"), minus]
 
 
 def add_kernel(a, ta, b, tb, out_a, out_b):
@@ -543,108 +543,114 @@
     return out[1], out[2:]
 
 
+def put_slice(i, values, kept, far, rest):
+    @pl.when(i == 0)
+    def _():
+        far[...] = values
+
+    @pl.when((i > 0) & (i < 4))
+    def _():
+        rest[jnp.clip(i - 1, 0, 2)] = values
+
+    @pl.when(i >= 4)
+    def _():
+        kept[lax.rem(i, 4)] = values
+
+
+def slice_columns(where, i):
+    step = lax.rem(i, 4)
+    shift = jnp.where(step == 0, 2, jnp.where(step == 3, 3, step - 1))
+    core = jnp.where(i < 4, 1 - where[1], where[1])
+    return tile(lax.rem(where[0] + shift, 4) * 2 + core, 512)
+
+
 def query_weight_kernel(where, *refs):
-    x, g, (gq, att, kept, sent, left) = refs[:8], refs[8:13], refs[13:]
+    x, g, (gq, att, kept, far, rest, left) = refs[:8], refs[8:13], refs[13:]
     left[:256] = gq[...].T
     left[256:] = att[...].T
 
     @pl.loop(0, 8)
     def _(i):
-        slot = lax.rem(i, 4)
-        core = jnp.where(i < 4, 1 - where[1], where[1])
-        columns = tile(lax.rem(where[0] + slot, 4) * 2 + core, 512)
+        columns = slice_columns(where, i)
         a = jnp.dot(left[:256], joined(x, columns), preferred_element_type=F32)
         b = jnp.dot(left[256:], joined(g, columns), preferred_element_type=F32)
 
-        @pl.when(i < 4)
-        def _():
-            sent[slot, :256] = a.astype(BF)
-            sent[slot, 256:] = b.astype(BF)
-
-        @pl.when(i >= 4)
-        def _():
-            kept[slot, :256] = a.astype(BF)
-            kept[slot, 256:] = b.astype(BF)
+        put_slice(i, jnp.concatenate([a, b], 0).astype(BF), kept, far, rest)
 
 
 def query_weights(where, x, g, gq, att):
     return call(
         query_weight_kernel,
         "query_weights",
-        [shape(4, 512, 512)] * 2,
+        [shape(4, 512, 512), shape(512, 512), shape(3, 512, 512)],
         room=20,
         in_specs=[SMEM] + [WHOLE] * 15,
-        out_specs=[WHOLE] * 2,
+        out_specs=[WHOLE] * 3,
         scratch_shapes=[pltpu.VMEM((512, 512), BF)],
     )(where, *x, *g, gq, att)
 
 
 def key_weight_kernel(where, *refs):
-    x, (left, kept, sent) = refs[:8], refs[8:]
+    x, (left, kept, far, rest) = refs[:8], refs[8:]
 
     @pl.loop(0, 8)
     def _(i):
-        slot = lax.rem(i, 4)
-        core = jnp.where(i < 4, 1 - where[1], where[1])
-        columns = tile(lax.rem(where[0] + slot, 4) * 2 + core, 512)
+        columns = slice_columns(where, i)
         a = jnp.dot(left[...], joined(x, columns), preferred_element_type=F32).astype(BF)
 
-        @pl.when(i < 4)
-        def _():
-            sent[slot] = a
-
-        @pl.when(i >= 4)
-        def _():
-            kept[slot] = a
+        put_slice(i, a, kept, far, rest)
 
 
 def key_weights(where, x, left):
     return call(
         key_weight_kernel,
         "key_weights",
-        [shape(4, 512, 512)] * 2,
+        [shape(4, 512, 512), shape(512, 512), shape(3, 512, 512)],
         room=16,
         in_specs=[SMEM] + [WHOLE] * 9,
+        out_specs=[WHOLE] * 3,
+    )(where, *x, left)
+
+
+def sum_far_kernel(kept, recv, low, high):
+    low[...] = kept[0, :256] + recv[:256]
+    high[...] = kept[0, 256:] + recv[256:]
+
+
+def swap_weights(parts, name):
+    kept, far, rest = parts
+    return kept, swap_core(far, name + "_far"), swap_core(rest, name)
+
+
+def sum_far(parts, name):
+    kept, far, rest = parts
+    low, high = call(
+        sum_far_kernel,
+        name + "_far",
+        [shape(256, 512)] * 2,
+        in_specs=[WHOLE] * 2,
         out_specs=[WHOLE] * 2,
-    )(where, *x, left)
-
-
-def sum_cores_kernel(a, b, own, plus_low, plus_high, far_low, far_high, minus_low, minus_high):
-    own[...] = a[0] + b[0]
-    outs = ((plus_low, plus_high), (far_low, far_high), (minus_low, minus_high))
-    for d, (low, high) in enumerate(outs):
-        low[...] = a[d + 1, :256] + b[d + 1, :256]
-        high[...] = a[d + 1, 256:] + b[d + 1, 256:]
-
-
-def sum_cores(keep, recv, name):
-    parts = call(
-        sum_cores_kernel,
-        name + "_cores",
-        [shape(n, 512) for n in (512,) + (256,) * 6],
-        in_specs=[WHOLE] * 2,
-        out_specs=[WHOLE] * 7,
-    )(keep, recv)
-    return parts, send_z(parts[3], 1, name), send_z(parts[4], 3, name)
-
-
-def join_kernel(plus_low, to_plus, plus_high, minus_low, minus_high, to_minus, out_a, out_b):
-    out_a[:256] = plus_low[...] + to_plus[...]
-    out_a[256:] = plus_high[...]
-    out_b[:256] = minus_low[...]
-    out_b[256:] = minus_high[...] + to_minus[...]
+    )(kept, far)
+    return kept, rest, send_z(low, 1, name + "_far"), send_z(high, 3, name + "_far")
+
+
+def sum_near_kernel(kept, rest, to_plus, to_minus, own, plus, minus):
+    own[...] = kept[1] + rest[0]
+    plus[:256] = kept[2, :256] + rest[1, :256] + to_plus[...]
+    plus[256:] = kept[2, 256:] + rest[1, 256:]
+    minus[:256] = kept[3, :256] + rest[2, :256]
+    minus[256:] = kept[3, 256:] + rest[2, 256:] + to_minus[...]
 
 
 def sum_near(state, name):
-    parts, to_plus, to_minus = state
-    plus, minus = call(
-        join_kernel,
+    own, plus, minus = call(
+        sum_near_kernel,
         name + "_near",
-        [shape(512, 512)] * 2,
-        in_specs=[WHOLE] * 6,
-        out_specs=[WHOLE] * 2,
-    )(parts[1], to_plus, parts[2], parts[5], parts[6], to_minus)
-    return parts[0], send_z(plus, 1, name), send_z(minus, 3, name)
+        [shape(512, 512)] * 3,
+        in_specs=[WHOLE] * 4,
+        out_specs=[WHOLE] * 3,
+    )(*state)
+    return own, send_z(plus, 1, name), send_z(minus, 3, name)
 
 
 def sum_weights_kernel(a0, a1, a2, b0, b1, b2, in_grad, out_grad):
@@ -746,6 +752,7 @@
         kernel,
         name + "_placed",
         shape(2048, 512),
+        room=56,
         grid=(4,),
         in_specs=[SMEM, block, pl.BlockSpec((1, 256), fixed)]
         + [pl.BlockSpec(pieces[0].shape, fixed)] * 4
@@ -773,11 +780,11 @@
 
     picked = pick_rows(where, route_index, hidden_in, cotangent)
     picked = [picked[0]] + [send_z(picked[d], d) for d in (1, 2, 3)]
-    w_in = unpack_weights(w_qkv.transpose(0, 2, 1, 3).reshape(24576, 128))
     both_own, rows_own = own_rows(where, picked, gain, code)
     column = gather_first(both_own)
+    w_in = unpack_weights(w_qkv.transpose(0, 2, 1, 3).reshape(24576, 128))
     x = gather_x(column)
-    g_near = gather_g(column, (x[4], x[5]))
+    g_near = gather_g(column, (x[3], x[6]))
 
     queries, own_pair, table = project(x, w_in)
     chip_pair = swap_chip(own_pair, "pair")
@@ -793,22 +800,21 @@
     recv = swap_core(sent, "key_grads")
     out_terms = reduce_add(out_state, "out")
     chip_part = swap_chip(chip_sum(mid, recv), "key_grads")
-    kept_a, sent_a = query_weights(where, x, g, grad_q, attended)
-    recv_a = swap_core(sent_a, "query_weights")
+    swapped_a = swap_weights(query_weights(where, x, g, grad_q, attended), "query_weights")
 
     gp_kv, parts = feature_parts(
         near, recv, chip_part, grad_q, table, x, w_in, gain, out_terms[1:]
     )
     grad_state = reduce_start(parts, "grad")
-    state_a = sum_cores(kept_a, recv_a, "query_weights")
+    state_a = sum_far(swapped_a, "query_weights")
     grad_terms = reduce_add(grad_state, "grad")
     terms_a = sum_near(state_a, "query_weights")
-    kept_b, sent_b = key_weights(where, x, gp_kv)
-    recv_b = swap_core(sent_b, "key_weights")
+    swapped_b = swap_weights(key_weights(where, x, gp_kv), "key_weights")
+    state_b = sum_far(swapped_b, "key_weights")
     column = reduce_column(grad_terms, out_terms, terms_a[1:])
-    state_b = sum_cores(kept_b, recv_b, "key_weights")
+    terms_b = sum_near(state_b, "key_weights")
     final = final_rows(where, *column, rows_own, gain)
-    terms_b = sum_near(state_b, "key_weights")
+    grad_w_qkv, grad_w_out = sum_weights(terms_a, terms_b)
     other, gain_part = other_columns(where, final)
 
     chips = (z - jnp.arange(4)) % 4
@@ -820,7 +826,6 @@
     grad_in = place_rows(where, grad_base, places, final, other, 1, "grad")
     hidden_out = place_rows(where, hidden, places, final, other, 0, "out")
     grad_gain = gain_part + other[0, :, 1024:].astype(F32) + other[1, :, 1024:].astype(F32)
-    grad_w_qkv, grad_w_out = sum_weights(terms_a, terms_b)
     return (
         hidden_out.reshape(2, 1024, 512),
         grad_in.reshape(2, 1024, 512),

time: 223 us -> 218 us (0.978)
  starting transfers between devices: 81.7 us -> 68.6 us
  Pallas kernels: 58.2 us -> 64 us
    ppermute x7 -> x9, starting transfers between devices: 30.8 us -> 15.6 us  [swap_core(): return lax.ppermute(values, 'cmp', [(k, k ^ 1) for k in range(8)])]
    ppermute x24, waiting for transfers between devices: 44.2 us -> 31.5 us  [ring(): return lax.ppermute(values, BOTH, ring_pairs(second, shift))]
    ppermute x14, waiting for transfers between devices: 7.37 us -> 16.6 us  [send_z(): return lax.ppermute(values, 'cmp', pairs)]
    pallas_call x28, Pallas kernels: 58.2 us -> 64 us  [invoke(): pl.pallas_call(body, out_shape=out_shape, compiler_params=pltpu.CompilerP...]
    ppermute x2, waiting for transfers between devices: 4.15 us -> 8.2 us  [swap_chip(): return lax.ppermute(values, 'cmp', [(k, k ^ 2) for k in range(8)])]
    ppermute x24, starting transfers between devices: 30.5 us -> 32.8 us  [ring(): return lax.ppermute(values, BOTH, ring_pairs(second, shift))]
  transfers between devices with their start and end apart: 47 -> 49, of which waited for: 18 -> 14; matrix products, arithmetic and copies ran while one was open for 1% -> 2% of each run, Pallas kernels for 22% -> 23%
where the time goes in v2:
time: 218 us; the launch traced here: 217 us
  starting transfers between devices  68.6 us (31%)
  Pallas kernels  64 us (29%)
  waiting for transfers between devices  57.4 us (26%)
  local copies, waits for them, and re-layouts  16.3 us (7%)
  between operations  8.5 us (4%)
  other arithmetic  2.22 us (1%)
    pallas_call x28, Pallas kernels, invoke(): pl.pallas_call(body, out_shape=out_shape, compiler_params=pltpu.CompilerP...  64 us
    ppermute x24, starting transfers between devices, ring(): return lax.ppermute(values, BOTH, ring_pairs(second, shift))  32.8 us
    ppermute x24, waiting for transfers between devices, ring(): return lax.ppermute(values, BOTH, ring_pairs(second, shift))  31.5 us
    ppermute x14, starting transfers between devices, send_z(): return lax.ppermute(values, 'cmp', pairs)  18.2 us
    ppermute x14, waiting for transfers between devices, send_z(): return lax.ppermute(values, 'cmp', pairs)  16.6 us
    ppermute x9, starting transfers between devices, swap_core(): return lax.ppermute(values, 'cmp', [(k, k ^ 1) for k in range(8)])  15.6 us
    unnamed x63, local copies, waits for them, and re-layouts  13.6 us
    ppermute x2, waiting for transfers between devices, swap_chip(): return lax.ppermute(values, 'cmp', [(k, k ^ 2) for k in range(8)])  8.2 us
  transfers between devices with their start and end apart: 49, of which 14 were waited for; matrix products, arithmetic and copies ran while one was open for 2% of the time, Pallas kernels for 23%

profile of v2, /device:TPU:1, one launch (start us, length us, event | category | flops | bytes accessed | tf_op | source)
XLA Modules:
  0.0 217.0 jit_solution(7935100518040004887)
XLA Ops:
  1.3 3.5 %pick_rows.1 = (bf16[2,2,32,512]{3,2,1,0:T(8,128)(2,1)}, bf16[2,2,32,512]{3,2,1,0:T(8,128)(2,1)}, bf16[2,2,32,512]{3,2,1,0:T(8,128)(2,1)}, bf16[2,2,32,512]{3,2,1,0:T(8,128)(2,1)}) custom-call(s32[2]{0:T(128)} %pad_add_fusion.1.refs_0_, s32[2,1,128]{2,1,0:T(1,128)} %refs_1_.1, bf16[2,1024,512]{2,1,0:T(8,128)(2,1)} %refs_2_.1, bf16[2,1024,512]{2,1,0:T(8,128)(2,1)} %refs_3_.1), custom_call_target="tpu_custom_call" | custom-call | flops 1 | bytes 1 | tf_op jit(solution)/shard_map/pick_rows/pallas_call | solution.py:78
  7.3 3.3 %collective-permute-start.1 = (bf16[2,2,32,512]{3,2,1,0:T(8,128)(2,1)}, bf16[2,2,32,512]{3,2,1,0:T(8,128)(2,1)S(1)}, u32[]{:S(2)}, u32[]{:S(2)}) collective-permute-start(bf16[2,2,32,512]{3,2,1,0:T(8,128)(2,1)} %get-tuple-element.69), channel_id=1, source_target_pairs={{0,4},{1,5},{2,6},{3,7},{4,0},{5,1},{6,2},{7,3},{8,12},{9,13},{10,... | collective-permute-start | bytes 393224 | tf_op jit(solution)/shard_map/rows_z_2/ppermute | solution.py:37
  12.9 3.7 %collective-permute-done.1.refs_3_ = bf16[2,2,32,512]{3,2,1,0:T(8,128)(2,1)S(1)} collective-permute-done((bf16[2,2,32,512]{3,2,1,0:T(8,128)(2,1)}, bf16[2,2,32,512]{3,2,1,0:T(8,128)(2,1)S(1)}, u32[]{:S(2)}, u32[]{:S(2)}) %collective-permute-start.1) | collective-permute-done | bytes 131104 | tf_op jit(solution)/shard_map/rows_z_2/ppermute | solution.py:37
  27.5 2.8 %copy-done.1 = bf16[4096,2,3,128]{3,1,2,0:T(2,128)(2,1)S(1)} copy-done((bf16[4096,2,3,128]{3,1,2,0:T(2,128)(2,1)S(1)}, bf16[4096,2,3,128]{3,1,2,0:T(2,128)(2,1)}, u32[]{:S(2)}) %copy-start.1) | copy-done | bytes 6291480
  32.7 6.5 %collective-permute-done.5.refs_2_ = bf16[32,8320]{1,0:T(8,128)(2,1)S(1)} collective-permute-done((bf16[32,8320]{1,0:T(8,128)(2,1)S(1)}, bf16[32,8320]{1,0:T(8,128)(2,1)S(1)}, u32[]{:S(2)}, u32[]{:S(2)}) %collective-permute-start.5) | collective-permute-done | bytes 532512 | tf_op jit(solution)/shard_map/rows_first_2/ppermute | solution.py:31
  43.4 5.6 %collective-permute-done.10.refs_7_.refs_8_.refs_12_ = bf16[64,4224]{1,0:T(8,128)(2,1)S(1)} collective-permute-done((bf16[64,4224]{1,0:T(8,128)(2,1)S(1)}, bf16[64,4224]{1,0:T(8,128)(2,1)S(1)}, u32[]{:S(2)}, u32[]{:S(2)}) %collective-permute-start.10) | collective-permute-done | bytes 540704 | tf_op jit(solution)/shard_map/x_1_second_3/ppermute | solution.py:31
  51.7 2.8 %collective-permute-done.8.refs_5_.refs_3_.refs_4_.refs_8_ = bf16[64,4224]{1,0:T(8,128)(2,1)S(1)} collective-permute-done((bf16[64,4224]{1,0:T(8,128)(2,1)S(1)}, bf16[64,4224]{1,0:T(8,128)(2,1)S(1)}, u32[]{:S(2)}, u32[]{:S(2)}) %collective-permute-start.8) | collective-permute-done | bytes 540704 | tf_op jit(solution)/shard_map/x_2_second_1/ppermute | solution.py:31
  57.7 2.9 %collective-permute-done.11.refs_5_.refs_6_.refs_10_ = bf16[64,4224]{1,0:T(8,128)(2,1)S(1)} collective-permute-done((bf16[64,4224]{1,0:T(8,128)(2,1)S(1)}, bf16[64,4224]{1,0:T(8,128)(2,1)S(1)}, u32[]{:S(2)}, u32[]{:S(2)}) %collective-permute-start.11) | collective-permute-done | bytes 540704 | tf_op jit(solution)/shard_map/x_far_second_3/ppermute | solution.py:31
  60.6 5.3 %project.1 = (bf16[512,256]{1,0:T(8,128)(2,1)S(1)}, bf16[528,512]{1,0:T(8,128)(2,1)S(1)}, f32[512,384]{1,0:T(8,128)S(1)}) custom-call(bf16[64,4224]{1,0:T(8,128)(2,1)S(1)} %get-tuple-element.73.refs_4_.refs_0_.refs_1_.refs_5_, bf16[64,4224]{1,0:T(8,128)(2,1)S(1)} %get-tuple-element.74.refs_1_.refs_2_.refs_6_, ...), custom_call_target="tpu_custom_call" | custom-call | flops 1 | bytes 1 | tf_op jit(solution)/shard_map/project/pallas_call | solution.py:78
  69.3 8.2 %collective-permute-done.14.refs_3_ = bf16[528,512]{1,0:T(8,128)(2,1)S(1)} collective-permute-done((bf16[528,512]{1,0:T(8,128)(2,1)S(1)}, bf16[528,512]{1,0:T(8,128)(2,1)S(1)}, u32[]{:S(2)}, u32[]{:S(2)}) %collective-permute-start.14) | collective-permute-done | bytes 540704 | tf_op jit(solution)/shard_map/pair_chip/ppermute | solution.py:47
  77.5 3.1 %collective-permute-start.15 = (bf16[528,512]{1,0:T(8,128)(2,1)S(1)}, bf16[528,512]{1,0:T(8,128)(2,1)S(1)}, u32[]{:S(2)}, u32[]{:S(2)}) collective-permute-start(bf16[528,512]{1,0:T(8,128)(2,1)S(1)} %collective-permute-done.14.refs_3_), channel_id=1, source_target_pairs={{0,1},{1,0},{2,3},{3,2},{4,5},{5,4},{6,7},{7,6},{8,9},{9,8},{10,11... | collective-permute-start | bytes 1622024 | tf_op jit(solution)/shard_map/far_pair_core/ppermute | solution.py:42
  83.7 6.3 %attention_forward.1 = (bf16[512,256]{1,0:T(8,128)(2,1)S(1)}, bf16[2,512,2048]{2,1,0:T(8,128)(2,1)S(1)}) custom-call(bf16[512,256]{1,0:T(8,128)(2,1)S(1)} %get-tuple-element.75.refs_2_.refs_0_, bf16[528,512]{1,0:T(8,128)(2,1)S(1)} %get-tuple-element.76.refs_1_, bf16[528,512]{1,0:T(8,128)(2,1)S(1)} %collective-permute-done.13.refs_2_, ...), custom_call_target="tpu_custom_call" | custom-call | flops 1 | bytes 1 | tf_op jit(solution)/shard_map/attention_forward/pallas_call | solution.py:78
  95.9 5.1 %attention_backward.1 = (bf16[512,256]{1,0:T(8,128)(2,1)S(1)}, bf16[512,512]{1,0:T(8,128)(2,1)S(1)}, bf16[512,512]{1,0:T(8,128)(2,1)S(1)}, bf16[1024,512]{1,0:T(8,128)(2,1)S(1)}) custom-call(bf16[512,256]{1,0:T(8,128)(2,1)S(1)} %get-tuple-element.75.refs_2_.refs_0_, bf16[528,512]{1,0:T(8,128)(2,1)S(1)} %get-tuple-element.76.refs_1_, ...), custom_call_target="tpu_custom_call" | custom-call | flops 1 | bytes 1 | tf_op jit(solution)/shard_map/attention_backward/pallas_call | solution.py:78
  106.0 4.8 %query_weights.1 = (bf16[4,512,512]{2,1,0:T(8,128)(2,1)S(1)}, bf16[512,512]{1,0:T(8,128)(2,1)S(1)}, bf16[3,512,512]{2,1,0:T(8,128)(2,1)S(1)}) custom-call(s32[2]{0:T(128)S(1)} %copy-done.26, bf16[64,4224]{1,0:T(8,128)(2,1)S(1)} %get-tuple-element.73.refs_4_.refs_0_.refs_1_.refs_5_, bf16[64,4224]{1,0:T(8,128)(2,1)S(1)} %get-tuple-element.74.refs_1_.refs_2_.refs_6_, ...), custom_call_target="tpu_custom_call" | custom-call | flops 1 | bytes 1 | tf_op jit(solution)/shard_map/query_weights/pallas_call | solution.py:78
  112.7 4.7 %collective-permute-done.25.refs_17_.refs_5_ = bf16[128,4096]{1,0:T(8,128)(2,1)S(1)} collective-permute-done((bf16[128,4096]{1,0:T(8,128)(2,1)S(1)}, bf16[128,4096]{1,0:T(8,128)(2,1)S(1)}, u32[]{:S(2)}, u32[]{:S(2)}) %collective-permute-start.25) | collective-permute-done | bytes 1048608 | tf_op jit(solution)/shard_map/out_second_1/ppermute | solution.py:31
  120.1 6.2 %feature_parts.1 = (bf16[512,768]{1,0:T(8,128)(2,1)}, bf16[512,512]{1,0:T(8,128)(2,1)S(1)}, bf16[128,4224]{1,0:T(8,128)(2,1)S(1)}, bf16[128,4224]{1,0:T(8,128)(2...) custom-call(bf16[512,512]{1,0:T(8,128)(2,1)S(1)} %get-tuple-element.83.refs_0_, ...), custom_call_target="tpu_custom_call" | custom-call | flops 30000001024 | bytes 1 | tf_op jit(solution)/shard_map/feature_parts/pallas_call | solution.py:78
  131.1 4.8 %collective-permute-done.26.refs_1_ = bf16[64,4224]{1,0:T(8,128)(2,1)S(1)} collective-permute-done((bf16[64,4224]{1,0:T(8,128)(2,1)S(1)}, bf16[64,4224]{1,0:T(8,128)(2,1)S(1)}, u32[]{:S(2)}, u32[]{:S(2)}) %collective-permute-start.26) | collective-permute-done | bytes 540704 | tf_op jit(solution)/shard_map/grad_second_3/ppermute | solution.py:31
  136.2 2.7 %collective-permute-start.30 = (bf16[128,4224]{1,0:T(8,128)(2,1)S(1)}, bf16[128,4224]{1,0:T(8,128)(2,1)S(1)}, u32[]{:S(2)}, u32[]{:S(2)}) collective-permute-start(bf16[128,4224]{1,0:T(8,128)(2,1)S(1)} %get-tuple-element.102), channel_id=1, source_target_pairs={{0,96},{1,25},{2,98},{3,27},{4,100},{5,29},{6,102},{7,31},{8,104},... | collective-permute-start | bytes 3244040 | tf_op jit(solution)/shard_map/grad_second_1/ppermute | solution.py:31
  139.2 5.7 %key_weights.1 = (bf16[4,512,512]{2,1,0:T(8,128)(2,1)S(1)}, bf16[512,512]{1,0:T(8,128)(2,1)S(1)}, bf16[3,512,512]{2,1,0:T(8,128)(2,1)}) custom-call(s32[2]{0:T(128)S(1)} %copy-done.26, bf16[64,4224]{1,0:T(8,128)(2,1)S(1)} %get-tuple-element.73.refs_4_.refs_0_.refs_1_.refs_5_, bf16[64,4224]{1,0:T(8,128)(2,1)S(1)} %get-tuple-element.74.refs_1_.refs_2_.refs_6_, ...), custom_call_target="tpu_custom_call" | custom-call | flops 1 | bytes 1 | tf_op jit(solution)/shard_map/key_weights/pallas_call | solution.py:78
  150.3 11.5 %collective-permute-done.35.refs_7_.refs_1_ = bf16[512,512]{1,0:T(8,128)(2,1)S(1)} collective-permute-done((bf16[512,512]{1,0:T(8,128)(2,1)S(1)}, bf16[512,512]{1,0:T(8,128)(2,1)S(1)}, u32[]{:S(2)}, u32[]{:S(2)}) %collective-permute-start.35) | collective-permute-done | bytes 524320 | tf_op jit(solution)/shard_map/query_weights_z_1/ppermute | solution.py:37
  164.9 3.8 %collective-permute-start.38 = (bf16[32,8320]{1,0:T(8,128)(2,1)}, bf16[32,8320]{1,0:T(8,128)(2,1)}, u32[]{:S(2)}, u32[]{:S(2)}) collective-permute-start(bf16[32,8320]{1,0:T(8,128)(2,1)} %get-tuple-element.114), channel_id=1, source_target_pairs={{0,16},{1,65},{2,18},{3,67},{4,20},{5,69},{6,22},{7,71},{8,24},{9,... | collective-permute-start | bytes 1597448 | tf_op jit(solution)/shard_map/sum_first_2/ppermute | solution.py:31
  202.4 2.9 %collective-permute-start.48 = (bf16[4,32,1152]{2,1,0:T(8,128)(2,1)S(1)}, bf16[4,32,1152]{2,1,0:T(8,128)(2,1)S(1)}, u32[]{:S(2)}, u32[]{:S(2)}) collective-permute-start(bf16[4,32,1152]{2,1,0:T(8,128)(2,1)S(1)} %get-tuple-element.126), channel_id=1, source_target_pairs={{0,1},{1,0},{2,3},{3,2},{4,5},{5,4},{6,7},{7,6},{8,9},{9,8},{10,11... | collective-permute-start | bytes 884744 | tf_op jit(solution)/shard_map/final_core/ppermute | solution.py:42
  207.8 4.6 %grad_placed.1.refs_8_ = bf16[2048,512]{1,0:T(8,128)(2,1)} custom-call(s32[2]{0:T(128)} %pad_add_fusion.1.refs_0_, bf16[2048,512]{1,0:T(8,128)(2,1)} %bitcast.47, s32[1,256]{1,0:T(1,128)} %reshape.156.refs_2_, bf16[32,2176]{1,0:T(8,128)(2,1)} %copy-done.2, bf16[32,2176]{1,0:T(8,128)(2,1)} %copy-done.5, bf16[32,2176]{1,0:T(8,128)(2,1)} %copy-done.6, ...), custom_call_target="tpu_custom_call" | custom-call | flops 1 | bytes 1 | tf_op jit(solution)/shard_map/grad_placed/pallas_call | solution.py:78
  212.4 4.6 %out_placed.1 = bf16[2048,512]{1,0:T(8,128)(2,1)} custom-call(s32[2]{0:T(128)} %pad_add_fusion.1.refs_0_, bf16[2048,512]{1,0:T(8,128)(2,1)} %bitcast.48, s32[1,256]{1,0:T(1,128)} %reshape.156.refs_2_, bf16[32,2176]{1,0:T(8,128)(2,1)} %copy-done.2, bf16[32,2176]{1,0:T(8,128)(2,1)} %copy-done.5, bf16[32,2176]{1,0:T(8,128)(2,1)} %copy-done.6, ...), custom_call_target="tpu_custom_call" | custom-call | flops 1 | bytes 1 | tf_op jit(solution)/shard_map/out_placed/pallas_call | solution.py:78
  (186 shorter events, 93.2 us)
Async XLA Ops:
  23.8 15.3 %collective-permute-start.5 = (bf16[32,8320]{1,0:T(8,128)(2,1)S(1)}, bf16[32,8320]{1,0:T(8,128)(2,1)S(1)}, u32[]{:S(2)}, u32[]{:S(2)}) collective-permute-start(bf16[32,8320]{1,0:T(8,128)(2,1)S(1)} %get-tuple-element.71.refs_0_), channel_id=1, source_target_pairs={{0,16},{1,65},{2,18},{3,67},{4,20},{5,69},{6,22},{7,71},{8,24},{9,... | collective-permute-start | bytes 1597448 | tf_op jit(solution)/shard_map/rows_first_2/ppermute | solution.py:31
  26.5 12.7 %collective-permute-start.4 = (bf16[32,8320]{1,0:T(8,128)(2,1)S(1)}, bf16[32,8320]{1,0:T(8,128)(2,1)S(1)}, u32[]{:S(2)}, u32[]{:S(2)}) collective-permute-start(bf16[32,8320]{1,0:T(8,128)(2,1)S(1)} %get-tuple-element.71.refs_0_), channel_id=1, source_target_pairs={{0,24},{1,97},{2,26},{3,99},{4,28},{5,101},{6,30},{7,103},{8,0},{9... | collective-permute-start | bytes 1597448 | tf_op jit(solution)/shard_map/rows_first_1/ppermute | solution.py:31
  41.9 12.5 %collective-permute-start.8 = (bf16[64,4224]{1,0:T(8,128)(2,1)S(1)}, bf16[64,4224]{1,0:T(8,128)(2,1)S(1)}, u32[]{:S(2)}, u32[]{:S(2)}) collective-permute-start(bf16[64,4224]{1,0:T(8,128)(2,1)S(1)} %get-tuple-element.74.refs_1_.refs_2_.refs_6_), channel_id=1, source_target_pairs={{0,96},{1,25},{2,98},{3,27},{4,100},{5,29},{6,102},{7,31},{8,104},... | collective-permute-start | bytes 1622024 | tf_op jit(solution)/shard_map/x_2_second_1/ppermute | solution.py:31
  42.9 11.8 %collective-permute-start.12 = (bf16[64,4224]{1,0:T(8,128)(2,1)S(1)}, bf16[64,4224]{1,0:T(8,128)(2,1)S(1)}, u32[]{:S(2)}, u32[]{:S(2)}) collective-permute-start(bf16[64,4224]{1,0:T(8,128)(2,1)S(1)} %get-tuple-element.73.refs_4_.refs_0_.refs_1_.refs_5_), channel_id=1, source_target_pairs={{0,32},{1,9},{2,34},{3,11},{4,36},{5,13},{6,38},{7,15},{8,40},{9,1... | collective-permute-start | bytes 1622024 | tf_op jit(solution)/shard_map/x_2_second_3/ppermute | solution.py:31
  54.8 25.8 %collective-permute-start.17 = (bf16[128,4096]{1,0:T(8,128)(2,1)S(1)}, bf16[128,4096]{1,0:T(8,128)(2,1)S(1)}, u32[]{:S(2)}, u32[]{:S(2)}) collective-permute-start(bf16[128,4096]{1,0:T(8,128)(2,1)S(1)} %stack_g.1.refs_11_.refs_0_.refs_9_), channel_id=1, source_target_pairs={{0,32},{1,9},{2,34},{3,11},{4,36},{5,13},{6,38},{7,15},{8,40},{9,1... | collective-permute-start | bytes 3145736 | tf_op jit(solution)/shard_map/g_second_3/ppermute | solution.py:31
  55.8 24.8 %collective-permute-start.16 = (bf16[128,4096]{1,0:T(8,128)(2,1)S(1)}, bf16[128,4096]{1,0:T(8,128)(2,1)S(1)}, u32[]{:S(2)}, u32[]{:S(2)}) collective-permute-start(bf16[128,4096]{1,0:T(8,128)(2,1)S(1)} %stack_g.1.refs_11_.refs_0_.refs_9_), channel_id=1, source_target_pairs={{0,96},{1,25},{2,98},{3,27},{4,100},{5,29},{6,102},{7,31},{8,104},... | collective-permute-start | bytes 3145736 | tf_op jit(solution)/shard_map/g_second_1/ppermute | solution.py:31
  66.8 16.9 %collective-permute-start.13 = (bf16[528,512]{1,0:T(8,128)(2,1)S(1)}, bf16[528,512]{1,0:T(8,128)(2,1)S(1)}, u32[]{:S(2)}, u32[]{:S(2)}) collective-permute-start(bf16[528,512]{1,0:T(8,128)(2,1)S(1)} %get-tuple-element.76.refs_1_), channel_id=1, source_target_pairs={{0,1},{1,0},{2,3},{3,2},{4,5},{5,4},{6,7},{7,6},{8,9},{9,8},{10,11... | collective-permute-start | bytes 1622024 | tf_op jit(solution)/shard_map/pair_core/ppermute | solution.py:42
  80.7 13.3 %collective-permute-start.19 = (bf16[64,4096]{1,0:T(8,128)(2,1)S(1)}, bf16[64,4096]{1,0:T(8,128)(2,1)S(1)}, u32[]{:S(2)}, u32[]{:S(2)}) collective-permute-start(bf16[64,4096]{1,0:T(8,128)(2,1)S(1)} %get-tuple-element.80), channel_id=1, source_target_pairs={{0,32},{1,9},{2,34},{3,11},{4,36},{5,13},{6,38},{7,15},{8,40},{9,1... | collective-permute-start | bytes 1572872 | tf_op jit(solution)/shard_map/g_far_second_3/ppermute | solution.py:31
  81.7 12.3 %collective-permute-start.18 = (bf16[64,4096]{1,0:T(8,128)(2,1)S(1)}, bf16[64,4096]{1,0:T(8,128)(2,1)S(1)}, u32[]{:S(2)}, u32[]{:S(2)}) collective-permute-start(bf16[64,4096]{1,0:T(8,128)(2,1)S(1)} %get-tuple-element.78.refs_6_), channel_id=1, source_target_pairs={{0,96},{1,25},{2,98},{3,27},{4,100},{5,29},{6,102},{7,31},{8,104},... | collective-permute-start | bytes 1572872 | tf_op jit(solution)/shard_map/g_far_second_1/ppermute | solution.py:31
  103.4 14.0 %collective-permute-start.25 = (bf16[128,4096]{1,0:T(8,128)(2,1)S(1)}, bf16[128,4096]{1,0:T(8,128)(2,1)S(1)}, u32[]{:S(2)}, u32[]{:S(2)}) collective-permute-start(bf16[128,4096]{1,0:T(8,128)(2,1)S(1)} %get-tuple-element.92), channel_id=1, source_target_pairs={{0,96},{1,25},{2,98},{3,27},{4,100},{5,29},{6,102},{7,31},{8,104},... | collective-permute-start | bytes 3145736 | tf_op jit(solution)/shard_map/out_second_1/ppermute | solution.py:31
  104.9 15.2 %collective-permute-start.24 = (bf16[128,4096]{1,0:T(8,128)(2,1)S(1)}, bf16[128,4096]{1,0:T(8,128)(2,1)S(1)}, u32[]{:S(2)}, u32[]{:S(2)}) collective-permute-start(bf16[128,4096]{1,0:T(8,128)(2,1)S(1)} %get-tuple-element.90.refs_2_), channel_id=1, source_target_pairs={{0,32},{1,9},{2,34},{3,11},{4,36},{5,13},{6,38},{7,15},{8,40},{9,1... | collective-permute-start | bytes 3145736 | tf_op jit(solution)/shard_map/out_second_3/ppermute | solution.py:31
  105.0 15.1 %collective-permute-start.23 = (bf16[512,512]{1,0:T(8,128)(2,1)S(1)}, bf16[512,512]{1,0:T(8,128)(2,1)S(1)}, u32[]{:S(2)}, u32[]{:S(2)}) collective-permute-start(bf16[512,512]{1,0:T(8,128)(2,1)S(1)} %chip_sum.1.refs_16_), channel_id=1, source_target_pairs={{0,2},{1,3},{2,0},{3,1},{4,6},{5,7},{6,4},{7,5},{8,10},{9,11},{10,... | collective-permute-start | bytes 1572872 | tf_op jit(solution)/shard_map/key_grads_chip/ppermute | solution.py:47
  110.8 18.2 %collective-permute-start.28 = (bf16[512,512]{1,0:T(8,128)(2,1)S(1)}, bf16[512,512]{1,0:T(8,128)(2,1)S(1)}, u32[]{:S(2)}, u32[]{:S(2)}) collective-permute-start(bf16[512,512]{1,0:T(8,128)(2,1)S(1)} %get-tuple-element.91.refs_15_), channel_id=1, source_target_pairs={{0,1},{1,0},{2,3},{3,2},{4,5},{5,4},{6,7},{7,6},{8,9},{9,8},{10,11... | collective-permute-start | bytes 1572872 | tf_op jit(solution)/shard_map/query_weights_far_core/ppermute | solution.py:42
  112.6 26.3 %collective-permute-start.31 = (bf16[3,512,512]{2,1,0:T(8,128)(2,1)S(1)}, bf16[3,512,512]{2,1,0:T(8,128)(2,1)S(1)}, u32[]{:S(2)}, u32[]{:S(2)}) collective-permute-start(bf16[3,512,512]{2,1,0:T(8,128)(2,1)S(1)} %get-tuple-element.104), channel_id=1, source_target_pairs={{0,1},{1,0},{2,3},{3,2},{4,5},{5,4},{6,7},{7,6},{8,9},{9,8},{10,11... | collective-permute-start | bytes 4718600 | tf_op jit(solution)/shard_map/query_weights_core/ppermute | solution.py:42
  136.2 27.0 %collective-permute-start.30 = (bf16[128,4224]{1,0:T(8,128)(2,1)S(1)}, bf16[128,4224]{1,0:T(8,128)(2,1)S(1)}, u32[]{:S(2)}, u32[]{:S(2)}) collective-permute-start(bf16[128,4224]{1,0:T(8,128)(2,1)S(1)} %get-tuple-element.102), channel_id=1, source_target_pairs={{0,96},{1,25},{2,98},{3,27},{4,100},{5,29},{6,102},{7,31},{8,104},... | collective-permute-start | bytes 3244040 | tf_op jit(solution)/shard_map/grad_second_1/ppermute | solution.py:31
  138.9 24.3 %collective-permute-start.29 = (bf16[128,4224]{1,0:T(8,128)(2,1)S(1)}, bf16[128,4224]{1,0:T(8,128)(2,1)S(1)}, u32[]{:S(2)}, u32[]{:S(2)}) collective-permute-start(bf16[128,4224]{1,0:T(8,128)(2,1)S(1)} %get-tuple-element.101.refs_4_), channel_id=1, source_target_pairs={{0,32},{1,9},{2,34},{3,11},{4,36},{5,13},{6,38},{7,15},{8,40},{9,1... | collective-permute-start | bytes 3244040 | tf_op jit(solution)/shard_map/grad_second_3/ppermute | solution.py:31
  147.0 14.8 %collective-permute-start.35 = (bf16[512,512]{1,0:T(8,128)(2,1)S(1)}, bf16[512,512]{1,0:T(8,128)(2,1)S(1)}, u32[]{:S(2)}, u32[]{:S(2)}) collective-permute-start(bf16[512,512]{1,0:T(8,128)(2,1)S(1)} %get-tuple-element.110), channel_id=1, source_target_pairs={{0,2},{1,3},{2,4},{3,5},{4,6},{5,7},{6,0},{7,1},{8,10},{9,11},{10,... | collective-permute-start | bytes 1572872 | tf_op jit(solution)/shard_map/query_weights_z_1/ppermute | solution.py:37
  147.6 14.5 %collective-permute-start.36 = (bf16[512,512]{1,0:T(8,128)(2,1)S(1)}, bf16[512,512]{1,0:T(8,128)(2,1)S(1)}, u32[]{:S(2)}, u32[]{:S(2)}) collective-permute-start(bf16[512,512]{1,0:T(8,128)(2,1)S(1)} %get-tuple-element.111), channel_id=1, source_target_pairs={{0,6},{1,7},{2,0},{3,1},{4,2},{5,3},{6,4},{7,5},{8,14},{9,15},{10,... | collective-permute-start | bytes 1572872 | tf_op jit(solution)/shard_map/query_weights_z_3/ppermute | solution.py:37
  149.7 23.2 %collective-permute-start.40 = (bf16[3,512,512]{2,1,0:T(8,128)(2,1)}, bf16[3,512,512]{2,1,0:T(8,128)(2,1)}, u32[]{:S(2)}, u32[]{:S(2)}) collective-permute-start(bf16[3,512,512]{2,1,0:T(8,128)(2,1)} %get-tuple-element.116), channel_id=1, source_target_pairs={{0,1},{1,0},{2,3},{3,2},{4,5},{5,4},{6,7},{7,6},{8,9},{9,8},{10,11... | collective-permute-start | bytes 4718600 | tf_op jit(solution)/shard_map/key_weights_core/ppermute | solution.py:42
  164.9 24.7 %collective-permute-start.37 = (bf16[32,8320]{1,0:T(8,128)(2,1)}, bf16[32,8320]{1,0:T(8,128)(2,1)}, u32[]{:S(2)}, u32[]{:S(2)}) collective-permute-start(bf16[32,8320]{1,0:T(8,128)(2,1)} %get-tuple-element.113), channel_id=1, source_target_pairs={{0,8},{1,33},{2,10},{3,35},{4,12},{5,37},{6,14},{7,39},{8,16},{9,4... | collective-permute-start | bytes 1597448 | tf_op jit(solution)/shard_map/sum_first_3/ppermute | solution.py:31
  164.9 24.7 %collective-permute-start.38 = (bf16[32,8320]{1,0:T(8,128)(2,1)}, bf16[32,8320]{1,0:T(8,128)(2,1)}, u32[]{:S(2)}, u32[]{:S(2)}) collective-permute-start(bf16[32,8320]{1,0:T(8,128)(2,1)} %get-tuple-element.114), channel_id=1, source_target_pairs={{0,16},{1,65},{2,18},{3,67},{4,20},{5,69},{6,22},{7,71},{8,24},{9,... | collective-permute-start | bytes 1597448 | tf_op jit(solution)/shard_map/sum_first_2/ppermute | solution.py:31
  169.5 20.2 %collective-permute-start.39 = (bf16[32,8320]{1,0:T(8,128)(2,1)}, bf16[32,8320]{1,0:T(8,128)(2,1)}, u32[]{:S(2)}, u32[]{:S(2)}) collective-permute-start(bf16[32,8320]{1,0:T(8,128)(2,1)} %get-tuple-element.115), channel_id=1, source_target_pairs={{0,24},{1,97},{2,26},{3,99},{4,28},{5,101},{6,30},{7,103},{8,0},{9... | collective-permute-start | bytes 1597448 | tf_op jit(solution)/shard_map/sum_first_1/ppermute | solution.py:31
  177.3 17.3 %collective-permute-start.46 = (bf16[512,512]{1,0:T(8,128)(2,1)}, bf16[512,512]{1,0:T(8,128)(2,1)S(1)}, u32[]{:S(2)}, u32[]{:S(2)}) collective-permute-start(bf16[512,512]{1,0:T(8,128)(2,1)} %get-tuple-element.123), channel_id=1, source_target_pairs={{0,2},{1,3},{2,4},{3,5},{4,6},{5,7},{6,0},{7,1},{8,10},{9,11},{10,... | collective-permute-start | bytes 1572872 | tf_op jit(solution)/shard_map/key_weights_z_1/ppermute | solution.py:37
  177.3 18.1 %collective-permute-start.47 = (bf16[512,512]{1,0:T(8,128)(2,1)}, bf16[512,512]{1,0:T(8,128)(2,1)}, u32[]{:S(2)}, u32[]{:S(2)}) collective-permute-start(bf16[512,512]{1,0:T(8,128)(2,1)} %get-tuple-element.124), channel_id=1, source_target_pairs={{0,6},{1,7},{2,0},{3,1},{4,2},{5,3},{6,4},{7,5},{8,14},{9,15},{10,... | collective-permute-start | bytes 1572872 | tf_op jit(solution)/shard_map/key_weights_z_3/ppermute | solution.py:37
  (56 other events, 414.6 us)

commit v3 on v2

--- a/solution.py
+++ b/solution.py
@@ -64,7 +64,7 @@
 
 
 ORDER = []
-COSTS = {"out_add": 20, "feature_parts": 30, "sum_column": 30, "query_weights_near": 20, "stack_g": 20, "halves_g": 5}
+COSTS = {"out_add": 20, "feature_parts": 30, "sum_column": 30, "query_weights_near": 20, "stack_g": 20, "halves_g": 5, "final_rows": 20}
 
 
 def call(kernel, name, out_shape, room=8, after=(), cost=0, **options):
@@ -136,7 +136,7 @@
         pick_kernel,
         "pick_rows",
         [shape(2, 2, 32, 512)] * 4,
-        room=56,
+        room=12,
         grid=(2,),
         in_specs=[SMEM, pl.BlockSpec((1, 1, 128), lambda s: (s, 0, 0)), block, block],
         out_specs=[pl.BlockSpec((2, 2, 32, 512), lambda s: (0, 0, 0, 0))] * 4,
@@ -240,15 +240,19 @@
 
 
 def add_kernel(a, ta, b, tb, out_a, out_b):
-    out_a[:64] = a[:64] + ta[...]
-    out_a[64:] = a[64:]
-    out_b[:64] = b[:64]
-    out_b[64:] = b[64:] + tb[...]
+    half = ta.shape[0]
+    out_a[:half] = a[:half] + ta[...]
+    out_a[half:] = a[half:]
+    out_b[:half] = b[:half]
+    out_b[half:] = b[half:] + tb[...]
 
 
 def sum_column_kernel(og, ug, vg, oo, uo, vo, *outs):
-    for i, out in enumerate(outs):
-        rows = slice(i * 32, i * 32 + 32)
+    row = 0
+    for out in outs:
+        count = out.shape[0]
+        rows = slice(row, row + count)
+        row += count
         for own, u, v, at in ((oo, uo, vo, slice(0, 4096)), (og, ug, vg, slice(4096, 4096 + WIDE))):
             total = own[rows].astype(F32) + u[rows].astype(F32) + v[rows].astype(F32)
             out[:, at] = total.astype(BF)
@@ -271,16 +275,27 @@
     return own, ring(plus, True, 3, name), ring(minus, True, 1, name)
 
 
-def reduce_column(grad_terms, out_terms, after):
-    parts = call(
+def reduce_column(grad_terms, out_terms):
+    own, plus, far_low, far_high, minus = call(
         sum_column_kernel,
         "sum_column",
-        [shape(32, 4096 + WIDE)] * 4,
-        after=after,
+        [shape(n, 4096 + WIDE) for n in (32, 32, 16, 16, 32)],
         in_specs=[WHOLE] * 6,
-        out_specs=[WHOLE] * 4,
+        out_specs=[WHOLE] * 5,
     )(*grad_terms, *out_terms)
-    return [parts[0]] + [ring(parts[i], False, 4 - i, "sum") for i in (1, 2, 3)]
+    return own, plus, ring(far_low, False, 3, "sum_far"), minus, ring(far_high, False, 1, "sum_far")
+
+
+def reduce_rows(state):
+    own, plus, to_plus, minus, to_minus = state
+    plus, minus = call(
+        add_kernel,
+        "sum_add",
+        [shape(*plus.shape)] * 2,
+        in_specs=[WHOLE] * 4,
+        out_specs=[WHOLE] * 2,
+    )(plus, to_plus, minus, to_minus)
+    return own, ring(plus, False, 3, "sum"), ring(minus, False, 1, "sum")
 
 
 X_PIECES = (64,) * 8
@@ -591,25 +606,58 @@
 
 
 def key_weight_kernel(where, *refs):
-    x, (left, kept, far, rest) = refs[:8], refs[8:]
+    x, (left, kept, sent) = refs[:8], refs[8:]
 
     @pl.loop(0, 8)
     def _(i):
         columns = slice_columns(where, i)
         a = jnp.dot(left[...], joined(x, columns), preferred_element_type=F32).astype(BF)
 
-        put_slice(i, a, kept, far, rest)
+        @pl.when(i < 4)
+        def _():
+            sent[lax.rem(i, 4)] = a
+
+        @pl.when(i >= 4)
+        def _():
+            kept[lax.rem(i, 4)] = a
 
 
 def key_weights(where, x, left):
     return call(
         key_weight_kernel,
         "key_weights",
-        [shape(4, 512, 512), shape(512, 512), shape(3, 512, 512)],
+        [shape(4, 512, 512)] * 2,
         room=16,
         in_specs=[SMEM] + [WHOLE] * 9,
+        out_specs=[WHOLE] * 2,
+    )(where, *x, left)
+
+
+def sum_all_kernel(kept, recv, low, high, rest):
+    low[...] = kept[0, :256] + recv[0, :256]
+    high[...] = kept[0, 256:] + recv[0, 256:]
+    for i in range(3):
+        rest[i] = kept[i + 1] + recv[i + 1]
+
+
+def sum_all(kept, recv, name, after):
+    low, high, rest = call(
+        sum_all_kernel,
+        name + "_all",
+        [shape(256, 512), shape(256, 512), shape(3, 512, 512)],
+        after=after,
+        in_specs=[WHOLE] * 2,
         out_specs=[WHOLE] * 3,
-    )(where, *x, left)
+    )(kept, recv)
+    return rest, send_z(low, 1, name + "_far"), send_z(high, 3, name + "_far")
+
+
+def sum_near_all_kernel(rest, to_plus, to_minus, own, plus, minus):
+    own[...] = rest[0]
+    plus[:256] = rest[1, :256] + to_plus[...]
+    plus[256:] = rest[1, 256:]
+    minus[:256] = rest[2, :256]
+    minus[256:] = rest[2, 256:] + to_minus[...]
 
 
 def sum_far_kernel(kept, recv, low, high):
@@ -622,12 +670,13 @@
     return kept, swap_core(far, name + "_far"), swap_core(rest, name)
 
 
-def sum_far(parts, name):
+def sum_far(parts, name, after):
     kept, far, rest = parts
     low, high = call(
         sum_far_kernel,
         name + "_far",
         [shape(256, 512)] * 2,
+        after=after,
         in_specs=[WHOLE] * 2,
         out_specs=[WHOLE] * 2,
     )(kept, far)
@@ -644,10 +693,10 @@
 
 def sum_near(state, name):
     own, plus, minus = call(
-        sum_near_kernel,
+        sum_near_kernel if len(state) == 4 else sum_near_all_kernel,
         name + "_near",
         [shape(512, 512)] * 3,
-        in_specs=[WHOLE] * 4,
+        in_specs=[WHOLE] * len(state),
         out_specs=[WHOLE] * 3,
     )(*state)
     return own, send_z(plus, 1, name), send_z(minus, 3, name)
@@ -672,14 +721,13 @@
     )(*a, *b)
 
 
-def final_rows_kernel(where, own, u, t, v, rows, gain, o0, o1, o2, o3, total):
+def final_rows_kernel(where, own, u, v, rows, gain, o0, o1, o2, o3, total):
     x = rows[...].astype(F32)
     inverse = lax.rsqrt(jnp.mean(x * x, -1, keepdims=True) + EPS)
     unit = x * inverse
 
     def summed(at):
-        first = own[:, at].astype(F32) + u[:, at].astype(F32)
-        return first + (t[:, at].astype(F32) + v[:, at].astype(F32))
+        return own[:, at].astype(F32) + u[:, at].astype(F32) + v[:, at].astype(F32)
 
     total[:, :4096] = summed(slice(0, 4096)).astype(BF)
     scaled = summed(slice(4096, 8192)) * gain[...]
@@ -730,36 +778,36 @@
     return swap_core(sent, "final"), gain
 
 
-def place_rows(where, base, places, pieces, other, half, name):
-    def kernel(where, base, places, p0, p1, p2, p3, other, out, rows):
-        step = pl.program_id(0)
-
-        @pl.when(step == 0)
-        def _():
+def place_kernel(where, hidden, grads, places, p0, p1, p2, p3, other, out_h, out_g, rows):
+    step = pl.program_id(0)
+
+    @pl.when(step == 0)
+    def _():
+        for half in range(2):
+            columns = slice(half * 512, half * 512 + 512)
             start = pl.multiple_of(half * 1024 + where[1] * 512, 512)
             for d, piece in enumerate((p0, p1, p2, p3)):
-                rows[d * 32 : d * 32 + 32] = piece[:, pl.ds(start, 512)]
-                rows[128 + d * 32 : 160 + d * 32] = other[d, :, half * 512 : half * 512 + 512]
-
-        token = step * 512 + lax.broadcasted_iota(jnp.int32, (512, 256), 0)
-        hot = (token == places[...]).astype(F32).astype(BF)
-        added = jnp.dot(hot, rows[...], preferred_element_type=F32)
-        out[...] = (base[...].astype(F32) + added).astype(BF)
-
-    block = pl.BlockSpec((512, 512), lambda i: (i, 0))
-    fixed = lambda i: (0, 0)
-    return call(
-        kernel,
-        name + "_placed",
-        shape(2048, 512),
-        room=56,
-        grid=(4,),
-        in_specs=[SMEM, block, pl.BlockSpec((1, 256), fixed)]
-        + [pl.BlockSpec(pieces[0].shape, fixed)] * 4
-        + [pl.BlockSpec(other.shape, lambda i: (0, 0, 0))],
-        out_specs=block,
-        scratch_shapes=[pltpu.VMEM((256, 512), BF)],
-    )(where, base, places, *pieces, other)
+                rows[d * 32 : d * 32 + 32, columns] = piece[:, pl.ds(start, 512)]
+                rows[128 + d * 32 : 160 + d * 32, columns] = other[d, :, columns]
+
+    token = step * 256 + lax.broadcasted_iota(jnp.int32, (256, 256), 0)
+    hot = (token == places[...]).astype(F32).astype(BF)
+    added = jnp.dot(hot, rows[...], preferred_element_type=F32)
+    out_h[...] = (hidden[...].astype(F32) + added[:, :512]).astype(BF)
+    out_g[...] = (grads[...].astype(F32) + added[:, 512:]).astype(BF)
+
+
+def place_rows(where, hidden, grads, places, pieces, other):
+    block = pl.BlockSpec((256, 512), lambda i: (i, 0))
+    return call(
+        place_kernel,
+        "place_rows",
+        [pltpu.HBM((2048, 512), BF)] * 2,
+        grid=(8,),
+        in_specs=[SMEM, block, block] + [WHOLE] * 6,
+        out_specs=[block] * 2,
+        scratch_shapes=[pltpu.VMEM((256, 1024), BF)],
+    )(where, hidden, grads, places, *pieces, other)
 
 
 def shards(hidden_in, route_index, norm_gain, w_qkv, w_out, cotangent):
@@ -778,7 +826,8 @@
     code = (lane == own_index // 32) | (lane == own_index % 32 + 32) | (lane == context + 64)
     code = code.astype(F32).astype(BF)
 
-    picked = pick_rows(where, route_index, hidden_in, cotangent)
+    from_hbm = lambda v: pltpu.with_memory_space_constraint(v, pltpu.HBM)
+    picked = pick_rows(where, route_index, from_hbm(hidden_in), from_hbm(cotangent))
     picked = [picked[0]] + [send_z(picked[d], d) for d in (1, 2, 3)]
     both_own, rows_own = own_rows(where, picked, gain, code)
     column = gather_first(both_own)
@@ -802,16 +851,16 @@
     chip_part = swap_chip(chip_sum(mid, recv), "key_grads")
     swapped_a = swap_weights(query_weights(where, x, g, grad_q, attended), "query_weights")
 
-    gp_kv, parts = feature_parts(
-        near, recv, chip_part, grad_q, table, x, w_in, gain, out_terms[1:]
-    )
+    gp_kv, parts = feature_parts(near, recv, chip_part, grad_q, table, x, w_in, gain, ())
     grad_state = reduce_start(parts, "grad")
-    state_a = sum_far(swapped_a, "query_weights")
+    state_a = sum_far(swapped_a, "query_weights", out_terms[1:])
     grad_terms = reduce_add(grad_state, "grad")
     terms_a = sum_near(state_a, "query_weights")
-    swapped_b = swap_weights(key_weights(where, x, gp_kv), "key_weights")
-    state_b = sum_far(swapped_b, "key_weights")
-    column = reduce_column(grad_terms, out_terms, terms_a[1:])
+    kept_b, sent_b = key_weights(where, x, gp_kv)
+    recv_b = swap_core(sent_b, "key_weights")
+    column = reduce_column(grad_terms, out_terms)
+    state_b = sum_all(kept_b, recv_b, "key_weights", terms_a[1:])
+    column = reduce_rows(column)
     terms_b = sum_near(state_b, "key_weights")
     final = final_rows(where, *column, rows_own, gain)
     grad_w_qkv, grad_w_out = sum_weights(terms_a, terms_b)
@@ -821,10 +870,9 @@
     by_chip = (local_index + jnp.arange(2, dtype=jnp.int32)[:, None] * 1024).reshape(4, 2, 32)
     by_core = jnp.stack([dyn(by_chip, core, 1), dyn(by_chip, 1 - core, 1)])
     places = jnp.stack([dyn(by_core, chips[d], 1) for d in range(4)], 1).reshape(1, 256)
-    hidden = hidden_in.reshape(2048, 512)
-    grad_base = cotangent.reshape(2048, 512)
-    grad_in = place_rows(where, grad_base, places, final, other, 1, "grad")
-    hidden_out = place_rows(where, hidden, places, final, other, 0, "out")
+    hidden_out, grad_in = place_rows(
+        where, hidden_in.reshape(2048, 512), cotangent.reshape(2048, 512), places, final, other
+    )
     grad_gain = gain_part + other[0, :, 1024:].astype(F32) + other[1, :, 1024:].astype(F32)
     return (
         hidden_out.reshape(2, 1024, 512),

time: 218 us -> 211 us (0.968)
  Pallas kernels: 64 us -> 56.3 us
  starting transfers between devices: 68.6 us -> 72.7 us
  local copies, waits for them, and re-layouts: 16.3 us -> 13.8 us
    pallas_call x28, Pallas kernels: 64 us -> 56.3 us  [invoke(): pl.pallas_call(body, out_shape=out_shape, compiler_params=pltpu.CompilerP...]
    ppermute x14, waiting for transfers between devices: 16.6 us -> 9.6 us  [send_z(): return lax.ppermute(values, 'cmp', pairs)]
    ppermute x9 -> x8, starting transfers between devices: 15.6 us -> 20.1 us  [swap_core(): return lax.ppermute(values, 'cmp', [(k, k ^ 1) for k in range(8)])]
    unnamed x63 -> x45, local copies, waits for them, and re-layouts: 13.6 us -> 9.98 us
    ppermute x2, waiting for transfers between devices: 8.2 us -> 11.5 us  [swap_chip(): return lax.ppermute(values, 'cmp', [(k, k ^ 2) for k in range(8)])]
    ppermute x24 -> x25, waiting for transfers between devices: 31.5 us -> 34.3 us  [ring(): return lax.ppermute(values, BOTH, ring_pairs(second, shift))]
    ppermute x24 -> x25, starting transfers between devices: 32.8 us -> 30.8 us  [ring(): return lax.ppermute(values, BOTH, ring_pairs(second, shift))]
  transfers between devices with their start and end apart: 49 -> 49, of which waited for: 14 -> 21; matrix products, arithmetic and copies ran while one was open for 2% -> 2% of each run, Pallas kernels for 23% -> 22%
where the time goes in v3:
time: 211 us
  starting transfers between devices  72.7 us (34%)
  waiting for transfers between devices  57.4 us (27%)
  Pallas kernels  56.3 us (27%)
  local copies, waits for them, and re-layouts  13.8 us (7%)
  between operations  8.77 us (4%)
    pallas_call x28, Pallas kernels, invoke(): pl.pallas_call(body, out_shape=out_shape, compiler_params=pltpu.CompilerP...  56.3 us
    ppermute x25, waiting for transfers between devices, ring(): return lax.ppermute(values, BOTH, ring_pairs(second, shift))  34.3 us
    ppermute x25, starting transfers between devices, ring(): return lax.ppermute(values, BOTH, ring_pairs(second, shift))  30.8 us
    ppermute x8, starting transfers between devices, swap_core(): return lax.ppermute(values, 'cmp', [(k, k ^ 1) for k in range(8)])  20.1 us
    ppermute x14, starting transfers between devices, send_z(): return lax.ppermute(values, 'cmp', pairs)  19.6 us
    ppermute x2, waiting for transfers between devices, swap_chip(): return lax.ppermute(values, 'cmp', [(k, k ^ 2) for k in range(8)])  11.5 us
    unnamed x45, local copies, waits for them, and re-layouts  9.98 us
    ppermute x14, waiting for transfers between devices, send_z(): return lax.ppermute(values, 'cmp', pairs)  9.6 us
  transfers between devices with their start and end apart: 49, of which 21 were waited for; matrix products, arithmetic and copies ran while one was open for 2% of the time, Pallas kernels for 22%

profile of v3, /device:TPU:1, one launch (start us, length us, event | category | flops | bytes accessed | tf_op | source)
XLA Modules:
  0.0 210.5 jit_solution(15582238790856711317)
XLA Ops:
  1.4 2.7 %pick_rows.1 = (bf16[2,2,32,512]{3,2,1,0:T(8,128)(2,1)S(1)}, bf16[2,2,32,512]{3,2,1,0:T(8,128)(2,1)S(1)}, bf16[2,2,32,512]{3,2,1,0:T(8,128)(2,1)S(1)}, bf16[2,2,32,512]{3,2,1,0:T(8,128)(2,1)S(1)}) custom-call(s32[2]{0:T(128)S(1)} %pad_add_fusion.1.refs_0_, s32[2,1,128]{2,1,0:T(1,128)S(1)} %copy-done.16, bf16[2,1024,512]{2,1,0:T(8,128)(2,1)} %refs_2_.1, ...), custom_call_target="tpu_custom_call" | custom-call | flops 1 | bytes 1 | tf_op jit(solution)/shard_map/pick_rows/pallas_call | solution.py:78
  6.7 3.3 %collective-permute-start.1 = (bf16[2,2,32,512]{3,2,1,0:T(8,128)(2,1)S(1)}, bf16[2,2,32,512]{3,2,1,0:T(8,128)(2,1)S(1)}, u32[]{:S(2)}, u32[]{:S(2)}) collective-permute-start(bf16[2,2,32,512]{3,2,1,0:T(8,128)(2,1)S(1)} %get-tuple-element.74), channel_id=1, source_target_pairs={{0,4},{1,5},{2,6},{3,7},{4,0},{5,1},{6,2},{7,3},{8,12},{9,13},{10,... | collective-permute-start | bytes 393224 | tf_op jit(solution)/shard_map/rows_z_2/ppermute | solution.py:37
  12.0 3.7 %collective-permute-done.1.refs_3_ = bf16[2,2,32,512]{3,2,1,0:T(8,128)(2,1)S(1)} collective-permute-done((bf16[2,2,32,512]{3,2,1,0:T(8,128)(2,1)S(1)}, bf16[2,2,32,512]{3,2,1,0:T(8,128)(2,1)S(1)}, u32[]{:S(2)}, u32[]{:S(2)}) %collective-permute-start.1) | collective-permute-done | bytes 131104 | tf_op jit(solution)/shard_map/rows_z_2/ppermute | solution.py:37
  24.9 2.8 %copy-done.3 = bf16[4096,2,3,128]{3,1,2,0:T(2,128)(2,1)S(1)} copy-done((bf16[4096,2,3,128]{3,1,2,0:T(2,128)(2,1)S(1)}, bf16[4096,2,3,128]{3,1,2,0:T(2,128)(2,1)}, u32[]{:S(2)}) %copy-start.3) | copy-done | bytes 6291480
  30.0 6.5 %collective-permute-done.5.refs_2_ = bf16[32,8320]{1,0:T(8,128)(2,1)S(1)} collective-permute-done((bf16[32,8320]{1,0:T(8,128)(2,1)S(1)}, bf16[32,8320]{1,0:T(8,128)(2,1)S(1)}, u32[]{:S(2)}, u32[]{:S(2)}) %collective-permute-start.5) | collective-permute-done | bytes 532512 | tf_op jit(solution)/shard_map/rows_first_2/ppermute | solution.py:31
  40.8 5.6 %collective-permute-done.10.refs_7_.refs_8_.refs_12_ = bf16[64,4224]{1,0:T(8,128)(2,1)S(1)} collective-permute-done((bf16[64,4224]{1,0:T(8,128)(2,1)S(1)}, bf16[64,4224]{1,0:T(8,128)(2,1)S(1)}, u32[]{:S(2)}, u32[]{:S(2)}) %collective-permute-start.10) | collective-permute-done | bytes 540704 | tf_op jit(solution)/shard_map/x_1_second_3/ppermute | solution.py:31
  49.0 2.8 %collective-permute-done.8.refs_5_.refs_3_.refs_4_.refs_8_ = bf16[64,4224]{1,0:T(8,128)(2,1)S(1)} collective-permute-done((bf16[64,4224]{1,0:T(8,128)(2,1)S(1)}, bf16[64,4224]{1,0:T(8,128)(2,1)S(1)}, u32[]{:S(2)}, u32[]{:S(2)}) %collective-permute-start.8) | collective-permute-done | bytes 540704 | tf_op jit(solution)/shard_map/x_2_second_1/ppermute | solution.py:31
  55.0 2.9 %collective-permute-done.11.refs_5_.refs_6_.refs_10_ = bf16[64,4224]{1,0:T(8,128)(2,1)S(1)} collective-permute-done((bf16[64,4224]{1,0:T(8,128)(2,1)S(1)}, bf16[64,4224]{1,0:T(8,128)(2,1)S(1)}, u32[]{:S(2)}, u32[]{:S(2)}) %collective-permute-start.11) | collective-permute-done | bytes 540704 | tf_op jit(solution)/shard_map/x_far_second_3/ppermute | solution.py:31
  57.9 5.3 %project.1 = (bf16[512,256]{1,0:T(8,128)(2,1)S(1)}, bf16[528,512]{1,0:T(8,128)(2,1)S(1)}, f32[512,384]{1,0:T(8,128)S(1)}) custom-call(bf16[64,4224]{1,0:T(8,128)(2,1)S(1)} %get-tuple-element.78.refs_4_.refs_0_.refs_1_.refs_5_, bf16[64,4224]{1,0:T(8,128)(2,1)S(1)} %get-tuple-element.79.refs_1_.refs_2_.refs_6_, ...), custom_call_target="tpu_custom_call" | custom-call | flops 1 | bytes 1 | tf_op jit(solution)/shard_map/project/pallas_call | solution.py:78
  66.7 8.2 %collective-permute-done.14.refs_3_ = bf16[528,512]{1,0:T(8,128)(2,1)S(1)} collective-permute-done((bf16[528,512]{1,0:T(8,128)(2,1)S(1)}, bf16[528,512]{1,0:T(8,128)(2,1)S(1)}, u32[]{:S(2)}, u32[]{:S(2)}) %collective-permute-start.14) | collective-permute-done | bytes 540704 | tf_op jit(solution)/shard_map/pair_chip/ppermute | solution.py:47
  74.9 3.1 %collective-permute-start.15 = (bf16[528,512]{1,0:T(8,128)(2,1)S(1)}, bf16[528,512]{1,0:T(8,128)(2,1)S(1)}, u32[]{:S(2)}, u32[]{:S(2)}) collective-permute-start(bf16[528,512]{1,0:T(8,128)(2,1)S(1)} %collective-permute-done.14.refs_3_), channel_id=1, source_target_pairs={{0,1},{1,0},{2,3},{3,2},{4,5},{5,4},{6,7},{7,6},{8,9},{9,8},{10,11... | collective-permute-start | bytes 1622024 | tf_op jit(solution)/shard_map/far_pair_core/ppermute | solution.py:42
  81.1 6.3 %attention_forward.1 = (bf16[512,256]{1,0:T(8,128)(2,1)S(1)}, bf16[2,512,2048]{2,1,0:T(8,128)(2,1)S(1)}) custom-call(bf16[512,256]{1,0:T(8,128)(2,1)S(1)} %get-tuple-element.80.refs_2_.refs_0_, bf16[528,512]{1,0:T(8,128)(2,1)S(1)} %get-tuple-element.81.refs_1_, bf16[528,512]{1,0:T(8,128)(2,1)S(1)} %collective-permute-done.13.refs_2_, ...), custom_call_target="tpu_custom_call" | custom-call | flops 1 | bytes 1 | tf_op jit(solution)/shard_map/attention_forward/pallas_call | solution.py:78
  93.3 5.2 %attention_backward.1 = (bf16[512,256]{1,0:T(8,128)(2,1)S(1)}, bf16[512,512]{1,0:T(8,128)(2,1)S(1)}, bf16[512,512]{1,0:T(8,128)(2,1)S(1)}, bf16[1024,512]{1,0:T(8,128)(2,1)S(1)}) custom-call(bf16[512,256]{1,0:T(8,128)(2,1)S(1)} %get-tuple-element.80.refs_2_.refs_0_, bf16[528,512]{1,0:T(8,128)(2,1)S(1)} %get-tuple-element.81.refs_1_, ...), custom_call_target="tpu_custom_call" | custom-call | flops 1 | bytes 1 | tf_op jit(solution)/shard_map/attention_backward/pallas_call | solution.py:78
  105.4 4.8 %query_weights.1 = (bf16[4,512,512]{2,1,0:T(8,128)(2,1)S(1)}, bf16[512,512]{1,0:T(8,128)(2,1)S(1)}, bf16[3,512,512]{2,1,0:T(8,128)(2,1)S(1)}) custom-call(s32[2]{0:T(128)S(1)} %pad_add_fusion.1.refs_0_, bf16[64,4224]{1,0:T(8,128)(2,1)S(1)} %get-tuple-element.78.refs_4_.refs_0_.refs_1_.refs_5_, ...), custom_call_target="tpu_custom_call" | custom-call | flops 1 | bytes 1 | tf_op jit(solution)/shard_map/query_weights/pallas_call | solution.py:78
  111.6 3.4 %collective-permute-done.23.refs_2_ = bf16[512,512]{1,0:T(8,128)(2,1)S(1)} collective-permute-done((bf16[512,512]{1,0:T(8,128)(2,1)S(1)}, bf16[512,512]{1,0:T(8,128)(2,1)S(1)}, u32[]{:S(2)}, u32[]{:S(2)}) %collective-permute-start.23) | collective-permute-done | bytes 524320 | tf_op jit(solution)/shard_map/key_grads_chip/ppermute | solution.py:47
  114.9 6.2 %feature_parts.1 = (bf16[512,768]{1,0:T(8,128)(2,1)}, bf16[512,512]{1,0:T(8,128)(2,1)S(1)}, bf16[128,4224]{1,0:T(8,128)(2,1)S(1)}, bf16[128,4224]{1,0:T(8,128)(2...) custom-call(bf16[512,512]{1,0:T(8,128)(2,1)S(1)} %get-tuple-element.88.refs_0_, ...), custom_call_target="tpu_custom_call" | custom-call | flops 30000001024 | bytes 1 | tf_op jit(solution)/shard_map/feature_parts/pallas_call | solution.py:78
  126.1 4.8 %collective-permute-done.24.refs_1_ = bf16[64,4224]{1,0:T(8,128)(2,1)S(1)} collective-permute-done((bf16[64,4224]{1,0:T(8,128)(2,1)S(1)}, bf16[64,4224]{1,0:T(8,128)(2,1)S(1)}, u32[]{:S(2)}, u32[]{:S(2)}) %collective-permute-start.24) | collective-permute-done | bytes 540704 | tf_op jit(solution)/shard_map/grad_second_3/ppermute | solution.py:31
  131.1 2.7 %collective-permute-start.30 = (bf16[128,4224]{1,0:T(8,128)(2,1)S(1)}, bf16[128,4224]{1,0:T(8,128)(2,1)S(1)}, u32[]{:S(2)}, u32[]{:S(2)}) collective-permute-start(bf16[128,4224]{1,0:T(8,128)(2,1)S(1)} %get-tuple-element.107), channel_id=1, source_target_pairs={{0,96},{1,25},{2,98},{3,27},{4,100},{5,29},{6,102},{7,31},{8,104},... | collective-permute-start | bytes 3244040 | tf_op jit(solution)/shard_map/grad_second_1/ppermute | solution.py:31
  136.8 4.5 %key_weights.1 = (bf16[4,512,512]{2,1,0:T(8,128)(2,1)S(1)}, bf16[4,512,512]{2,1,0:T(8,128)(2,1)S(1)}) custom-call(s32[2]{0:T(128)S(1)} %pad_add_fusion.1.refs_0_, bf16[64,4224]{1,0:T(8,128)(2,1)S(1)} %get-tuple-element.78.refs_4_.refs_0_.refs_1_.refs_5_, bf16[64,4224]{1,0:T(8,128)(2,1)S(1)} %get-tuple-element.79.refs_1_.refs_2_.refs_6_, ...), custom_call_target="tpu_custom_call" | custom-call | flops 1 | bytes 1 | tf_op jit(solution)/shard_map/key_weights/pallas_call | solution.py:78
  141.3 3.2 %collective-permute-start.36 = (bf16[4,512,512]{2,1,0:T(8,128)(2,1)S(1)}, bf16[4,512,512]{2,1,0:T(8,128)(2,1)S(1)}, u32[]{:S(2)}, u32[]{:S(2)}) collective-permute-start(bf16[4,512,512]{2,1,0:T(8,128)(2,1)S(1)} %get-tuple-element.118), channel_id=1, source_target_pairs={{0,1},{1,0},{2,3},{3,2},{4,5},{5,4},{6,7},{7,6},{8,9},{9,8},{10,11... | collective-permute-start | bytes 6291464 | tf_op jit(solution)/shard_map/key_weights_core/ppermute | solution.py:42
  145.9 3.4 %collective-permute-done.29.refs_1_ = bf16[128,4224]{1,0:T(8,128)(2,1)S(1)} collective-permute-done((bf16[128,4224]{1,0:T(8,128)(2,1)S(1)}, bf16[128,4224]{1,0:T(8,128)(2,1)S(1)}, u32[]{:S(2)}, u32[]{:S(2)}) %collective-permute-start.29) | collective-permute-done | bytes 1081376 | tf_op jit(solution)/shard_map/grad_second_3/ppermute | solution.py:31
  155.5 3.1 %collective-permute-done.34.refs_1_ = bf16[16,8320]{1,0:T(8,128)(2,1)S(1)} collective-permute-done((bf16[16,8320]{1,0:T(8,128)(2,1)S(1)}, bf16[16,8320]{1,0:T(8,128)(2,1)S(1)}, u32[]{:S(2)}, u32[]{:S(2)}) %collective-permute-start.34) | collective-permute-done | bytes 266272 | tf_op jit(solution)/shard_map/sum_far_first_3/ppermute | solution.py:31
  191.2 7.4 %collective-permute-start.48 = (bf16[4,32,1152]{2,1,0:T(8,128)(2,1)S(1)}, bf16[4,32,1152]{2,1,0:T(8,128)(2,1)S(1)}, u32[]{:S(2)}, u32[]{:S(2)}) collective-permute-start(bf16[4,32,1152]{2,1,0:T(8,128)(2,1)S(1)} %get-tuple-element.134), channel_id=1, source_target_pairs={{0,1},{1,0},{2,3},{3,2},{4,5},{5,4},{6,7},{7,6},{8,9},{9,8},{10,11... | collective-permute-start | bytes 884744 | tf_op jit(solution)/shard_map/final_core/ppermute | solution.py:42
  205.5 5.1 %place_rows.1 = (bf16[2048,512]{1,0:T(8,128)(2,1)}, bf16[2048,512]{1,0:T(8,128)(2,1)}) custom-call(s32[2]{0:T(128)S(1)} %pad_add_fusion.1.refs_0_, bf16[2048,512]{1,0:T(8,128)(2,1)S(1)} %bitcast.42, bf16[2048,512]{1,0:T(8,128)(2,1)S(1)} %bitcast.43, s32[1,256]{1,0:T(1,128)S(1)} %reshape.157.refs_3_, ...), custom_call_target="tpu_custom_call" | custom-call | flops 1 | bytes 1 | tf_op jit(solution)/shard_map/place_rows/pallas_call | solution.py:78
  (168 shorter events, 95.0 us)
Async XLA Ops:
  21.2 15.3 %collective-permute-start.5 = (bf16[32,8320]{1,0:T(8,128)(2,1)S(1)}, bf16[32,8320]{1,0:T(8,128)(2,1)S(1)}, u32[]{:S(2)}, u32[]{:S(2)}) collective-permute-start(bf16[32,8320]{1,0:T(8,128)(2,1)S(1)} %get-tuple-element.76.refs_0_), channel_id=1, source_target_pairs={{0,16},{1,65},{2,18},{3,67},{4,20},{5,69},{6,22},{7,71},{8,24},{9,... | collective-permute-start | bytes 1597448 | tf_op jit(solution)/shard_map/rows_first_2/ppermute | solution.py:31
  23.8 12.7 %collective-permute-start.4 = (bf16[32,8320]{1,0:T(8,128)(2,1)S(1)}, bf16[32,8320]{1,0:T(8,128)(2,1)S(1)}, u32[]{:S(2)}, u32[]{:S(2)}) collective-permute-start(bf16[32,8320]{1,0:T(8,128)(2,1)S(1)} %get-tuple-element.76.refs_0_), channel_id=1, source_target_pairs={{0,24},{1,97},{2,26},{3,99},{4,28},{5,101},{6,30},{7,103},{8,0},{9... | collective-permute-start | bytes 1597448 | tf_op jit(solution)/shard_map/rows_first_1/ppermute | solution.py:31
  39.3 12.5 %collective-permute-start.8 = (bf16[64,4224]{1,0:T(8,128)(2,1)S(1)}, bf16[64,4224]{1,0:T(8,128)(2,1)S(1)}, u32[]{:S(2)}, u32[]{:S(2)}) collective-permute-start(bf16[64,4224]{1,0:T(8,128)(2,1)S(1)} %get-tuple-element.79.refs_1_.refs_2_.refs_6_), channel_id=1, source_target_pairs={{0,96},{1,25},{2,98},{3,27},{4,100},{5,29},{6,102},{7,31},{8,104},... | collective-permute-start | bytes 1622024 | tf_op jit(solution)/shard_map/x_2_second_1/ppermute | solution.py:31
  40.3 11.8 %collective-permute-start.12 = (bf16[64,4224]{1,0:T(8,128)(2,1)S(1)}, bf16[64,4224]{1,0:T(8,128)(2,1)S(1)}, u32[]{:S(2)}, u32[]{:S(2)}) collective-permute-start(bf16[64,4224]{1,0:T(8,128)(2,1)S(1)} %get-tuple-element.78.refs_4_.refs_0_.refs_1_.refs_5_), channel_id=1, source_target_pairs={{0,32},{1,9},{2,34},{3,11},{4,36},{5,13},{6,38},{7,15},{8,40},{9,1... | collective-permute-start | bytes 1622024 | tf_op jit(solution)/shard_map/x_2_second_3/ppermute | solution.py:31
  46.3 11.6 %collective-permute-start.11 = (bf16[64,4224]{1,0:T(8,128)(2,1)S(1)}, bf16[64,4224]{1,0:T(8,128)(2,1)S(1)}, u32[]{:S(2)}, u32[]{:S(2)}) collective-permute-start(bf16[64,4224]{1,0:T(8,128)(2,1)S(1)} %collective-permute-done.10.refs_7_.refs_8_.refs_12_), channel_id=1, source_target_pairs={{0,32},{1,9},{2,34},{3,11},{4,36},{5,13},{6,38},{7,15},{8,40},{9,1... | collective-permute-start | bytes 1622024 | tf_op jit(solution)/shard_map/x_far_second_3/ppermute | solution.py:31
  46.3 11.6 %collective-permute-start.9 = (bf16[64,4224]{1,0:T(8,128)(2,1)S(1)}, bf16[64,4224]{1,0:T(8,128)(2,1)S(1)}, u32[]{:S(2)}, u32[]{:S(2)}) collective-permute-start(bf16[64,4224]{1,0:T(8,128)(2,1)S(1)} %collective-permute-done.7.refs_2_.refs_3_.refs_7_), channel_id=1, source_target_pairs={{0,96},{1,25},{2,98},{3,27},{4,100},{5,29},{6,102},{7,31},{8,104},... | collective-permute-start | bytes 1622024 | tf_op jit(solution)/shard_map/x_far_second_1/ppermute | solution.py:31
  52.2 25.8 %collective-permute-start.17 = (bf16[128,4096]{1,0:T(8,128)(2,1)S(1)}, bf16[128,4096]{1,0:T(8,128)(2,1)S(1)}, u32[]{:S(2)}, u32[]{:S(2)}) collective-permute-start(bf16[128,4096]{1,0:T(8,128)(2,1)S(1)} %stack_g.1.refs_11_.refs_0_.refs_9_), channel_id=1, source_target_pairs={{0,32},{1,9},{2,34},{3,11},{4,36},{5,13},{6,38},{7,15},{8,40},{9,1... | collective-permute-start | bytes 3145736 | tf_op jit(solution)/shard_map/g_second_3/ppermute | solution.py:31
  53.2 24.8 %collective-permute-start.16 = (bf16[128,4096]{1,0:T(8,128)(2,1)S(1)}, bf16[128,4096]{1,0:T(8,128)(2,1)S(1)}, u32[]{:S(2)}, u32[]{:S(2)}) collective-permute-start(bf16[128,4096]{1,0:T(8,128)(2,1)S(1)} %stack_g.1.refs_11_.refs_0_.refs_9_), channel_id=1, source_target_pairs={{0,96},{1,25},{2,98},{3,27},{4,100},{5,29},{6,102},{7,31},{8,104},... | collective-permute-start | bytes 3145736 | tf_op jit(solution)/shard_map/g_second_1/ppermute | solution.py:31
  63.2 11.7 %collective-permute-start.14 = (bf16[528,512]{1,0:T(8,128)(2,1)S(1)}, bf16[528,512]{1,0:T(8,128)(2,1)S(1)}, u32[]{:S(2)}, u32[]{:S(2)}) collective-permute-start(bf16[528,512]{1,0:T(8,128)(2,1)S(1)} %get-tuple-element.81.refs_1_), channel_id=1, source_target_pairs={{0,2},{1,3},{2,0},{3,1},{4,6},{5,7},{6,4},{7,5},{8,10},{9,11},{10,... | collective-permute-start | bytes 1622024 | tf_op jit(solution)/shard_map/pair_chip/ppermute | solution.py:47
  64.2 16.8 %collective-permute-start.13 = (bf16[528,512]{1,0:T(8,128)(2,1)S(1)}, bf16[528,512]{1,0:T(8,128)(2,1)S(1)}, u32[]{:S(2)}, u32[]{:S(2)}) collective-permute-start(bf16[528,512]{1,0:T(8,128)(2,1)S(1)} %get-tuple-element.81.refs_1_), channel_id=1, source_target_pairs={{0,1},{1,0},{2,3},{3,2},{4,5},{5,4},{6,7},{7,6},{8,9},{9,8},{10,11... | collective-permute-start | bytes 1622024 | tf_op jit(solution)/shard_map/pair_core/ppermute | solution.py:42
  78.1 13.2 %collective-permute-start.19 = (bf16[64,4096]{1,0:T(8,128)(2,1)S(1)}, bf16[64,4096]{1,0:T(8,128)(2,1)S(1)}, u32[]{:S(2)}, u32[]{:S(2)}) collective-permute-start(bf16[64,4096]{1,0:T(8,128)(2,1)S(1)} %get-tuple-element.85), channel_id=1, source_target_pairs={{0,32},{1,9},{2,34},{3,11},{4,36},{5,13},{6,38},{7,15},{8,40},{9,1... | collective-permute-start | bytes 1572872 | tf_op jit(solution)/shard_map/g_far_second_3/ppermute | solution.py:31
  79.0 12.3 %collective-permute-start.18 = (bf16[64,4096]{1,0:T(8,128)(2,1)S(1)}, bf16[64,4096]{1,0:T(8,128)(2,1)S(1)}, u32[]{:S(2)}, u32[]{:S(2)}) collective-permute-start(bf16[64,4096]{1,0:T(8,128)(2,1)S(1)} %get-tuple-element.83.refs_6_), channel_id=1, source_target_pairs={{0,96},{1,25},{2,98},{3,27},{4,100},{5,29},{6,102},{7,31},{8,104},... | collective-permute-start | bytes 1572872 | tf_op jit(solution)/shard_map/g_far_second_1/ppermute | solution.py:31
  101.7 13.2 %collective-permute-start.23 = (bf16[512,512]{1,0:T(8,128)(2,1)S(1)}, bf16[512,512]{1,0:T(8,128)(2,1)S(1)}, u32[]{:S(2)}, u32[]{:S(2)}) collective-permute-start(bf16[512,512]{1,0:T(8,128)(2,1)S(1)} %chip_sum.1.refs_16_), channel_id=1, source_target_pairs={{0,2},{1,3},{2,0},{3,1},{4,6},{5,7},{6,4},{7,5},{8,10},{9,11},{10,... | collective-permute-start | bytes 1572872 | tf_op jit(solution)/shard_map/key_grads_chip/ppermute | solution.py:47
  102.8 21.1 %collective-permute-start.27 = (bf16[128,4096]{1,0:T(8,128)(2,1)S(1)}, bf16[128,4096]{1,0:T(8,128)(2,1)S(1)}, u32[]{:S(2)}, u32[]{:S(2)}) collective-permute-start(bf16[128,4096]{1,0:T(8,128)(2,1)S(1)} %get-tuple-element.95.refs_2_), channel_id=1, source_target_pairs={{0,32},{1,9},{2,34},{3,11},{4,36},{5,13},{6,38},{7,15},{8,40},{9,1... | collective-permute-start | bytes 3145736 | tf_op jit(solution)/shard_map/out_second_3/ppermute | solution.py:31
  103.7 18.4 %collective-permute-start.28 = (bf16[128,4096]{1,0:T(8,128)(2,1)S(1)}, bf16[128,4096]{1,0:T(8,128)(2,1)S(1)}, u32[]{:S(2)}, u32[]{:S(2)}) collective-permute-start(bf16[128,4096]{1,0:T(8,128)(2,1)S(1)} %get-tuple-element.104), channel_id=1, source_target_pairs={{0,96},{1,25},{2,98},{3,27},{4,100},{5,29},{6,102},{7,31},{8,104},... | collective-permute-start | bytes 3145736 | tf_op jit(solution)/shard_map/out_second_1/ppermute | solution.py:31
  110.2 13.7 %collective-permute-start.26 = (bf16[512,512]{1,0:T(8,128)(2,1)S(1)}, bf16[512,512]{1,0:T(8,128)(2,1)S(1)}, u32[]{:S(2)}, u32[]{:S(2)}) collective-permute-start(bf16[512,512]{1,0:T(8,128)(2,1)S(1)} %get-tuple-element.96.refs_15_), channel_id=1, source_target_pairs={{0,1},{1,0},{2,3},{3,2},{4,5},{5,4},{6,7},{7,6},{8,9},{9,8},{10,11... | collective-permute-start | bytes 1572872 | tf_op jit(solution)/shard_map/query_weights_far_core/ppermute | solution.py:42
  111.5 22.3 %collective-permute-start.31 = (bf16[3,512,512]{2,1,0:T(8,128)(2,1)S(1)}, bf16[3,512,512]{2,1,0:T(8,128)(2,1)S(1)}, u32[]{:S(2)}, u32[]{:S(2)}) collective-permute-start(bf16[3,512,512]{2,1,0:T(8,128)(2,1)S(1)} %get-tuple-element.109), channel_id=1, source_target_pairs={{0,1},{1,0},{2,3},{3,2},{4,5},{5,4},{6,7},{7,6},{8,9},{9,8},{10,11... | collective-permute-start | bytes 4718600 | tf_op jit(solution)/shard_map/query_weights_core/ppermute | solution.py:42
  131.1 14.8 %collective-permute-start.30 = (bf16[128,4224]{1,0:T(8,128)(2,1)S(1)}, bf16[128,4224]{1,0:T(8,128)(2,1)S(1)}, u32[]{:S(2)}, u32[]{:S(2)}) collective-permute-start(bf16[128,4224]{1,0:T(8,128)(2,1)S(1)} %get-tuple-element.107), channel_id=1, source_target_pairs={{0,96},{1,25},{2,98},{3,27},{4,100},{5,29},{6,102},{7,31},{8,104},... | collective-permute-start | bytes 3244040 | tf_op jit(solution)/shard_map/grad_second_1/ppermute | solution.py:31
  133.8 15.5 %collective-permute-start.29 = (bf16[128,4224]{1,0:T(8,128)(2,1)S(1)}, bf16[128,4224]{1,0:T(8,128)(2,1)S(1)}, u32[]{:S(2)}, u32[]{:S(2)}) collective-permute-start(bf16[128,4224]{1,0:T(8,128)(2,1)S(1)} %get-tuple-element.106.refs_4_), channel_id=1, source_target_pairs={{0,32},{1,9},{2,34},{3,11},{4,36},{5,13},{6,38},{7,15},{8,40},{9,1... | collective-permute-start | bytes 3244040 | tf_op jit(solution)/shard_map/grad_second_3/ppermute | solution.py:31
  134.1 18.0 %collective-permute-start.37 = (bf16[512,512]{1,0:T(8,128)(2,1)S(1)}, bf16[512,512]{1,0:T(8,128)(2,1)S(1)}, u32[]{:S(2)}, u32[]{:S(2)}) collective-permute-start(bf16[512,512]{1,0:T(8,128)(2,1)S(1)} %get-tuple-element.119), channel_id=1, source_target_pairs={{0,2},{1,3},{2,4},{3,5},{4,6},{5,7},{6,0},{7,1},{8,10},{9,11},{10,... | collective-permute-start | bytes 1572872 | tf_op jit(solution)/shard_map/query_weights_z_1/ppermute | solution.py:37
  135.1 17.0 %collective-permute-start.38 = (bf16[512,512]{1,0:T(8,128)(2,1)S(1)}, bf16[512,512]{1,0:T(8,128)(2,1)S(1)}, u32[]{:S(2)}, u32[]{:S(2)}) collective-permute-start(bf16[512,512]{1,0:T(8,128)(2,1)S(1)} %get-tuple-element.120), channel_id=1, source_target_pairs={{0,6},{1,7},{2,0},{3,1},{4,2},{5,3},{6,4},{7,5},{8,14},{9,15},{10,... | collective-permute-start | bytes 1572872 | tf_op jit(solution)/shard_map/query_weights_z_3/ppermute | solution.py:37
  159.6 17.9 %collective-permute-start.40 = (bf16[32,8320]{1,0:T(8,128)(2,1)}, bf16[32,8320]{1,0:T(8,128)(2,1)}, u32[]{:S(2)}, u32[]{:S(2)}) collective-permute-start(bf16[32,8320]{1,0:T(8,128)(2,1)} %get-tuple-element.123), channel_id=1, source_target_pairs={{0,24},{1,97},{2,26},{3,99},{4,28},{5,101},{6,30},{7,103},{8,0},{9... | collective-permute-start | bytes 1597448 | tf_op jit(solution)/shard_map/sum_first_1/ppermute | solution.py:31
  159.6 17.9 %collective-permute-start.39 = (bf16[32,8320]{1,0:T(8,128)(2,1)}, bf16[32,8320]{1,0:T(8,128)(2,1)}, u32[]{:S(2)}, u32[]{:S(2)}) collective-permute-start(bf16[32,8320]{1,0:T(8,128)(2,1)} %get-tuple-element.122.refs_3_), channel_id=1, source_target_pairs={{0,8},{1,33},{2,10},{3,35},{4,12},{5,37},{6,14},{7,39},{8,16},{9,4... | collective-permute-start | bytes 1597448 | tf_op jit(solution)/shard_map/sum_first_3/ppermute | solution.py:31
  161.1 12.5 %collective-permute-start.41 = (bf16[256,512]{1,0:T(8,128)(2,1)S(1)}, bf16[256,512]{1,0:T(8,128)(2,1)S(1)}, u32[]{:S(2)}, u32[]{:S(2)}) collective-permute-start(bf16[256,512]{1,0:T(8,128)(2,1)S(1)} %get-tuple-element.121.refs_4_), channel_id=1, source_target_pairs={{0,2},{1,3},{2,4},{3,5},{4,6},{5,7},{6,0},{7,1},{8,10},{9,11},{10,... | collective-permute-start | bytes 786440 | tf_op jit(solution)/shard_map/key_weights_far_z_1/ppermute | solution.py:37
  (47 other events, 381.3 us)

commit v4 on v3

--- a/solution.py
+++ b/solution.py
@@ -470,43 +470,68 @@
     )(q, *pieces, table)
 
 
-def backward_kernel(q, kv0, kv1, kv2, kv3, probs, grad, att, table, gq, near, mid, sent):
+def backward_part(h, first, kvs, q, probs, grad, att, outs):
     scale = 128 ** (-0.5)
-    places = ((near, 0), (sent, 512), (mid, 0), (sent, 0))
+    head = slice(h * 128, h * 128 + 128)
+    g = grad[:, head]
+    delta = jnp.sum(g.astype(F32) * att[:, head].astype(F32), -1, keepdims=True)
+    total = None
+    for i, (kv, out) in enumerate(zip(kvs, outs)):
+        p = probs[h, :, (first + i) * 512 : (first + i + 1) * 512]
+        key, value = kv[:512, h * 256 : h * 256 + 128], kv[:512, h * 256 + 128 : h * 256 + 256]
+        dp = lax.dot_general(g, value, LAST, preferred_element_type=F32)
+        ds = (p.astype(F32) * (dp - delta)).astype(BF)
+        part = jnp.dot(ds, key, preferred_element_type=F32)
+        total = part if total is None else total + part
+        dk = lax.dot_general(ds, q[:, head], ROWS, preferred_element_type=F32) * scale
+        dv = lax.dot_general(p, g, ROWS, preferred_element_type=F32)
+        row = 0
+        for ref in out:
+            rows = slice(row, row + ref.shape[0])
+            ref[:, h * 256 : h * 256 + 128] = dk[rows].astype(BF)
+            ref[:, h * 256 + 128 : h * 256 + 256] = dv[rows].astype(BF)
+            row += ref.shape[0]
+    return total
+
+
+def backward_far_kernel(q, kv2, kv3, probs, grad, att, total, mid, sent):
+    for h in range(2):
+        part = backward_part(h, 2, (kv2, kv3), q, probs, grad, att, ((mid,), (sent,)))
+        total[:, h * 128 : h * 128 + 128] = part
+
+
+def backward_near_kernel(q, kv0, kv1, probs, grad, att, table, total, gq, near, sent_a, sent_b):
     for h in range(2):
         head = slice(h * 128, h * 128 + 128)
-        g = grad[:, head]
-        delta = jnp.sum(g.astype(F32) * att[:, head].astype(F32), -1, keepdims=True)
-        total = None
-        for i, kv in enumerate((kv0, kv1, kv2, kv3)):
-            p = probs[h, :, i * 512 : (i + 1) * 512]
-            key, value = kv[:512, h * 256 : h * 256 + 128], kv[:512, h * 256 + 128 : h * 256 + 256]
-            dp = lax.dot_general(g, value, LAST, preferred_element_type=F32)
-            ds = (p.astype(F32) * (dp - delta)).astype(BF)
-            part = jnp.dot(ds, key, preferred_element_type=F32)
-            total = part if total is None else total + part
-            dk = lax.dot_general(ds, q[:, head], ROWS, preferred_element_type=F32) * scale
-            dv = lax.dot_general(p, g, ROWS, preferred_element_type=F32)
-            out, row = places[i]
-            out[row : row + 512, h * 256 : h * 256 + 128] = dk.astype(BF)
-            out[row : row + 512, h * 256 + 128 : h * 256 + 256] = dv.astype(BF)
-        u = total * scale
+        part = backward_part(h, 0, (kv0, kv1), q, probs, grad, att, ((near,), (sent_a, sent_b)))
+        u = (part + total[:, head]) * 128 ** (-0.5)
         gq[:, head] = (u * table[:, :128] - pltpu.roll(u, 64, 1) * table[:, 128:256]).astype(BF)
 
 
-def attend_back(q, pieces, probs, grad, att, table):
-    return call(
-        backward_kernel,
-        "attention_backward",
-        [shape(512, 256), shape(512, 512), shape(512, 512), shape(1024, 512)],
-        room=20,
-        in_specs=[WHOLE] * 9,
+def attend_back_far(q, pieces, probs, grad, att):
+    return call(
+        backward_far_kernel,
+        "attention_backward_far",
+        [shape(512, 256, dtype=F32), shape(512, 512), shape(512, 512)],
+        room=16,
+        in_specs=[WHOLE] * 6,
+        out_specs=[WHOLE] * 3,
+    )(q, *pieces[2:], probs, grad, att)
+
+
+def attend_back_near(q, pieces, probs, grad, att, table, total):
+    return call(
+        backward_near_kernel,
+        "attention_backward_near",
+        [shape(512, 256), shape(512, 512), shape(256, 512), shape(256, 512)],
+        room=16,
+        in_specs=[WHOLE] * 8,
         out_specs=[WHOLE] * 4,
-    )(q, *pieces, probs, grad, att, table)
+    )(q, *pieces[:2], probs, grad, att, table, total)
 
 
 def chip_sum_kernel(mid, recv, out):
-    out[...] = mid[...] + recv[:512]
+    out[...] = mid[...] + recv[...]
 
 
 def chip_sum(mid, recv):
@@ -519,9 +544,10 @@
     )(mid, recv)
 
 
-def feature_kernel(near, recv, chip, gq, table, *refs):
+def feature_kernel(near, recv_a, recv_b, chip, gq, table, *refs):
     x, w, gain, gp, gp_kv, parts, ride = refs[:8], refs[8], refs[9], refs[10], refs[11], refs[12:17], refs[17]
-    own = near[...].astype(F32) + recv[512:].astype(F32) + chip[...].astype(F32)
+    recv = joined((recv_a, recv_b))
+    own = near[...].astype(F32) + recv.astype(F32) + chip[...].astype(F32)
     gp[:, :256] = gq[...]
     for h in range(2):
         u = own[:, h * 256 : h * 256 + 128]
@@ -551,10 +577,10 @@
         [shape(512, 768), shape(512, 512)] + [shape(n, WIDE) for n in G_PIECES],
         room=26,
         after=after,
-        in_specs=[WHOLE] * 15,
+        in_specs=[WHOLE] * 16,
         out_specs=[WHOLE] * 7,
         scratch_shapes=[pltpu.VMEM((32, 128), F32)],
-    )(near, recv, chip, gq, table, *x, w, gain)
+    )(near, *recv, chip, gq, table, *x, w, gain)
     return out[1], out[2:]
 
 
@@ -753,12 +779,16 @@
     return [parts[0]] + [send_z(parts[d], d, "final") for d in (1, 2, 3)]
 
 
-def columns_kernel(where, p0, p1, p2, p3, out, gain):
+def columns_kernel(where, p0, p1, p2, p3, out, mine, gain):
     total = jnp.zeros((32, EXTRA), F32)
     for d, piece in enumerate((p0, p1, p2, p3)):
         for half in range(2):
-            start = pl.multiple_of(half * 1024 + (1 - where[1]) * 512, 512)
-            out[d, :, half * 512 : half * 512 + 512] = piece[:, pl.ds(start, 512)]
+            columns = slice(half * 512, half * 512 + 512)
+            first = half * 1024
+            start = pl.multiple_of(first + (1 - where[1]) * 512, 512)
+            out[d, :, columns] = piece[:, pl.ds(start, 512)]
+            start = pl.multiple_of(first + where[1] * 512, 512)
+            mine[d, :, columns] = piece[:, pl.ds(start, 512)]
         total += piece[:, 2048:].astype(F32)
     high = total.astype(BF)
     low = (total - high.astype(F32)).astype(BF)
@@ -768,46 +798,46 @@
 
 
 def other_columns(where, pieces):
-    sent, gain = call(
+    sent, mine, gain = call(
         columns_kernel,
         "columns",
-        [shape(4, 32, 1024 + EXTRA), shape(32, EXTRA, dtype=F32)],
+        [shape(4, 32, 1024 + EXTRA), shape(4, 32, 1024), shape(32, EXTRA, dtype=F32)],
         in_specs=[SMEM] + [WHOLE] * 4,
-        out_specs=[WHOLE] * 2,
+        out_specs=[WHOLE] * 3,
     )(where, *pieces)
-    return swap_core(sent, "final"), gain
-
-
-def place_kernel(where, hidden, grads, places, p0, p1, p2, p3, other, out_h, out_g, rows):
+    return mine, swap_core(sent, "final"), gain
+
+
+def place_kernel(hidden, grads, index, mine, other, where, out_h, out_g, rows):
     step = pl.program_id(0)
 
     @pl.when(step == 0)
     def _():
-        for half in range(2):
-            columns = slice(half * 512, half * 512 + 512)
-            start = pl.multiple_of(half * 1024 + where[1] * 512, 512)
-            for d, piece in enumerate((p0, p1, p2, p3)):
-                rows[d * 32 : d * 32 + 32, columns] = piece[:, pl.ds(start, 512)]
-                rows[128 + d * 32 : 160 + d * 32, columns] = other[d, :, columns]
-
-    token = step * 256 + lax.broadcasted_iota(jnp.int32, (256, 256), 0)
-    hot = (token == places[...]).astype(F32).astype(BF)
-    added = jnp.dot(hot, rows[...], preferred_element_type=F32)
+        for d in range(4):
+            first = lax.rem(where[0] - d + 4, 4) * 64
+            rows[pl.ds(pl.multiple_of(first + where[1] * 32, 32), 32), :] = mine[d]
+            rows[pl.ds(pl.multiple_of(first + (1 - where[1]) * 32, 32), 32), :] = other[d, :, :1024]
+
+    slab = step // 4
+    token = (step - slab * 4) * 256 + lax.broadcasted_iota(jnp.int32, (256, 128), 0)
+    hot = (token == index[0]).astype(F32).astype(BF)
+    own = rows[pl.ds(pl.multiple_of(slab * 128, 128), 128), :]
+    added = jnp.dot(hot, own, preferred_element_type=F32)
     out_h[...] = (hidden[...].astype(F32) + added[:, :512]).astype(BF)
     out_g[...] = (grads[...].astype(F32) + added[:, 512:]).astype(BF)
 
 
-def place_rows(where, hidden, grads, places, pieces, other):
+def place_rows(where, hidden, grads, index, mine, other):
     block = pl.BlockSpec((256, 512), lambda i: (i, 0))
     return call(
         place_kernel,
         "place_rows",
         [pltpu.HBM((2048, 512), BF)] * 2,
         grid=(8,),
-        in_specs=[SMEM, block, block] + [WHOLE] * 6,
+        in_specs=[block, block, pl.BlockSpec((1, 1, 128), lambda i: (i // 4, 0, 0)), WHOLE, WHOLE, SMEM],
         out_specs=[block] * 2,
         scratch_shapes=[pltpu.VMEM((256, 1024), BF)],
-    )(where, hidden, grads, places, *pieces, other)
+    )(hidden, grads, index, mine, other, where)
 
 
 def shards(hidden_in, route_index, norm_gain, w_qkv, w_out, cotangent):
@@ -845,10 +875,13 @@
 
     out_state = reduce_start(output_parts(attended, w_back), "out")
     grad_attended = attended_grad(g, w_back)
-    grad_q, near, mid, sent = attend_back(queries, pieces, probs, grad_attended, attended, table)
-    recv = swap_core(sent, "key_grads")
+    total, mid, sent = attend_back_far(queries, pieces, probs, grad_attended, attended)
+    chip_part = swap_chip(chip_sum(mid, swap_core(sent, "key_far")), "key_grads")
+    grad_q, near, *sent = attend_back_near(
+        queries, pieces, probs, grad_attended, attended, table, total
+    )
+    recv = [swap_core(part, "key_near") for part in sent]
     out_terms = reduce_add(out_state, "out")
-    chip_part = swap_chip(chip_sum(mid, recv), "key_grads")
     swapped_a = swap_weights(query_weights(where, x, g, grad_q, attended), "query_weights")
 
     gp_kv, parts = feature_parts(near, recv, chip_part, grad_q, table, x, w_in, gain, ())
@@ -864,14 +897,15 @@
     terms_b = sum_near(state_b, "key_weights")
     final = final_rows(where, *column, rows_own, gain)
     grad_w_qkv, grad_w_out = sum_weights(terms_a, terms_b)
-    other, gain_part = other_columns(where, final)
-
-    chips = (z - jnp.arange(4)) % 4
-    by_chip = (local_index + jnp.arange(2, dtype=jnp.int32)[:, None] * 1024).reshape(4, 2, 32)
-    by_core = jnp.stack([dyn(by_chip, core, 1), dyn(by_chip, 1 - core, 1)])
-    places = jnp.stack([dyn(by_core, chips[d], 1) for d in range(4)], 1).reshape(1, 256)
+    mine, other, gain_part = other_columns(where, final)
+
     hidden_out, grad_in = place_rows(
-        where, hidden_in.reshape(2048, 512), cotangent.reshape(2048, 512), places, final, other
+        where,
+        from_hbm(hidden_in.reshape(2048, 512)),
+        from_hbm(cotangent.reshape(2048, 512)),
+        route_index,
+        mine,
+        other,
     )
     grad_gain = gain_part + other[0, :, 1024:].astype(F32) + other[1, :, 1024:].astype(F32)
     return (

time: 211 us -> 205 us (0.972)
  waiting for transfers between devices: 57.4 us -> 67.8 us
  local copies, waits for them, and re-layouts: 13.8 us -> 5.61 us
  between operations: 8.77 us -> 0.97 us
    ppermute x14, waiting for transfers between devices: 9.6 us -> 18.8 us  [send_z(): return lax.ppermute(values, 'cmp', pairs)]
    unnamed x45 -> x22, local copies, waits for them, and re-layouts: 9.98 us -> 4.45 us
    ppermute x25, waiting for transfers between devices: 34.3 us -> 39.6 us  [ring(): return lax.ppermute(values, BOTH, ring_pairs(second, shift))]
    ppermute x2, waiting for transfers between devices: 11.5 us -> 8.17 us  [swap_chip(): return lax.ppermute(values, 'cmp', [(k, k ^ 2) for k in range(8)])]
    ppermute x25, starting transfers between devices: 30.8 us -> 33.1 us  [ring(): return lax.ppermute(values, BOTH, ring_pairs(second, shift))]
    pallas_call x28 -> x29, Pallas kernels: 56.3 us -> 55.3 us  [invoke(): pl.pallas_call(body, out_shape=out_shape, compiler_params=pltpu.CompilerP...]
    ppermute x8 -> x10, starting transfers between devices: 20.1 us -> 20.3 us  [swap_core(): return lax.ppermute(values, 'cmp', [(k, k ^ 1) for k in range(8)])]
  transfers between devices with their start and end apart: 49 -> 51, of which waited for: 21 -> 25; matrix products, arithmetic and copies ran while one was open for 2% -> 1% of each run, Pallas kernels for 22% -> 19%
where the time goes in v4:
time: 205 us
  starting transfers between devices  74.5 us (36%)
  waiting for transfers between devices  67.8 us (33%)
  Pallas kernels  55.3 us (27%)
  local copies, waits for them, and re-layouts  5.61 us (3%)
    pallas_call x29, Pallas kernels, invoke(): pl.pallas_call(body, out_shape=out_shape, compiler_params=pltpu.CompilerP...  55.3 us
    ppermute x25, waiting for transfers between devices, ring(): return lax.ppermute(values, BOTH, ring_pairs(second, shift))  39.6 us
    ppermute x25, starting transfers between devices, ring(): return lax.ppermute(values, BOTH, ring_pairs(second, shift))  33.1 us
    ppermute x10, starting transfers between devices, swap_core(): return lax.ppermute(values, 'cmp', [(k, k ^ 1) for k in range(8)])  20.3 us
    ppermute x14, starting transfers between devices, send_z(): return lax.ppermute(values, 'cmp', pairs)  19 us
    ppermute x14, waiting for transfers between devices, send_z(): return lax.ppermute(values, 'cmp', pairs)  18.8 us
    ppermute x2, waiting for transfers between devices, swap_chip(): return lax.ppermute(values, 'cmp', [(k, k ^ 2) for k in range(8)])  8.17 us
    unnamed x22, local copies, waits for them, and re-layouts  4.45 us
  transfers between devices with their start and end apart: 51, of which 25 were waited for; matrix products, arithmetic and copies ran while one was open for 1% of the time, Pallas kernels for 19%

profile of v4, /device:TPU:1, one launch (start us, length us, event | category | flops | bytes accessed | tf_op | source)
XLA Modules:
  0.0 205.0 jit_solution(5139548068698032991)
XLA Ops:
  6.7 3.3 %collective-permute-start.1 = (bf16[2,2,32,512]{3,2,1,0:T(8,128)(2,1)S(1)}, bf16[2,2,32,512]{3,2,1,0:T(8,128)(2,1)S(1)}, u32[]{:S(2)}, u32[]{:S(2)}) collective-permute-start(bf16[2,2,32,512]{3,2,1,0:T(8,128)(2,1)S(1)} %get-tuple-element.78), channel_id=1, source_target_pairs={{0,4},{1,5},{2,6},{3,7},{4,0},{5,1},{6,2},{7,3},{8,12},{9,13},{10,... | collective-permute-start | bytes 393224 | tf_op jit(solution)/shard_map/rows_z_2/ppermute | solution.py:37
  12.0 3.7 %collective-permute-done.1.refs_3_ = bf16[2,2,32,512]{3,2,1,0:T(8,128)(2,1)S(1)} collective-permute-done((bf16[2,2,32,512]{3,2,1,0:T(8,128)(2,1)S(1)}, bf16[2,2,32,512]{3,2,1,0:T(8,128)(2,1)S(1)}, u32[]{:S(2)}, u32[]{:S(2)}) %collective-permute-start.1) | collective-permute-done | bytes 131104 | tf_op jit(solution)/shard_map/rows_z_2/ppermute | solution.py:37
  30.0 6.5 %collective-permute-done.5.refs_2_ = bf16[32,8320]{1,0:T(8,128)(2,1)S(1)} collective-permute-done((bf16[32,8320]{1,0:T(8,128)(2,1)S(1)}, bf16[32,8320]{1,0:T(8,128)(2,1)S(1)}, u32[]{:S(2)}, u32[]{:S(2)}) %collective-permute-start.5) | collective-permute-done | bytes 532512 | tf_op jit(solution)/shard_map/rows_first_2/ppermute | solution.py:31
  40.8 5.6 %collective-permute-done.10.refs_7_.refs_8_.refs_13_ = bf16[64,4224]{1,0:T(8,128)(2,1)S(1)} collective-permute-done((bf16[64,4224]{1,0:T(8,128)(2,1)S(1)}, bf16[64,4224]{1,0:T(8,128)(2,1)S(1)}, u32[]{:S(2)}, u32[]{:S(2)}) %collective-permute-start.10) | collective-permute-done | bytes 540704 | tf_op jit(solution)/shard_map/x_1_second_3/ppermute | solution.py:31
  57.9 5.3 %project.1 = (bf16[512,256]{1,0:T(8,128)(2,1)S(1)}, bf16[528,512]{1,0:T(8,128)(2,1)S(1)}, f32[512,384]{1,0:T(8,128)S(1)}) custom-call(bf16[64,4224]{1,0:T(8,128)(2,1)S(1)} %get-tuple-element.82.refs_4_.refs_0_.refs_1_.refs_6_, bf16[64,4224]{1,0:T(8,128)(2,1)S(1)} %get-tuple-element.83.refs_1_.refs_2_.refs_7_, ...), custom_call_target="tpu_custom_call" | custom-call | flops 1 | bytes 1 | tf_op jit(solution)/shard_map/project/pallas_call | solution.py:78
  66.7 8.2 %collective-permute-done.14.refs_3_.refs_1_ = bf16[528,512]{1,0:T(8,128)(2,1)S(1)} collective-permute-done((bf16[528,512]{1,0:T(8,128)(2,1)S(1)}, bf16[528,512]{1,0:T(8,128)(2,1)S(1)}, u32[]{:S(2)}, u32[]{:S(2)}) %collective-permute-start.14) | collective-permute-done | bytes 540704 | tf_op jit(solution)/shard_map/pair_chip/ppermute | solution.py:47
  74.9 3.1 %collective-permute-start.15 = (bf16[528,512]{1,0:T(8,128)(2,1)S(1)}, bf16[528,512]{1,0:T(8,128)(2,1)S(1)}, u32[]{:S(2)}, u32[]{:S(2)}) collective-permute-start(bf16[528,512]{1,0:T(8,128)(2,1)S(1)} %collective-permute-done.14.refs_3_.refs_1_), channel_id=1, source_target_pairs={{0,1},{1,0},{2,3},{3,2},{4,5},{5,4},{6,7},{7,6},{8,9},{9,8},{10,11... | collective-permute-start | bytes 1622024 | tf_op jit(solution)/shard_map/far_pair_core/ppermute | solution.py:42
  81.1 6.4 %attention_forward.1 = (bf16[512,256]{1,0:T(8,128)(2,1)S(1)}, bf16[2,512,2048]{2,1,0:T(8,128)(2,1)S(1)}) custom-call(bf16[512,256]{1,0:T(8,128)(2,1)S(1)} %get-tuple-element.84.refs_2_.refs_0_, bf16[528,512]{1,0:T(8,128)(2,1)S(1)} %get-tuple-element.85.refs_1_, bf16[528,512]{1,0:T(8,128)(2,1)S(1)} %collective-permute-done.13.refs_2_, ...), custom_call_target="tpu_custom_call" | custom-call | flops 1 | bytes 1 | tf_op jit(solution)/shard_map/attention_forward/pallas_call | solution.py:78
  103.7 3.4 %collective-permute-done.24.refs_1_ = bf16[64,4096]{1,0:T(8,128)(2,1)S(1)} collective-permute-done((bf16[64,4096]{1,0:T(8,128)(2,1)S(1)}, bf16[64,4096]{1,0:T(8,128)(2,1)S(1)}, u32[]{:S(2)}, u32[]{:S(2)}) %collective-permute-start.24) | collective-permute-done | bytes 524320 | tf_op jit(solution)/shard_map/out_second_3/ppermute | solution.py:31
  107.4 4.8 %query_weights.1 = (bf16[4,512,512]{2,1,0:T(8,128)(2,1)S(1)}, bf16[512,512]{1,0:T(8,128)(2,1)S(1)}, bf16[3,512,512]{2,1,0:T(8,128)(2,1)S(1)}) custom-call(s32[2]{0:T(128)S(1)} %pad_add_fusion.refs_0_.refs_5_, bf16[64,4224]{1,0:T(8,128)(2,1)S(1)} %get-tuple-element.82.refs_4_.refs_0_.refs_1_.refs_6_, ...), custom_call_target="tpu_custom_call" | custom-call | flops 1 | bytes 1 | tf_op jit(solution)/shard_map/query_weights/pallas_call | solution.py:78
  116.1 6.2 %feature_parts.1 = (bf16[512,768]{1,0:T(8,128)(2,1)}, bf16[512,512]{1,0:T(8,128)(2,1)S(1)}, bf16[128,4224]{1,0:T(8,128)(2,1)S(1)}, bf16[128,4224]{1,0:T(8,128)(2...) custom-call(bf16[512,512]{1,0:T(8,128)(2,1)S(1)} %get-tuple-element.95.refs_0_, ...), custom_call_target="tpu_custom_call" | custom-call | flops 30000001024 | bytes 1 | tf_op jit(solution)/shard_map/feature_parts/pallas_call | solution.py:78
  128.8 3.2 %collective-permute-done.26.refs_1_ = bf16[64,4224]{1,0:T(8,128)(2,1)S(1)} collective-permute-done((bf16[64,4224]{1,0:T(8,128)(2,1)S(1)}, bf16[64,4224]{1,0:T(8,128)(2,1)S(1)}, u32[]{:S(2)}, u32[]{:S(2)}) %collective-permute-start.26) | collective-permute-done | bytes 540704 | tf_op jit(solution)/shard_map/grad_second_3/ppermute | solution.py:31
  132.7 3.2 %collective-permute-start.32 = (bf16[128,4224]{1,0:T(8,128)(2,1)S(1)}, bf16[128,4224]{1,0:T(8,128)(2,1)S(1)}, u32[]{:S(2)}, u32[]{:S(2)}) collective-permute-start(bf16[128,4224]{1,0:T(8,128)(2,1)S(1)} %get-tuple-element.114), channel_id=1, source_target_pairs={{0,96},{1,25},{2,98},{3,27},{4,100},{5,29},{6,102},{7,31},{8,104},... | collective-permute-start | bytes 3244040 | tf_op jit(solution)/shard_map/grad_second_1/ppermute | solution.py:31
  138.9 4.5 %key_weights.1 = (bf16[4,512,512]{2,1,0:T(8,128)(2,1)S(1)}, bf16[4,512,512]{2,1,0:T(8,128)(2,1)S(1)}) custom-call(s32[2]{0:T(128)S(1)} %pad_add_fusion.refs_0_.refs_5_, bf16[64,4224]{1,0:T(8,128)(2,1)S(1)} %get-tuple-element.82.refs_4_.refs_0_.refs_1_.refs_6_, bf16[64,4224]{1,0:T(8,128)(2,1)S(1)} %get-tuple-element.83.refs_1_.refs_2_.refs_7_, ...), custom_call_target="tpu_custom_call" | custom-call | flops 1 | bytes 1 | tf_op jit(solution)/shard_map/key_weights/pallas_call | solution.py:78
  143.4 3.4 %collective-permute-start.38 = (bf16[4,512,512]{2,1,0:T(8,128)(2,1)S(1)}, bf16[4,512,512]{2,1,0:T(8,128)(2,1)S(1)}, u32[]{:S(2)}, u32[]{:S(2)}) collective-permute-start(bf16[4,512,512]{2,1,0:T(8,128)(2,1)S(1)} %get-tuple-element.125), channel_id=1, source_target_pairs={{0,1},{1,0},{2,3},{3,2},{4,5},{5,4},{6,7},{7,6},{8,9},{9,8},{10,11... | collective-permute-start | bytes 6291464 | tf_op jit(solution)/shard_map/key_weights_core/ppermute | solution.py:42
  148.0 3.4 %collective-permute-done.31.refs_1_ = bf16[128,4224]{1,0:T(8,128)(2,1)S(1)} collective-permute-done((bf16[128,4224]{1,0:T(8,128)(2,1)S(1)}, bf16[128,4224]{1,0:T(8,128)(2,1)S(1)}, u32[]{:S(2)}, u32[]{:S(2)}) %collective-permute-start.31) | collective-permute-done | bytes 1081376 | tf_op jit(solution)/shard_map/grad_second_3/ppermute | solution.py:31
  152.2 3.0 %collective-permute-start.37 = (bf16[16,8320]{1,0:T(8,128)(2,1)S(1)}, bf16[16,8320]{1,0:T(8,128)(2,1)S(1)}, u32[]{:S(2)}, u32[]{:S(2)}) collective-permute-start(bf16[16,8320]{1,0:T(8,128)(2,1)S(1)} %get-tuple-element.124), channel_id=1, source_target_pairs={{0,24},{1,97},{2,26},{3,99},{4,28},{5,101},{6,30},{7,103},{8,0},{9... | collective-permute-start | bytes 798728 | tf_op jit(solution)/shard_map/sum_far_first_1/ppermute | solution.py:31
  155.4 3.1 %collective-permute-done.37.refs_3_ = bf16[16,8320]{1,0:T(8,128)(2,1)S(1)} collective-permute-done((bf16[16,8320]{1,0:T(8,128)(2,1)S(1)}, bf16[16,8320]{1,0:T(8,128)(2,1)S(1)}, u32[]{:S(2)}, u32[]{:S(2)}) %collective-permute-start.37) | collective-permute-done | bytes 266272 | tf_op jit(solution)/shard_map/sum_far_first_1/ppermute | solution.py:31
  158.5 3.1 %collective-permute-done.36.refs_1_ = bf16[16,8320]{1,0:T(8,128)(2,1)S(1)} collective-permute-done((bf16[16,8320]{1,0:T(8,128)(2,1)S(1)}, bf16[16,8320]{1,0:T(8,128)(2,1)S(1)}, u32[]{:S(2)}, u32[]{:S(2)}) %collective-permute-start.36) | collective-permute-done | bytes 266272 | tf_op jit(solution)/shard_map/sum_far_first_3/ppermute | solution.py:31
  165.5 3.3 %collective-permute-done.44.refs_2_ = bf16[256,512]{1,0:T(8,128)(2,1)S(1)} collective-permute-done((bf16[256,512]{1,0:T(8,128)(2,1)S(1)}, bf16[256,512]{1,0:T(8,128)(2,1)S(1)}, u32[]{:S(2)}, u32[]{:S(2)}) %collective-permute-start.44) | collective-permute-done | bytes 262176 | tf_op jit(solution)/shard_map/key_weights_far_z_3/ppermute | solution.py:37
  168.8 3.4 %collective-permute-done.43.refs_1_ = bf16[256,512]{1,0:T(8,128)(2,1)S(1)} collective-permute-done((bf16[256,512]{1,0:T(8,128)(2,1)S(1)}, bf16[256,512]{1,0:T(8,128)(2,1)S(1)}, u32[]{:S(2)}, u32[]{:S(2)}) %collective-permute-start.43) | collective-permute-done | bytes 262176 | tf_op jit(solution)/shard_map/key_weights_far_z_1/ppermute | solution.py:37
  179.0 3.6 %collective-permute-done.48.refs_4_ = bf16[512,512]{1,0:T(8,128)(2,1)S(1)} collective-permute-done((bf16[512,512]{1,0:T(8,128)(2,1)S(1)}, bf16[512,512]{1,0:T(8,128)(2,1)S(1)}, u32[]{:S(2)}, u32[]{:S(2)}) %collective-permute-start.48) | collective-permute-done | bytes 524320 | tf_op jit(solution)/shard_map/key_weights_z_1/ppermute | solution.py:37
  189.0 7.0 %collective-permute-start.50 = (bf16[4,32,1152]{2,1,0:T(8,128)(2,1)S(1)}, bf16[4,32,1152]{2,1,0:T(8,128)(2,1)S(1)}, u32[]{:S(2)}, u32[]{:S(2)}) collective-permute-start(bf16[4,32,1152]{2,1,0:T(8,128)(2,1)S(1)} %get-tuple-element.142), channel_id=1, source_target_pairs={{0,1},{1,0},{2,3},{3,2},{4,5},{5,4},{6,7},{7,6},{8,9},{9,8},{10,11... | collective-permute-start | bytes 884744 | tf_op jit(solution)/shard_map/final_core/ppermute | solution.py:42
  197.8 7.2 %place_rows.1 = (bf16[2048,512]{1,0:T(8,128)(2,1)}, bf16[2048,512]{1,0:T(8,128)(2,1)}) custom-call(bf16[2048,512]{1,0:T(8,128)(2,1)} %bitcast.44, bf16[2048,512]{1,0:T(8,128)(2,1)} %bitcast.45, s32[2,1,128]{2,1,0:T(1,128)S(1)} %copy-done.9, bf16[4,32,1024]{2,1,0:T(8,128)(2,1)S(1)} %get-tuple-element.141.refs_3_, ...), custom_call_target="tpu_custom_call" | custom-call | flops 1 | bytes 1 | tf_op jit(solution)/shard_map/place_rows/pallas_call | solution.py:78
  (138 shorter events, 96.3 us)
Async XLA Ops:
  21.2 15.3 %collective-permute-start.5 = (bf16[32,8320]{1,0:T(8,128)(2,1)S(1)}, bf16[32,8320]{1,0:T(8,128)(2,1)S(1)}, u32[]{:S(2)}, u32[]{:S(2)}) collective-permute-start(bf16[32,8320]{1,0:T(8,128)(2,1)S(1)} %get-tuple-element.80.refs_0_), channel_id=1, source_target_pairs={{0,16},{1,65},{2,18},{3,67},{4,20},{5,69},{6,22},{7,71},{8,24},{9,... | collective-permute-start | bytes 1597448 | tf_op jit(solution)/shard_map/rows_first_2/ppermute | solution.py:31
  23.8 12.7 %collective-permute-start.4 = (bf16[32,8320]{1,0:T(8,128)(2,1)S(1)}, bf16[32,8320]{1,0:T(8,128)(2,1)S(1)}, u32[]{:S(2)}, u32[]{:S(2)}) collective-permute-start(bf16[32,8320]{1,0:T(8,128)(2,1)S(1)} %get-tuple-element.80.refs_0_), channel_id=1, source_target_pairs={{0,24},{1,97},{2,26},{3,99},{4,28},{5,101},{6,30},{7,103},{8,0},{9... | collective-permute-start | bytes 1597448 | tf_op jit(solution)/shard_map/rows_first_1/ppermute | solution.py:31
  39.3 12.5 %collective-permute-start.8 = (bf16[64,4224]{1,0:T(8,128)(2,1)S(1)}, bf16[64,4224]{1,0:T(8,128)(2,1)S(1)}, u32[]{:S(2)}, u32[]{:S(2)}) collective-permute-start(bf16[64,4224]{1,0:T(8,128)(2,1)S(1)} %get-tuple-element.83.refs_1_.refs_2_.refs_7_), channel_id=1, source_target_pairs={{0,96},{1,25},{2,98},{3,27},{4,100},{5,29},{6,102},{7,31},{8,104},... | collective-permute-start | bytes 1622024 | tf_op jit(solution)/shard_map/x_2_second_1/ppermute | solution.py:31
  40.3 11.9 %collective-permute-start.12 = (bf16[64,4224]{1,0:T(8,128)(2,1)S(1)}, bf16[64,4224]{1,0:T(8,128)(2,1)S(1)}, u32[]{:S(2)}, u32[]{:S(2)}) collective-permute-start(bf16[64,4224]{1,0:T(8,128)(2,1)S(1)} %get-tuple-element.82.refs_4_.refs_0_.refs_1_.refs_6_), channel_id=1, source_target_pairs={{0,32},{1,9},{2,34},{3,11},{4,36},{5,13},{6,38},{7,15},{8,40},{9,1... | collective-permute-start | bytes 1622024 | tf_op jit(solution)/shard_map/x_2_second_3/ppermute | solution.py:31
  46.3 11.6 %collective-permute-start.11 = (bf16[64,4224]{1,0:T(8,128)(2,1)S(1)}, bf16[64,4224]{1,0:T(8,128)(2,1)S(1)}, u32[]{:S(2)}, u32[]{:S(2)}) collective-permute-start(bf16[64,4224]{1,0:T(8,128)(2,1)S(1)} %collective-permute-done.10.refs_7_.refs_8_.refs_13_), channel_id=1, source_target_pairs={{0,32},{1,9},{2,34},{3,11},{4,36},{5,13},{6,38},{7,15},{8,40},{9,1... | collective-permute-start | bytes 1622024 | tf_op jit(solution)/shard_map/x_far_second_3/ppermute | solution.py:31
  46.3 11.6 %collective-permute-start.9 = (bf16[64,4224]{1,0:T(8,128)(2,1)S(1)}, bf16[64,4224]{1,0:T(8,128)(2,1)S(1)}, u32[]{:S(2)}, u32[]{:S(2)}) collective-permute-start(bf16[64,4224]{1,0:T(8,128)(2,1)S(1)} %collective-permute-done.7.refs_2_.refs_3_.refs_8_), channel_id=1, source_target_pairs={{0,96},{1,25},{2,98},{3,27},{4,100},{5,29},{6,102},{7,31},{8,104},... | collective-permute-start | bytes 1622024 | tf_op jit(solution)/shard_map/x_far_second_1/ppermute | solution.py:31
  52.2 25.8 %collective-permute-start.17 = (bf16[128,4096]{1,0:T(8,128)(2,1)S(1)}, bf16[128,4096]{1,0:T(8,128)(2,1)S(1)}, u32[]{:S(2)}, u32[]{:S(2)}) collective-permute-start(bf16[128,4096]{1,0:T(8,128)(2,1)S(1)} %stack_g.1.refs_11_.refs_0_.refs_9_), channel_id=1, source_target_pairs={{0,32},{1,9},{2,34},{3,11},{4,36},{5,13},{6,38},{7,15},{8,40},{9,1... | collective-permute-start | bytes 3145736 | tf_op jit(solution)/shard_map/g_second_3/ppermute | solution.py:31
  53.2 24.8 %collective-permute-start.16 = (bf16[128,4096]{1,0:T(8,128)(2,1)S(1)}, bf16[128,4096]{1,0:T(8,128)(2,1)S(1)}, u32[]{:S(2)}, u32[]{:S(2)}) collective-permute-start(bf16[128,4096]{1,0:T(8,128)(2,1)S(1)} %stack_g.1.refs_11_.refs_0_.refs_9_), channel_id=1, source_target_pairs={{0,96},{1,25},{2,98},{3,27},{4,100},{5,29},{6,102},{7,31},{8,104},... | collective-permute-start | bytes 3145736 | tf_op jit(solution)/shard_map/g_second_1/ppermute | solution.py:31
  63.2 11.7 %collective-permute-start.14 = (bf16[528,512]{1,0:T(8,128)(2,1)S(1)}, bf16[528,512]{1,0:T(8,128)(2,1)S(1)}, u32[]{:S(2)}, u32[]{:S(2)}) collective-permute-start(bf16[528,512]{1,0:T(8,128)(2,1)S(1)} %get-tuple-element.85.refs_1_), channel_id=1, source_target_pairs={{0,2},{1,3},{2,0},{3,1},{4,6},{5,7},{6,4},{7,5},{8,10},{9,11},{10,... | collective-permute-start | bytes 1622024 | tf_op jit(solution)/shard_map/pair_chip/ppermute | solution.py:47
  64.2 16.8 %collective-permute-start.13 = (bf16[528,512]{1,0:T(8,128)(2,1)S(1)}, bf16[528,512]{1,0:T(8,128)(2,1)S(1)}, u32[]{:S(2)}, u32[]{:S(2)}) collective-permute-start(bf16[528,512]{1,0:T(8,128)(2,1)S(1)} %get-tuple-element.85.refs_1_), channel_id=1, source_target_pairs={{0,1},{1,0},{2,3},{3,2},{4,5},{5,4},{6,7},{7,6},{8,9},{9,8},{10,11... | collective-permute-start | bytes 1622024 | tf_op jit(solution)/shard_map/pair_core/ppermute | solution.py:42
  78.1 11.8 %collective-permute-start.19 = (bf16[64,4096]{1,0:T(8,128)(2,1)S(1)}, bf16[64,4096]{1,0:T(8,128)(2,1)S(1)}, u32[]{:S(2)}, u32[]{:S(2)}) collective-permute-start(bf16[64,4096]{1,0:T(8,128)(2,1)S(1)} %get-tuple-element.89), channel_id=1, source_target_pairs={{0,32},{1,9},{2,34},{3,11},{4,36},{5,13},{6,38},{7,15},{8,40},{9,1... | collective-permute-start | bytes 1572872 | tf_op jit(solution)/shard_map/g_far_second_3/ppermute | solution.py:31
  97.7 18.4 %collective-permute-start.23 = (bf16[512,512]{1,0:T(8,128)(2,1)S(1)}, bf16[512,512]{1,0:T(8,128)(2,1)S(1)}, u32[]{:S(2)}, u32[]{:S(2)}) collective-permute-start(bf16[512,512]{1,0:T(8,128)(2,1)S(1)} %chip_sum.1.refs_8_), channel_id=1, source_target_pairs={{0,2},{1,3},{2,0},{3,1},{4,6},{5,7},{6,4},{7,5},{8,10},{9,11},{10,... | collective-permute-start | bytes 1572872 | tf_op jit(solution)/shard_map/key_grads_chip/ppermute | solution.py:47
  101.3 11.5 %collective-permute-start.21 = (bf16[256,512]{1,0:T(8,128)(2,1)S(1)}, bf16[256,512]{1,0:T(8,128)(2,1)S(1)}, u32[]{:S(2)}, u32[]{:S(2)}) collective-permute-start(bf16[256,512]{1,0:T(8,128)(2,1)S(1)} %get-tuple-element.96), channel_id=1, source_target_pairs={{0,1},{1,0},{2,3},{3,2},{4,5},{5,4},{6,7},{7,6},{8,9},{9,8},{10,11... | collective-permute-start | bytes 786440 | tf_op jit(solution)/shard_map/key_near_core/ppermute | solution.py:42
  101.4 13.6 %collective-permute-start.22 = (bf16[256,512]{1,0:T(8,128)(2,1)S(1)}, bf16[256,512]{1,0:T(8,128)(2,1)S(1)}, u32[]{:S(2)}, u32[]{:S(2)}) collective-permute-start(bf16[256,512]{1,0:T(8,128)(2,1)S(1)} %get-tuple-element.97), channel_id=1, source_target_pairs={{0,1},{1,0},{2,3},{3,2},{4,5},{5,4},{6,7},{7,6},{8,9},{9,8},{10,11... | collective-permute-start | bytes 786440 | tf_op jit(solution)/shard_map/key_near_core/ppermute | solution.py:42
  107.3 19.4 %collective-permute-start.29 = (bf16[128,4096]{1,0:T(8,128)(2,1)S(1)}, bf16[128,4096]{1,0:T(8,128)(2,1)S(1)}, u32[]{:S(2)}, u32[]{:S(2)}) collective-permute-start(bf16[128,4096]{1,0:T(8,128)(2,1)S(1)} %get-tuple-element.102.refs_16_), channel_id=1, source_target_pairs={{0,32},{1,9},{2,34},{3,11},{4,36},{5,13},{6,38},{7,15},{8,40},{9,1... | collective-permute-start | bytes 3145736 | tf_op jit(solution)/shard_map/out_second_3/ppermute | solution.py:31
  112.8 13.9 %collective-permute-start.30 = (bf16[128,4096]{1,0:T(8,128)(2,1)S(1)}, bf16[128,4096]{1,0:T(8,128)(2,1)S(1)}, u32[]{:S(2)}, u32[]{:S(2)}) collective-permute-start(bf16[128,4096]{1,0:T(8,128)(2,1)S(1)} %get-tuple-element.111), channel_id=1, source_target_pairs={{0,96},{1,25},{2,98},{3,27},{4,100},{5,29},{6,102},{7,31},{8,104},... | collective-permute-start | bytes 3145736 | tf_op jit(solution)/shard_map/out_second_1/ppermute | solution.py:31
  115.0 20.9 %collective-permute-start.33 = (bf16[3,512,512]{2,1,0:T(8,128)(2,1)S(1)}, bf16[3,512,512]{2,1,0:T(8,128)(2,1)S(1)}, u32[]{:S(2)}, u32[]{:S(2)}) collective-permute-start(bf16[3,512,512]{2,1,0:T(8,128)(2,1)S(1)} %get-tuple-element.116), channel_id=1, source_target_pairs={{0,1},{1,0},{2,3},{3,2},{4,5},{5,4},{6,7},{7,6},{8,9},{9,8},{10,11... | collective-permute-start | bytes 4718600 | tf_op jit(solution)/shard_map/query_weights_core/ppermute | solution.py:42
  132.7 15.3 %collective-permute-start.32 = (bf16[128,4224]{1,0:T(8,128)(2,1)S(1)}, bf16[128,4224]{1,0:T(8,128)(2,1)S(1)}, u32[]{:S(2)}, u32[]{:S(2)}) collective-permute-start(bf16[128,4224]{1,0:T(8,128)(2,1)S(1)} %get-tuple-element.114), channel_id=1, source_target_pairs={{0,96},{1,25},{2,98},{3,27},{4,100},{5,29},{6,102},{7,31},{8,104},... | collective-permute-start | bytes 3244040 | tf_op jit(solution)/shard_map/grad_second_1/ppermute | solution.py:31
  135.9 15.5 %collective-permute-start.31 = (bf16[128,4224]{1,0:T(8,128)(2,1)S(1)}, bf16[128,4224]{1,0:T(8,128)(2,1)S(1)}, u32[]{:S(2)}, u32[]{:S(2)}) collective-permute-start(bf16[128,4224]{1,0:T(8,128)(2,1)S(1)} %get-tuple-element.113.refs_4_), channel_id=1, source_target_pairs={{0,32},{1,9},{2,34},{3,11},{4,36},{5,13},{6,38},{7,15},{8,40},{9,1... | collective-permute-start | bytes 3244040 | tf_op jit(solution)/shard_map/grad_second_3/ppermute | solution.py:31
  136.1 19.1 %collective-permute-start.39 = (bf16[512,512]{1,0:T(8,128)(2,1)S(1)}, bf16[512,512]{1,0:T(8,128)(2,1)S(1)}, u32[]{:S(2)}, u32[]{:S(2)}) collective-permute-start(bf16[512,512]{1,0:T(8,128)(2,1)S(1)} %get-tuple-element.126), channel_id=1, source_target_pairs={{0,2},{1,3},{2,4},{3,5},{4,6},{5,7},{6,0},{7,1},{8,10},{9,11},{10,... | collective-permute-start | bytes 1572872 | tf_op jit(solution)/shard_map/query_weights_z_1/ppermute | solution.py:37
  137.1 18.1 %collective-permute-start.40 = (bf16[512,512]{1,0:T(8,128)(2,1)S(1)}, bf16[512,512]{1,0:T(8,128)(2,1)S(1)}, u32[]{:S(2)}, u32[]{:S(2)}) collective-permute-start(bf16[512,512]{1,0:T(8,128)(2,1)S(1)} %get-tuple-element.127), channel_id=1, source_target_pairs={{0,6},{1,7},{2,0},{3,1},{4,2},{5,3},{6,4},{7,5},{8,14},{9,15},{10,... | collective-permute-start | bytes 1572872 | tf_op jit(solution)/shard_map/query_weights_z_3/ppermute | solution.py:37
  143.4 11.8 %collective-permute-start.38 = (bf16[4,512,512]{2,1,0:T(8,128)(2,1)S(1)}, bf16[4,512,512]{2,1,0:T(8,128)(2,1)S(1)}, u32[]{:S(2)}, u32[]{:S(2)}) collective-permute-start(bf16[4,512,512]{2,1,0:T(8,128)(2,1)S(1)} %get-tuple-element.125), channel_id=1, source_target_pairs={{0,1},{1,0},{2,3},{3,2},{4,5},{5,4},{6,7},{7,6},{8,9},{9,8},{10,11... | collective-permute-start | bytes 6291464 | tf_op jit(solution)/shard_map/key_weights_core/ppermute | solution.py:42
  161.8 13.4 %collective-permute-start.42 = (bf16[32,8320]{1,0:T(8,128)(2,1)S(1)}, bf16[32,8320]{1,0:T(8,128)(2,1)S(1)}, u32[]{:S(2)}, u32[]{:S(2)}) collective-permute-start(bf16[32,8320]{1,0:T(8,128)(2,1)S(1)} %get-tuple-element.130), channel_id=1, source_target_pairs={{0,24},{1,97},{2,26},{3,99},{4,28},{5,101},{6,30},{7,103},{8,0},{9... | collective-permute-start | bytes 1597448 | tf_op jit(solution)/shard_map/sum_first_1/ppermute | solution.py:31
  162.1 13.0 %collective-permute-start.41 = (bf16[32,8320]{1,0:T(8,128)(2,1)S(1)}, bf16[32,8320]{1,0:T(8,128)(2,1)S(1)}, u32[]{:S(2)}, u32[]{:S(2)}) collective-permute-start(bf16[32,8320]{1,0:T(8,128)(2,1)S(1)} %get-tuple-element.129.refs_3_), channel_id=1, source_target_pairs={{0,8},{1,33},{2,10},{3,35},{4,12},{5,37},{6,14},{7,39},{8,16},{9,4... | collective-permute-start | bytes 1597448 | tf_op jit(solution)/shard_map/sum_first_3/ppermute | solution.py:31
  (38 other events, 344.1 us)

commit v5 on v4

--- a/solution.py
+++ b/solution.py
@@ -64,7 +64,7 @@
 
 
 ORDER = []
-COSTS = {"out_add": 20, "feature_parts": 30, "sum_column": 30, "query_weights_near": 20, "stack_g": 20, "halves_g": 5, "final_rows": 20}
+COSTS = {"out_add": 20, "feature_parts": 30, "sum_column": 30, "query_weights_near": 20, "stack_g": 20, "halves_g": 5}
 
 
 def call(kernel, name, out_shape, room=8, after=(), cost=0, **options):
@@ -494,9 +494,9 @@
     return total
 
 
-def backward_far_kernel(q, kv2, kv3, probs, grad, att, total, mid, sent):
+def backward_far_kernel(q, kv2, kv3, probs, grad, att, total, mid, sent_a, sent_b):
     for h in range(2):
-        part = backward_part(h, 2, (kv2, kv3), q, probs, grad, att, ((mid,), (sent,)))
+        part = backward_part(h, 2, (kv2, kv3), q, probs, grad, att, ((mid,), (sent_a, sent_b)))
         total[:, h * 128 : h * 128 + 128] = part
 
 
@@ -512,10 +512,10 @@
     return call(
         backward_far_kernel,
         "attention_backward_far",
-        [shape(512, 256, dtype=F32), shape(512, 512), shape(512, 512)],
+        [shape(512, 256, dtype=F32), shape(512, 512), shape(256, 512), shape(256, 512)],
         room=16,
         in_specs=[WHOLE] * 6,
-        out_specs=[WHOLE] * 3,
+        out_specs=[WHOLE] * 4,
     )(q, *pieces[2:], probs, grad, att)
 
 
@@ -530,8 +530,9 @@
     )(q, *pieces[:2], probs, grad, att, table, total)
 
 
-def chip_sum_kernel(mid, recv, out):
-    out[...] = mid[...] + recv[...]
+def chip_sum_kernel(mid, recv_a, recv_b, out):
+    out[:256] = mid[:256] + recv_a[...]
+    out[256:] = mid[256:] + recv_b[...]
 
 
 def chip_sum(mid, recv):
@@ -539,9 +540,9 @@
         chip_sum_kernel,
         "chip_sum",
         shape(512, 512),
-        in_specs=[WHOLE] * 2,
+        in_specs=[WHOLE] * 3,
         out_specs=WHOLE,
-    )(mid, recv)
+    )(mid, *recv)
 
 
 def feature_kernel(near, recv_a, recv_b, chip, gq, table, *refs):
@@ -823,8 +824,31 @@
     hot = (token == index[0]).astype(F32).astype(BF)
     own = rows[pl.ds(pl.multiple_of(slab * 128, 128), 128), :]
     added = jnp.dot(hot, own, preferred_element_type=F32)
-    out_h[...] = (hidden[...].astype(F32) + added[:, :512]).astype(BF)
-    out_g[...] = (grads[...].astype(F32) + added[:, 512:]).astype(BF)
+    at = tile(step, 256)
+    out_h[...] = (hidden[at, :].astype(F32) + added[:, :512]).astype(BF)
+    out_g[...] = (grads[at, :].astype(F32) + added[:, 512:]).astype(BF)
+
+
+def fetch_kernel(hidden, grads, out_h, out_g, semaphores):
+    copies = [
+        pltpu.make_async_copy(hidden, out_h, semaphores.at[0]),
+        pltpu.make_async_copy(grads, out_g, semaphores.at[1]),
+    ]
+    for copy in copies:
+        copy.start()
+    for copy in copies:
+        copy.wait()
+
+
+def fetch_bases(hidden, grads):
+    return call(
+        fetch_kernel,
+        "fetch_bases",
+        [pltpu.VMEM((2048, 512), BF)] * 2,
+        in_specs=[ANY, ANY],
+        out_specs=[WHOLE] * 2,
+        scratch_shapes=[pltpu.SemaphoreType.DMA((2,))],
+    )(hidden, grads)
 
 
 def place_rows(where, hidden, grads, index, mine, other):
@@ -834,7 +858,7 @@
         "place_rows",
         [pltpu.HBM((2048, 512), BF)] * 2,
         grid=(8,),
-        in_specs=[block, block, pl.BlockSpec((1, 1, 128), lambda i: (i // 4, 0, 0)), WHOLE, WHOLE, SMEM],
+        in_specs=[WHOLE, WHOLE, pl.BlockSpec((1, 1, 128), lambda i: (i // 4, 0, 0)), WHOLE, WHOLE, SMEM],
         out_specs=[block] * 2,
         scratch_shapes=[pltpu.VMEM((256, 1024), BF)],
     )(hidden, grads, index, mine, other, where)
@@ -875,8 +899,9 @@
 
     out_state = reduce_start(output_parts(attended, w_back), "out")
     grad_attended = attended_grad(g, w_back)
-    total, mid, sent = attend_back_far(queries, pieces, probs, grad_attended, attended)
-    chip_part = swap_chip(chip_sum(mid, swap_core(sent, "key_far")), "key_grads")
+    total, mid, *sent = attend_back_far(queries, pieces, probs, grad_attended, attended)
+    recv = [swap_core(part, "key_far") for part in sent]
+    chip_part = swap_chip(chip_sum(mid, recv), "key_grads")
     grad_q, near, *sent = attend_back_near(
         queries, pieces, probs, grad_attended, attended, table, total
     )
@@ -891,22 +916,18 @@
     terms_a = sum_near(state_a, "query_weights")
     kept_b, sent_b = key_weights(where, x, gp_kv)
     recv_b = swap_core(sent_b, "key_weights")
+    bases = fetch_bases(
+        from_hbm(hidden_in.reshape(2048, 512)), from_hbm(cotangent.reshape(2048, 512))
+    )
     column = reduce_column(grad_terms, out_terms)
     state_b = sum_all(kept_b, recv_b, "key_weights", terms_a[1:])
     column = reduce_rows(column)
+    final = final_rows(where, *column, rows_own, gain)
     terms_b = sum_near(state_b, "key_weights")
-    final = final_rows(where, *column, rows_own, gain)
+    mine, other, gain_part = other_columns(where, final)
+
+    hidden_out, grad_in = place_rows(where, *bases, route_index, mine, other)
     grad_w_qkv, grad_w_out = sum_weights(terms_a, terms_b)
-    mine, other, gain_part = other_columns(where, final)
-
-    hidden_out, grad_in = place_rows(
-        where,
-        from_hbm(hidden_in.reshape(2048, 512)),
-        from_hbm(cotangent.reshape(2048, 512)),
-        route_index,
-        mine,
-        other,
-    )
     grad_gain = gain_part + other[0, :, 1024:].astype(F32) + other[1, :, 1024:].astype(F32)
     return (
         hidden_out.reshape(2, 1024, 512),

time: 205 us -> 197 us (0.961)
  waiting for transfers between devices: 67.8 us -> 57.7 us
    ppermute x14, waiting for transfers between devices: 18.8 us -> 5.2 us  [send_z(): return lax.ppermute(values, 'cmp', pairs)]
    ppermute x10 -> x11, waiting for transfers between devices: 1.25 us -> 3.75 us  [swap_core(): return lax.ppermute(values, 'cmp', [(k, k ^ 1) for k in range(8)])]
    ppermute x10 -> x11, starting transfers between devices: 20.3 us -> 21.3 us  [swap_core(): return lax.ppermute(values, 'cmp', [(k, k ^ 1) for k in range(8)])]
    unnamed x22 -> x20, local copies, waits for them, and re-layouts: 4.45 us -> 5.08 us
    pallas_call x29 -> x30, Pallas kernels: 55.3 us -> 55.4 us  [invoke(): pl.pallas_call(body, out_shape=out_shape, compiler_params=pltpu.CompilerP...]
  transfers between devices with their start and end apart: 51 -> 52, of which waited for: 25 -> 21; matrix products, arithmetic and copies ran while one was open for 1% -> 0% of each run, Pallas kernels for 19% -> 25%
where the time goes in v5:
time: 197 us
  starting transfers between devices  75.6 us (38%)
  waiting for transfers between devices  57.7 us (29%)
  Pallas kernels  55.4 us (28%)
  local copies, waits for them, and re-layouts  6.25 us (3%)
    pallas_call x30, Pallas kernels, invoke(): pl.pallas_call(body, out_shape=out_shape, compiler_params=pltpu.CompilerP...  55.4 us
    ppermute x25, waiting for transfers between devices, ring(): return lax.ppermute(values, BOTH, ring_pairs(second, shift))  40.5 us
    ppermute x25, starting transfers between devices, ring(): return lax.ppermute(values, BOTH, ring_pairs(second, shift))  33 us
    ppermute x11, starting transfers between devices, swap_core(): return lax.ppermute(values, 'cmp', [(k, k ^ 1) for k in range(8)])  21.3 us
    ppermute x14, starting transfers between devices, send_z(): return lax.ppermute(values, 'cmp', pairs)  19.2 us
    ppermute x2, waiting for transfers between devices, swap_chip(): return lax.ppermute(values, 'cmp', [(k, k ^ 2) for k in range(8)])  8.17 us
    ppermute x14, waiting for transfers between devices, send_z(): return lax.ppermute(values, 'cmp', pairs)  5.2 us
    unnamed x20, local copies, waits for them, and re-layouts  5.08 us
  transfers between devices with their start and end apart: 52, of which 21 were waited for; matrix products, arithmetic and copies ran while one was open for 0% of the time, Pallas kernels for 25%

profile of v5, /device:TPU:1, one launch (start us, length us, event | category | flops | bytes accessed | tf_op | source)
XLA Modules:
  0.0 196.7 jit_solution(7359938926571677680)
XLA Ops:
  6.7 3.3 %collective-permute-start.1 = (bf16[2,2,32,512]{3,2,1,0:T(8,128)(2,1)S(1)}, bf16[2,2,32,512]{3,2,1,0:T(8,128)(2,1)S(1)}, u32[]{:S(2)}, u32[]{:S(2)}) collective-permute-start(bf16[2,2,32,512]{3,2,1,0:T(8,128)(2,1)S(1)} %get-tuple-element.81), channel_id=1, source_target_pairs={{0,4},{1,5},{2,6},{3,7},{4,0},{5,1},{6,2},{7,3},{8,12},{9,13},{10,... | collective-permute-start | bytes 393224 | tf_op jit(solution)/shard_map/rows_z_2/ppermute | solution.py:37
  12.0 3.7 %collective-permute-done.1.refs_3_ = bf16[2,2,32,512]{3,2,1,0:T(8,128)(2,1)S(1)} collective-permute-done((bf16[2,2,32,512]{3,2,1,0:T(8,128)(2,1)S(1)}, bf16[2,2,32,512]{3,2,1,0:T(8,128)(2,1)S(1)}, u32[]{:S(2)}, u32[]{:S(2)}) %collective-permute-start.1) | collective-permute-done | bytes 131104 | tf_op jit(solution)/shard_map/rows_z_2/ppermute | solution.py:37
  24.9 2.8 %copy-done.1 = bf16[4096,2,3,128]{3,1,2,0:T(2,128)(2,1)S(1)} copy-done((bf16[4096,2,3,128]{3,1,2,0:T(2,128)(2,1)S(1)}, bf16[4096,2,3,128]{3,1,2,0:T(2,128)(2,1)}, u32[]{:S(2)}) %copy-start.1) | copy-done | bytes 6291480
  30.0 6.5 %collective-permute-done.5.refs_2_ = bf16[32,8320]{1,0:T(8,128)(2,1)S(1)} collective-permute-done((bf16[32,8320]{1,0:T(8,128)(2,1)S(1)}, bf16[32,8320]{1,0:T(8,128)(2,1)S(1)}, u32[]{:S(2)}, u32[]{:S(2)}) %collective-permute-start.5) | collective-permute-done | bytes 532512 | tf_op jit(solution)/shard_map/rows_first_2/ppermute | solution.py:31
  40.8 5.6 %collective-permute-done.10.refs_7_.refs_8_.refs_13_ = bf16[64,4224]{1,0:T(8,128)(2,1)S(1)} collective-permute-done((bf16[64,4224]{1,0:T(8,128)(2,1)S(1)}, bf16[64,4224]{1,0:T(8,128)(2,1)S(1)}, u32[]{:S(2)}, u32[]{:S(2)}) %collective-permute-start.10) | collective-permute-done | bytes 540704 | tf_op jit(solution)/shard_map/x_1_second_3/ppermute | solution.py:31
  49.0 2.8 %collective-permute-done.8.refs_5_.refs_3_.refs_4_.refs_9_ = bf16[64,4224]{1,0:T(8,128)(2,1)S(1)} collective-permute-done((bf16[64,4224]{1,0:T(8,128)(2,1)S(1)}, bf16[64,4224]{1,0:T(8,128)(2,1)S(1)}, u32[]{:S(2)}, u32[]{:S(2)}) %collective-permute-start.8) | collective-permute-done | bytes 540704 | tf_op jit(solution)/shard_map/x_2_second_1/ppermute | solution.py:31
  55.0 2.9 %collective-permute-done.11.refs_5_.refs_6_.refs_11_ = bf16[64,4224]{1,0:T(8,128)(2,1)S(1)} collective-permute-done((bf16[64,4224]{1,0:T(8,128)(2,1)S(1)}, bf16[64,4224]{1,0:T(8,128)(2,1)S(1)}, u32[]{:S(2)}, u32[]{:S(2)}) %collective-permute-start.11) | collective-permute-done | bytes 540704 | tf_op jit(solution)/shard_map/x_far_second_3/ppermute | solution.py:31
  57.9 5.3 %project.1 = (bf16[512,256]{1,0:T(8,128)(2,1)S(1)}, bf16[528,512]{1,0:T(8,128)(2,1)S(1)}, f32[512,384]{1,0:T(8,128)S(1)}) custom-call(bf16[64,4224]{1,0:T(8,128)(2,1)S(1)} %get-tuple-element.85.refs_4_.refs_0_.refs_1_.refs_6_, bf16[64,4224]{1,0:T(8,128)(2,1)S(1)} %get-tuple-element.86.refs_1_.refs_2_.refs_7_, ...), custom_call_target="tpu_custom_call" | custom-call | flops 1 | bytes 1 | tf_op jit(solution)/shard_map/project/pallas_call | solution.py:78
  66.7 8.2 %collective-permute-done.14.refs_3_.refs_1_ = bf16[528,512]{1,0:T(8,128)(2,1)S(1)} collective-permute-done((bf16[528,512]{1,0:T(8,128)(2,1)S(1)}, bf16[528,512]{1,0:T(8,128)(2,1)S(1)}, u32[]{:S(2)}, u32[]{:S(2)}) %collective-permute-start.14) | collective-permute-done | bytes 540704 | tf_op jit(solution)/shard_map/pair_chip/ppermute | solution.py:47
  74.9 3.1 %collective-permute-start.15 = (bf16[528,512]{1,0:T(8,128)(2,1)S(1)}, bf16[528,512]{1,0:T(8,128)(2,1)S(1)}, u32[]{:S(2)}, u32[]{:S(2)}) collective-permute-start(bf16[528,512]{1,0:T(8,128)(2,1)S(1)} %collective-permute-done.14.refs_3_.refs_1_), channel_id=1, source_target_pairs={{0,1},{1,0},{2,3},{3,2},{4,5},{5,4},{6,7},{7,6},{8,9},{9,8},{10,11... | collective-permute-start | bytes 1622024 | tf_op jit(solution)/shard_map/far_pair_core/ppermute | solution.py:42
  81.1 6.4 %attention_forward.1 = (bf16[512,256]{1,0:T(8,128)(2,1)S(1)}, bf16[2,512,2048]{2,1,0:T(8,128)(2,1)S(1)}) custom-call(bf16[512,256]{1,0:T(8,128)(2,1)S(1)} %get-tuple-element.87.refs_2_.refs_0_, bf16[528,512]{1,0:T(8,128)(2,1)S(1)} %get-tuple-element.88.refs_1_, bf16[528,512]{1,0:T(8,128)(2,1)S(1)} %collective-permute-done.13.refs_2_, ...), custom_call_target="tpu_custom_call" | custom-call | flops 1 | bytes 1 | tf_op jit(solution)/shard_map/attention_forward/pallas_call | solution.py:78
  104.3 4.8 %query_weights.1 = (bf16[4,512,512]{2,1,0:T(8,128)(2,1)S(1)}, bf16[512,512]{1,0:T(8,128)(2,1)S(1)}, bf16[3,512,512]{2,1,0:T(8,128)(2,1)S(1)}) custom-call(s32[2]{0:T(128)S(1)} %pad_add_fusion.refs_0_.refs_5_, bf16[64,4224]{1,0:T(8,128)(2,1)S(1)} %get-tuple-element.85.refs_4_.refs_0_.refs_1_.refs_6_, ...), custom_call_target="tpu_custom_call" | custom-call | flops 1 | bytes 1 | tf_op jit(solution)/shard_map/query_weights/pallas_call | solution.py:78
  112.0 6.2 %feature_parts.1 = (bf16[512,768]{1,0:T(8,128)(2,1)}, bf16[512,512]{1,0:T(8,128)(2,1)S(1)}, bf16[128,4224]{1,0:T(8,128)(2,1)S(1)}, bf16[128,4224]{1,0:T(8,128)(2...) custom-call(bf16[512,512]{1,0:T(8,128)(2,1)S(1)} %get-tuple-element.99.refs_0_, ...), custom_call_target="tpu_custom_call" | custom-call | flops 30000001024 | bytes 1 | tf_op jit(solution)/shard_map/feature_parts/pallas_call | solution.py:78
  124.7 3.1 %collective-permute-done.33.refs_1_ = bf16[64,4224]{1,0:T(8,128)(2,1)S(1)} collective-permute-done((bf16[64,4224]{1,0:T(8,128)(2,1)S(1)}, bf16[64,4224]{1,0:T(8,128)(2,1)S(1)}, u32[]{:S(2)}, u32[]{:S(2)}) %collective-permute-start.33) | collective-permute-done | bytes 540704 | tf_op jit(solution)/shard_map/grad_second_3/ppermute | solution.py:31
  129.1 3.2 %collective-permute-start.36 = (bf16[128,4224]{1,0:T(8,128)(2,1)S(1)}, bf16[128,4224]{1,0:T(8,128)(2,1)S(1)}, u32[]{:S(2)}, u32[]{:S(2)}) collective-permute-start(bf16[128,4224]{1,0:T(8,128)(2,1)S(1)} %get-tuple-element.124), channel_id=1, source_target_pairs={{0,96},{1,25},{2,98},{3,27},{4,100},{5,29},{6,102},{7,31},{8,104},... | collective-permute-start | bytes 3244040 | tf_op jit(solution)/shard_map/grad_second_1/ppermute | solution.py:31
  135.3 4.5 %key_weights.1 = (bf16[4,512,512]{2,1,0:T(8,128)(2,1)S(1)}, bf16[4,512,512]{2,1,0:T(8,128)(2,1)S(1)}) custom-call(s32[2]{0:T(128)S(1)} %pad_add_fusion.refs_0_.refs_5_, bf16[64,4224]{1,0:T(8,128)(2,1)S(1)} %get-tuple-element.85.refs_4_.refs_0_.refs_1_.refs_6_, bf16[64,4224]{1,0:T(8,128)(2,1)S(1)} %get-tuple-element.86.refs_1_.refs_2_.refs_7_, ...), custom_call_target="tpu_custom_call" | custom-call | flops 1 | bytes 1 | tf_op jit(solution)/shard_map/key_weights/pallas_call | solution.py:78
  139.9 2.8 %collective-permute-start.39 = (bf16[4,512,512]{2,1,0:T(8,128)(2,1)S(1)}, bf16[4,512,512]{2,1,0:T(8,128)(2,1)S(1)}, u32[]{:S(2)}, u32[]{:S(2)}) collective-permute-start(bf16[4,512,512]{2,1,0:T(8,128)(2,1)S(1)} %get-tuple-element.131), channel_id=1, source_target_pairs={{0,1},{1,0},{2,3},{3,2},{4,5},{5,4},{6,7},{7,6},{8,9},{9,8},{10,11... | collective-permute-start | bytes 6291464 | tf_op jit(solution)/shard_map/key_weights_core/ppermute | solution.py:42
  144.9 3.0 %collective-permute-done.35.refs_1_ = bf16[128,4224]{1,0:T(8,128)(2,1)S(1)} collective-permute-done((bf16[128,4224]{1,0:T(8,128)(2,1)S(1)}, bf16[128,4224]{1,0:T(8,128)(2,1)S(1)}, u32[]{:S(2)}, u32[]{:S(2)}) %collective-permute-start.35) | collective-permute-done | bytes 1081376 | tf_op jit(solution)/shard_map/grad_second_3/ppermute | solution.py:31
  148.6 3.1 %collective-permute-start.38 = (bf16[16,8320]{1,0:T(8,128)(2,1)S(1)}, bf16[16,8320]{1,0:T(8,128)(2,1)S(1)}, u32[]{:S(2)}, u32[]{:S(2)}) collective-permute-start(bf16[16,8320]{1,0:T(8,128)(2,1)S(1)} %get-tuple-element.130), channel_id=1, source_target_pairs={{0,24},{1,97},{2,26},{3,99},{4,28},{5,101},{6,30},{7,103},{8,0},{9... | collective-permute-start | bytes 798728 | tf_op jit(solution)/shard_map/sum_far_first_1/ppermute | solution.py:31
  152.0 3.1 %collective-permute-done.38.refs_3_ = bf16[16,8320]{1,0:T(8,128)(2,1)S(1)} collective-permute-done((bf16[16,8320]{1,0:T(8,128)(2,1)S(1)}, bf16[16,8320]{1,0:T(8,128)(2,1)S(1)}, u32[]{:S(2)}, u32[]{:S(2)}) %collective-permute-start.38) | collective-permute-done | bytes 266272 | tf_op jit(solution)/shard_map/sum_far_first_1/ppermute | solution.py:31
  155.1 3.1 %collective-permute-done.37.refs_1_ = bf16[16,8320]{1,0:T(8,128)(2,1)S(1)} collective-permute-done((bf16[16,8320]{1,0:T(8,128)(2,1)S(1)}, bf16[16,8320]{1,0:T(8,128)(2,1)S(1)}, u32[]{:S(2)}, u32[]{:S(2)}) %collective-permute-start.37) | collective-permute-done | bytes 266272 | tf_op jit(solution)/shard_map/sum_far_first_3/ppermute | solution.py:31
  161.5 5.3 %collective-permute-done.43.refs_3_ = bf16[32,8320]{1,0:T(8,128)(2,1)S(1)} collective-permute-done((bf16[32,8320]{1,0:T(8,128)(2,1)S(1)}, bf16[32,8320]{1,0:T(8,128)(2,1)S(1)}, u32[]{:S(2)}, u32[]{:S(2)}) %collective-permute-start.43) | collective-permute-done | bytes 532512 | tf_op jit(solution)/shard_map/sum_first_1/ppermute | solution.py:31
  177.3 8.7 %collective-permute-start.49 = (bf16[4,32,1152]{2,1,0:T(8,128)(2,1)S(1)}, bf16[4,32,1152]{2,1,0:T(8,128)(2,1)S(1)}, u32[]{:S(2)}, u32[]{:S(2)}) collective-permute-start(bf16[4,32,1152]{2,1,0:T(8,128)(2,1)S(1)} %get-tuple-element.145), channel_id=1, source_target_pairs={{0,1},{1,0},{2,3},{3,2},{4,5},{5,4},{6,7},{7,6},{8,9},{9,8},{10,11... | collective-permute-start | bytes 884744 | tf_op jit(solution)/shard_map/final_core/ppermute | solution.py:42
  187.3 5.0 %place_rows.1 = (bf16[2048,512]{1,0:T(8,128)(2,1)}, bf16[2048,512]{1,0:T(8,128)(2,1)}) custom-call(bf16[2048,512]{1,0:T(8,128)(2,1)S(1)} %get-tuple-element.121.refs_6_.refs_0_, bf16[2048,512]{1,0:T(8,128)(2,1)S(1)} %get-tuple-element.122.refs_1_, s32[2,1,128]{2,1,0:T(1,128)S(1)} %copy-done.8, bf16[4,32,1024]{2,1,0:T(8,128)(2,1)S(1)} %get-tuple-element.144.refs_3_, ...), custom_call_target="tpu_custom_call" | custom-call | flops 1 | bytes 1 | tf_op jit(solution)/shard_map/place_rows/pallas_call | solution.py:78
  (139 shorter events, 89.4 us)
Async XLA Ops:
  21.2 15.3 %collective-permute-start.5 = (bf16[32,8320]{1,0:T(8,128)(2,1)S(1)}, bf16[32,8320]{1,0:T(8,128)(2,1)S(1)}, u32[]{:S(2)}, u32[]{:S(2)}) collective-permute-start(bf16[32,8320]{1,0:T(8,128)(2,1)S(1)} %get-tuple-element.83.refs_0_), channel_id=1, source_target_pairs={{0,16},{1,65},{2,18},{3,67},{4,20},{5,69},{6,22},{7,71},{8,24},{9,... | collective-permute-start | bytes 1597448 | tf_op jit(solution)/shard_map/rows_first_2/ppermute | solution.py:31
  23.8 12.7 %collective-permute-start.4 = (bf16[32,8320]{1,0:T(8,128)(2,1)S(1)}, bf16[32,8320]{1,0:T(8,128)(2,1)S(1)}, u32[]{:S(2)}, u32[]{:S(2)}) collective-permute-start(bf16[32,8320]{1,0:T(8,128)(2,1)S(1)} %get-tuple-element.83.refs_0_), channel_id=1, source_target_pairs={{0,24},{1,97},{2,26},{3,99},{4,28},{5,101},{6,30},{7,103},{8,0},{9... | collective-permute-start | bytes 1597448 | tf_op jit(solution)/shard_map/rows_first_1/ppermute | solution.py:31
  39.3 12.5 %collective-permute-start.8 = (bf16[64,4224]{1,0:T(8,128)(2,1)S(1)}, bf16[64,4224]{1,0:T(8,128)(2,1)S(1)}, u32[]{:S(2)}, u32[]{:S(2)}) collective-permute-start(bf16[64,4224]{1,0:T(8,128)(2,1)S(1)} %get-tuple-element.86.refs_1_.refs_2_.refs_7_), channel_id=1, source_target_pairs={{0,96},{1,25},{2,98},{3,27},{4,100},{5,29},{6,102},{7,31},{8,104},... | collective-permute-start | bytes 1622024 | tf_op jit(solution)/shard_map/x_2_second_1/ppermute | solution.py:31
  40.3 11.9 %collective-permute-start.12 = (bf16[64,4224]{1,0:T(8,128)(2,1)S(1)}, bf16[64,4224]{1,0:T(8,128)(2,1)S(1)}, u32[]{:S(2)}, u32[]{:S(2)}) collective-permute-start(bf16[64,4224]{1,0:T(8,128)(2,1)S(1)} %get-tuple-element.85.refs_4_.refs_0_.refs_1_.refs_6_), channel_id=1, source_target_pairs={{0,32},{1,9},{2,34},{3,11},{4,36},{5,13},{6,38},{7,15},{8,40},{9,1... | collective-permute-start | bytes 1622024 | tf_op jit(solution)/shard_map/x_2_second_3/ppermute | solution.py:31
  52.2 25.8 %collective-permute-start.17 = (bf16[128,4096]{1,0:T(8,128)(2,1)S(1)}, bf16[128,4096]{1,0:T(8,128)(2,1)S(1)}, u32[]{:S(2)}, u32[]{:S(2)}) collective-permute-start(bf16[128,4096]{1,0:T(8,128)(2,1)S(1)} %stack_g.1.refs_11_.refs_0_.refs_9_), channel_id=1, source_target_pairs={{0,32},{1,9},{2,34},{3,11},{4,36},{5,13},{6,38},{7,15},{8,40},{9,1... | collective-permute-start | bytes 3145736 | tf_op jit(solution)/shard_map/g_second_3/ppermute | solution.py:31
  53.2 24.8 %collective-permute-start.16 = (bf16[128,4096]{1,0:T(8,128)(2,1)S(1)}, bf16[128,4096]{1,0:T(8,128)(2,1)S(1)}, u32[]{:S(2)}, u32[]{:S(2)}) collective-permute-start(bf16[128,4096]{1,0:T(8,128)(2,1)S(1)} %stack_g.1.refs_11_.refs_0_.refs_9_), channel_id=1, source_target_pairs={{0,96},{1,25},{2,98},{3,27},{4,100},{5,29},{6,102},{7,31},{8,104},... | collective-permute-start | bytes 3145736 | tf_op jit(solution)/shard_map/g_second_1/ppermute | solution.py:31
  64.2 16.8 %collective-permute-start.13 = (bf16[528,512]{1,0:T(8,128)(2,1)S(1)}, bf16[528,512]{1,0:T(8,128)(2,1)S(1)}, u32[]{:S(2)}, u32[]{:S(2)}) collective-permute-start(bf16[528,512]{1,0:T(8,128)(2,1)S(1)} %get-tuple-element.88.refs_1_), channel_id=1, source_target_pairs={{0,1},{1,0},{2,3},{3,2},{4,5},{5,4},{6,7},{7,6},{8,9},{9,8},{10,11... | collective-permute-start | bytes 1622024 | tf_op jit(solution)/shard_map/pair_core/ppermute | solution.py:42
  78.1 13.3 %collective-permute-start.19 = (bf16[64,4096]{1,0:T(8,128)(2,1)S(1)}, bf16[64,4096]{1,0:T(8,128)(2,1)S(1)}, u32[]{:S(2)}, u32[]{:S(2)}) collective-permute-start(bf16[64,4096]{1,0:T(8,128)(2,1)S(1)} %get-tuple-element.92), channel_id=1, source_target_pairs={{0,32},{1,9},{2,34},{3,11},{4,36},{5,13},{6,38},{7,15},{8,40},{9,1... | collective-permute-start | bytes 1572872 | tf_op jit(solution)/shard_map/g_far_second_3/ppermute | solution.py:31
  79.0 12.4 %collective-permute-start.18 = (bf16[64,4096]{1,0:T(8,128)(2,1)S(1)}, bf16[64,4096]{1,0:T(8,128)(2,1)S(1)}, u32[]{:S(2)}, u32[]{:S(2)}) collective-permute-start(bf16[64,4096]{1,0:T(8,128)(2,1)S(1)} %get-tuple-element.90.refs_6_), channel_id=1, source_target_pairs={{0,96},{1,25},{2,98},{3,27},{4,100},{5,29},{6,102},{7,31},{8,104},... | collective-permute-start | bytes 1572872 | tf_op jit(solution)/shard_map/g_far_second_1/ppermute | solution.py:31
  89.9 13.2 %collective-permute-start.26 = (bf16[64,4096]{1,0:T(8,128)(2,1)S(1)}, bf16[64,4096]{1,0:T(8,128)(2,1)S(1)}, u32[]{:S(2)}, u32[]{:S(2)}) collective-permute-start(bf16[64,4096]{1,0:T(8,128)(2,1)S(1)} %get-tuple-element.105), channel_id=1, source_target_pairs={{0,96},{1,25},{2,98},{3,27},{4,100},{5,29},{6,102},{7,31},{8,104},... | collective-permute-start | bytes 1572872 | tf_op jit(solution)/shard_map/out_second_1/ppermute | solution.py:31
  91.2 12.0 %collective-permute-start.25 = (bf16[64,4096]{1,0:T(8,128)(2,1)S(1)}, bf16[64,4096]{1,0:T(8,128)(2,1)S(1)}, u32[]{:S(2)}, u32[]{:S(2)}) collective-permute-start(bf16[64,4096]{1,0:T(8,128)(2,1)S(1)} %get-tuple-element.94.refs_6_), channel_id=1, source_target_pairs={{0,32},{1,9},{2,34},{3,11},{4,36},{5,13},{6,38},{7,15},{8,40},{9,1... | collective-permute-start | bytes 1572872 | tf_op jit(solution)/shard_map/out_second_3/ppermute | solution.py:31
  98.6 13.3 %collective-permute-start.24 = (bf16[512,512]{1,0:T(8,128)(2,1)S(1)}, bf16[512,512]{1,0:T(8,128)(2,1)S(1)}, u32[]{:S(2)}, u32[]{:S(2)}) collective-permute-start(bf16[512,512]{1,0:T(8,128)(2,1)S(1)} %chip_sum.1.refs_8_), channel_id=1, source_target_pairs={{0,2},{1,3},{2,0},{3,1},{4,6},{5,7},{6,4},{7,5},{8,10},{9,11},{10,... | collective-permute-start | bytes 1572872 | tf_op jit(solution)/shard_map/key_grads_chip/ppermute | solution.py:47
  103.3 19.9 %collective-permute-start.29 = (bf16[128,4096]{1,0:T(8,128)(2,1)S(1)}, bf16[128,4096]{1,0:T(8,128)(2,1)S(1)}, u32[]{:S(2)}, u32[]{:S(2)}) collective-permute-start(bf16[128,4096]{1,0:T(8,128)(2,1)S(1)} %get-tuple-element.106.refs_16_), channel_id=1, source_target_pairs={{0,32},{1,9},{2,34},{3,11},{4,36},{5,13},{6,38},{7,15},{8,40},{9,1... | collective-permute-start | bytes 3145736 | tf_op jit(solution)/shard_map/out_second_3/ppermute | solution.py:31
  109.1 14.0 %collective-permute-start.30 = (bf16[128,4096]{1,0:T(8,128)(2,1)S(1)}, bf16[128,4096]{1,0:T(8,128)(2,1)S(1)}, u32[]{:S(2)}, u32[]{:S(2)}) collective-permute-start(bf16[128,4096]{1,0:T(8,128)(2,1)S(1)} %get-tuple-element.111), channel_id=1, source_target_pairs={{0,96},{1,25},{2,98},{3,27},{4,100},{5,29},{6,102},{7,31},{8,104},... | collective-permute-start | bytes 3145736 | tf_op jit(solution)/shard_map/out_second_1/ppermute | solution.py:31
  111.3 21.0 %collective-permute-start.27 = (bf16[3,512,512]{2,1,0:T(8,128)(2,1)S(1)}, bf16[3,512,512]{2,1,0:T(8,128)(2,1)S(1)}, u32[]{:S(2)}, u32[]{:S(2)}) collective-permute-start(bf16[3,512,512]{2,1,0:T(8,128)(2,1)S(1)} %get-tuple-element.110), channel_id=1, source_target_pairs={{0,1},{1,0},{2,3},{3,2},{4,5},{5,4},{6,7},{7,6},{8,9},{9,8},{10,11... | collective-permute-start | bytes 4718600 | tf_op jit(solution)/shard_map/query_weights_core/ppermute | solution.py:42
  129.1 15.8 %collective-permute-start.36 = (bf16[128,4224]{1,0:T(8,128)(2,1)S(1)}, bf16[128,4224]{1,0:T(8,128)(2,1)S(1)}, u32[]{:S(2)}, u32[]{:S(2)}) collective-permute-start(bf16[128,4224]{1,0:T(8,128)(2,1)S(1)} %get-tuple-element.124), channel_id=1, source_target_pairs={{0,96},{1,25},{2,98},{3,27},{4,100},{5,29},{6,102},{7,31},{8,104},... | collective-permute-start | bytes 3244040 | tf_op jit(solution)/shard_map/grad_second_1/ppermute | solution.py:31
  132.4 15.5 %collective-permute-start.35 = (bf16[128,4224]{1,0:T(8,128)(2,1)S(1)}, bf16[128,4224]{1,0:T(8,128)(2,1)S(1)}, u32[]{:S(2)}, u32[]{:S(2)}) collective-permute-start(bf16[128,4224]{1,0:T(8,128)(2,1)S(1)} %get-tuple-element.118.refs_4_), channel_id=1, source_target_pairs={{0,32},{1,9},{2,34},{3,11},{4,36},{5,13},{6,38},{7,15},{8,40},{9,1... | collective-permute-start | bytes 3244040 | tf_op jit(solution)/shard_map/grad_second_3/ppermute | solution.py:31
  132.6 19.2 %collective-permute-start.40 = (bf16[512,512]{1,0:T(8,128)(2,1)S(1)}, bf16[512,512]{1,0:T(8,128)(2,1)S(1)}, u32[]{:S(2)}, u32[]{:S(2)}) collective-permute-start(bf16[512,512]{1,0:T(8,128)(2,1)S(1)} %get-tuple-element.132), channel_id=1, source_target_pairs={{0,2},{1,3},{2,4},{3,5},{4,6},{5,7},{6,0},{7,1},{8,10},{9,11},{10,... | collective-permute-start | bytes 1572872 | tf_op jit(solution)/shard_map/query_weights_z_1/ppermute | solution.py:37
  133.3 18.4 %collective-permute-start.41 = (bf16[512,512]{1,0:T(8,128)(2,1)S(1)}, bf16[512,512]{1,0:T(8,128)(2,1)S(1)}, u32[]{:S(2)}, u32[]{:S(2)}) collective-permute-start(bf16[512,512]{1,0:T(8,128)(2,1)S(1)} %get-tuple-element.133), channel_id=1, source_target_pairs={{0,6},{1,7},{2,0},{3,1},{4,2},{5,3},{6,4},{7,5},{8,14},{9,15},{10,... | collective-permute-start | bytes 1572872 | tf_op jit(solution)/shard_map/query_weights_z_3/ppermute | solution.py:37
  139.9 11.9 %collective-permute-start.39 = (bf16[4,512,512]{2,1,0:T(8,128)(2,1)S(1)}, bf16[4,512,512]{2,1,0:T(8,128)(2,1)S(1)}, u32[]{:S(2)}, u32[]{:S(2)}) collective-permute-start(bf16[4,512,512]{2,1,0:T(8,128)(2,1)S(1)} %get-tuple-element.131), channel_id=1, source_target_pairs={{0,1},{1,0},{2,3},{3,2},{4,5},{5,4},{6,7},{7,6},{8,9},{9,8},{10,11... | collective-permute-start | bytes 6291464 | tf_op jit(solution)/shard_map/key_weights_core/ppermute | solution.py:42
  159.9 13.6 %collective-permute-start.48 = (bf16[256,512]{1,0:T(8,128)(2,1)S(1)}, bf16[256,512]{1,0:T(8,128)(2,1)S(1)}, u32[]{:S(2)}, u32[]{:S(2)}) collective-permute-start(bf16[256,512]{1,0:T(8,128)(2,1)S(1)} %get-tuple-element.142), channel_id=1, source_target_pairs={{0,6},{1,7},{2,0},{3,1},{4,2},{5,3},{6,4},{7,5},{8,14},{9,15},{10,... | collective-permute-start | bytes 786440 | tf_op jit(solution)/shard_map/key_weights_far_z_3/ppermute | solution.py:37
  161.5 12.0 %collective-permute-start.47 = (bf16[256,512]{1,0:T(8,128)(2,1)S(1)}, bf16[256,512]{1,0:T(8,128)(2,1)S(1)}, u32[]{:S(2)}, u32[]{:S(2)}) collective-permute-start(bf16[256,512]{1,0:T(8,128)(2,1)S(1)} %get-tuple-element.134.refs_4_), channel_id=1, source_target_pairs={{0,2},{1,3},{2,4},{3,5},{4,6},{5,7},{6,0},{7,1},{8,10},{9,11},{10,... | collective-permute-start | bytes 786440 | tf_op jit(solution)/shard_map/key_weights_far_z_1/ppermute | solution.py:37
  173.6 19.2 %collective-permute-start.50 = (bf16[512,512]{1,0:T(8,128)(2,1)S(1)}, bf16[512,512]{1,0:T(8,128)(2,1)S(1)}, u32[]{:S(2)}, u32[]{:S(2)}) collective-permute-start(bf16[512,512]{1,0:T(8,128)(2,1)S(1)} %get-tuple-element.149), channel_id=1, source_target_pairs={{0,2},{1,3},{2,4},{3,5},{4,6},{5,7},{6,0},{7,1},{8,10},{9,11},{10,... | collective-permute-start | bytes 1572872 | tf_op jit(solution)/shard_map/key_weights_z_1/ppermute | solution.py:37
  173.8 19.0 %collective-permute-start.51 = (bf16[512,512]{1,0:T(8,128)(2,1)S(1)}, bf16[512,512]{1,0:T(8,128)(2,1)S(1)}, u32[]{:S(2)}, u32[]{:S(2)}) collective-permute-start(bf16[512,512]{1,0:T(8,128)(2,1)S(1)} %get-tuple-element.150), channel_id=1, source_target_pairs={{0,6},{1,7},{2,0},{3,1},{4,2},{5,3},{6,4},{7,5},{8,14},{9,15},{10,... | collective-permute-start | bytes 1572872 | tf_op jit(solution)/shard_map/key_weights_z_3/ppermute | solution.py:37
  (38 other events, 328.6 us)

commit v6 on v5

--- a/solution.py
+++ b/solution.py
@@ -430,54 +430,105 @@
     )(*g, w)
 
 
-def forward_kernel(q, kv0, kv1, kv2, kv3, table, out, probs):
-    factor = 128 ** (-0.5) * 1.4426950408889634
-    key_places = [kv[512:513, :].astype(F32) + kv[513:514, :].astype(F32) for kv in (kv0, kv1, kv2, kv3)]
-
+EXP2 = 128 ** (-0.5) * 1.4426950408889634
+
+
+def masked_scores(q, kvs, table, rows, h):
+    query = q[rows, h * 128 : h * 128 + 128]
+    place = table[rows, 256:257]
+    scores = []
+    for kv in kvs:
+        s = lax.dot_general(query, kv[:512, h * 256 : h * 256 + 128], LAST, preferred_element_type=F32)
+        key_place = kv[512:513, :].astype(F32) + kv[513:514, :].astype(F32)
+        scores.append(jnp.where(place >= key_place, s, -jnp.inf))
+    return scores, jnp.max(jnp.maximum(scores[0], scores[1]), -1, keepdims=True)
+
+
+def weighted(ps, kvs, h):
+    parts = [
+        jnp.dot(p, kv[:512, h * 256 + 128 : h * 256 + 256], preferred_element_type=F32)
+        for p, kv in zip(ps, kvs)
+    ]
+    return parts[0] + parts[1]
+
+
+def forward_near_kernel(q, kv0, kv1, table, probs, sums, tops, totals):
     @pl.loop(0, 4)
     def _(step):
         rows = tile(step, 128)
-        place = table[rows, 256:257]
         for h in range(2):
-            query = q[rows, h * 128 : h * 128 + 128]
-            scores = []
-            for i, kv in enumerate((kv0, kv1, kv2, kv3)):
-                key = kv[:512, h * 256 : h * 256 + 128]
-                s = lax.dot_general(query, key, LAST, preferred_element_type=F32)
-                scores.append(jnp.where(place >= key_places[i], s, -jnp.inf))
-            top = jnp.maximum(jnp.maximum(scores[0], scores[1]), jnp.maximum(scores[2], scores[3]))
-            top = jnp.max(top, -1, keepdims=True)
-            exps = [jnp.exp2((s - top) * factor) for s in scores]
-            inverse = 1.0 / jnp.sum((exps[0] + exps[1]) + (exps[2] + exps[3]), -1, keepdims=True)
-            total = None
-            for i, kv in enumerate((kv0, kv1, kv2, kv3)):
-                p = (exps[i] * inverse).astype(BF)
-                probs[h, rows, i * 512 : (i + 1) * 512] = p
-                value = kv[:512, h * 256 + 128 : h * 256 + 256]
-                part = jnp.dot(p, value, preferred_element_type=F32)
-                total = part if total is None else total + part
-            out[rows, h * 128 : h * 128 + 128] = total.astype(BF)
-
-
-def attend(q, pieces, table):
-    return call(
-        forward_kernel,
-        "attention_forward",
-        [shape(512, 256), shape(2, 512, 2048)],
+            head = slice(h * 128, h * 128 + 128)
+            scores, top = masked_scores(q, (kv0, kv1), table, rows, h)
+            exps = [jnp.exp2((s - top) * EXP2) for s in scores]
+            total = jnp.sum(exps[0] + exps[1], -1, keepdims=True)
+            low = [e.astype(BF) for e in exps]
+            for i in range(2):
+                probs[h, rows, i * 512 : (i + 1) * 512] = low[i]
+            sums[rows, head] = weighted(low, (kv0, kv1), h)
+            tops[rows, head] = jnp.broadcast_to(top, (128, 128))
+            totals[rows, head] = jnp.broadcast_to(total, (128, 128))
+
+
+def forward_far_kernel(q, kv2, kv3, table, sums, tops, totals, out, probs, factors):
+    @pl.loop(0, 4)
+    def _(step):
+        rows = tile(step, 128)
+        for h in range(2):
+            head = slice(h * 128, h * 128 + 128)
+            scores, top = masked_scores(q, (kv2, kv3), table, rows, h)
+            near_top = tops[rows, head]
+            top = jnp.maximum(near_top, top)
+            exps = [jnp.exp2((s - top[:, :1]) * EXP2) for s in scores]
+            fade = jnp.exp2((near_top - top) * EXP2)
+            inverse = 1.0 / (totals[rows, head] * fade + jnp.sum(exps[0] + exps[1], -1, keepdims=True))
+            low = [(e * inverse[:, :1]).astype(BF) for e in exps]
+            for i in range(2):
+                probs[h, rows, i * 512 : (i + 1) * 512] = low[i]
+            factor = fade * inverse
+            factors[rows, head] = factor
+            out[rows, head] = (sums[rows, head] * factor + weighted(low, (kv2, kv3), h)).astype(BF)
+
+
+def attend_near(q, pieces, table):
+    return call(
+        forward_near_kernel,
+        "attention_near",
+        [shape(2, 512, 1024)] + [shape(512, 256, dtype=F32)] * 3,
         room=16,
-        in_specs=[WHOLE] * 6,
-        out_specs=[WHOLE] * 2,
+        in_specs=[WHOLE] * 4,
+        out_specs=[WHOLE] * 4,
     )(q, *pieces, table)
 
 
-def backward_part(h, first, kvs, q, probs, grad, att, outs):
+def attend_far(q, pieces, table, sums, tops, totals):
+    return call(
+        forward_far_kernel,
+        "attention_far",
+        [shape(512, 256), shape(2, 512, 1024), shape(512, 256, dtype=F32)],
+        room=16,
+        in_specs=[WHOLE] * 7,
+        out_specs=[WHOLE] * 3,
+    )(q, *pieces, table, sums, tops, totals)
+
+
+def relay_kernel(x, out):
+    out[...] = x[...]
+
+
+def relay(x):
+    return call(relay_kernel, "relay", shape(*x.shape), in_specs=[WHOLE], out_specs=WHOLE)(x)
+
+
+def backward_part(h, factor, kvs, q, probs, grad, att, outs):
     scale = 128 ** (-0.5)
     head = slice(h * 128, h * 128 + 128)
     g = grad[:, head]
     delta = jnp.sum(g.astype(F32) * att[:, head].astype(F32), -1, keepdims=True)
     total = None
     for i, (kv, out) in enumerate(zip(kvs, outs)):
-        p = probs[h, :, (first + i) * 512 : (first + i + 1) * 512]
+        p = probs[h, :, i * 512 : (i + 1) * 512]
+        if factor is not None:
+            p = (p.astype(F32) * factor).astype(BF)
         key, value = kv[:512, h * 256 : h * 256 + 128], kv[:512, h * 256 + 128 : h * 256 + 256]
         dp = lax.dot_general(g, value, LAST, preferred_element_type=F32)
         ds = (p.astype(F32) * (dp - delta)).astype(BF)
@@ -496,14 +547,15 @@
 
 def backward_far_kernel(q, kv2, kv3, probs, grad, att, total, mid, sent_a, sent_b):
     for h in range(2):
-        part = backward_part(h, 2, (kv2, kv3), q, probs, grad, att, ((mid,), (sent_a, sent_b)))
+        part = backward_part(h, None, (kv2, kv3), q, probs, grad, att, ((mid,), (sent_a, sent_b)))
         total[:, h * 128 : h * 128 + 128] = part
 
 
-def backward_near_kernel(q, kv0, kv1, probs, grad, att, table, total, gq, near, sent_a, sent_b):
+def backward_near_kernel(q, kv0, kv1, probs, factors, grad, att, table, total, gq, near, sent_a, sent_b):
     for h in range(2):
         head = slice(h * 128, h * 128 + 128)
-        part = backward_part(h, 0, (kv0, kv1), q, probs, grad, att, ((near,), (sent_a, sent_b)))
+        outs = ((near,), (sent_a, sent_b))
+        part = backward_part(h, factors[:, head][:, :1], (kv0, kv1), q, probs, grad, att, outs)
         u = (part + total[:, head]) * 128 ** (-0.5)
         gq[:, head] = (u * table[:, :128] - pltpu.roll(u, 64, 1) * table[:, 128:256]).astype(BF)
 
@@ -519,15 +571,15 @@
     )(q, *pieces[2:], probs, grad, att)
 
 
-def attend_back_near(q, pieces, probs, grad, att, table, total):
+def attend_back_near(q, pieces, probs, factors, grad, att, table, total):
     return call(
         backward_near_kernel,
         "attention_backward_near",
         [shape(512, 256), shape(512, 512), shape(256, 512), shape(256, 512)],
         room=16,
-        in_specs=[WHOLE] * 8,
+        in_specs=[WHOLE] * 9,
         out_specs=[WHOLE] * 4,
-    )(q, *pieces[:2], probs, grad, att, table, total)
+    )(q, *pieces[:2], probs, factors, grad, att, table, total)
 
 
 def chip_sum_kernel(mid, recv_a, recv_b, out):
@@ -892,18 +944,20 @@
     queries, own_pair, table = project(x, w_in)
     chip_pair = swap_chip(own_pair, "pair")
     core_pair = swap_core(own_pair, "pair")
-    far_pair = swap_core(chip_pair, "far_pair")
-    pieces = [own_pair, core_pair, chip_pair, far_pair]
+    pieces = [own_pair, core_pair]
+    probs_near, *near_state = attend_near(queries, pieces, table)
+    chip_pair = relay(chip_pair)
+    pieces += [chip_pair, swap_core(chip_pair, "far_pair")]
     g = gather_g_far(*g_near)
-    attended, probs = attend(queries, pieces, table)
+    attended, probs_far, factors = attend_far(queries, pieces[2:], table, *near_state)
 
     out_state = reduce_start(output_parts(attended, w_back), "out")
     grad_attended = attended_grad(g, w_back)
-    total, mid, *sent = attend_back_far(queries, pieces, probs, grad_attended, attended)
+    total, mid, *sent = attend_back_far(queries, pieces, probs_far, grad_attended, attended)
     recv = [swap_core(part, "key_far") for part in sent]
     chip_part = swap_chip(chip_sum(mid, recv), "key_grads")
     grad_q, near, *sent = attend_back_near(
-        queries, pieces, probs, grad_attended, attended, table, total
+        queries, pieces, probs_near, factors, grad_attended, attended, table, total
     )
     recv = [swap_core(part, "key_near") for part in sent]
     out_terms = reduce_add(out_state, "out")

time: 197 us -> 199 us (1.010)
  Pallas kernels: 55.4 us -> 58.6 us
    pallas_call x30 -> x32, Pallas kernels: 55.4 us -> 58.6 us  [invoke(): pl.pallas_call(body, out_shape=out_shape, compiler_params=pltpu.CompilerP...]
  transfers between devices with their start and end apart: 52 -> 52, of which waited for: 21 -> 22; matrix products, arithmetic and copies ran while one was open for 0% -> 0% of each run, Pallas kernels for 25% -> 27%
where the time goes in v6:
time: 199 us; the launch traced here: 198 us
  starting transfers between devices  74.3 us (37%)
  Pallas kernels  58.6 us (29%)
  waiting for transfers between devices  57.4 us (29%)
  local copies, waits for them, and re-layouts  6.25 us (3%)
    pallas_call x32, Pallas kernels, invoke(): pl.pallas_call(body, out_shape=out_shape, compiler_params=pltpu.CompilerP...  58.6 us
    ppermute x25, waiting for transfers between devices, ring(): return lax.ppermute(values, BOTH, ring_pairs(second, shift))  39.4 us
    ppermute x25, starting transfers between devices, ring(): return lax.ppermute(values, BOTH, ring_pairs(second, shift))  31.9 us
    ppermute x11, starting transfers between devices, swap_core(): return lax.ppermute(values, 'cmp', [(k, k ^ 1) for k in range(8)])  21.1 us
    ppermute x14, starting transfers between devices, send_z(): return lax.ppermute(values, 'cmp', pairs)  19.3 us
    ppermute x2, waiting for transfers between devices, swap_chip(): return lax.ppermute(values, 'cmp', [(k, k ^ 2) for k in range(8)])  8.68 us
    unnamed x20, local copies, waits for them, and re-layouts  5.08 us
    ppermute x14, waiting for transfers between devices, send_z(): return lax.ppermute(values, 'cmp', pairs)  4.95 us
  transfers between devices with their start and end apart: 52, of which 22 were waited for; matrix products, arithmetic and copies ran while one was open for 0% of the time, Pallas kernels for 27%

profile of v6, /device:TPU:1, one launch (start us, length us, event | category | flops | bytes accessed | tf_op | source)
XLA Modules:
  0.0 198.3 jit_solution(6073768843252415632)
XLA Ops:
  1.4 2.7 %pick_rows.1 = (bf16[2,2,32,512]{3,2,1,0:T(8,128)(2,1)S(1)}, bf16[2,2,32,512]{3,2,1,0:T(8,128)(2,1)S(1)}, bf16[2,2,32,512]{3,2,1,0:T(8,128)(2,1)S(1)}, bf16[2,2,32,512]{3,2,1,0:T(8,128)(2,1)S(1)}) custom-call(s32[2]{0:T(128)S(1)} %pad_add_fusion.refs_0_.refs_5_, s32[2,1,128]{2,1,0:T(1,128)S(1)} %copy-done.7, bf16[2,1024,512]{2,1,0:T(8,128)(2,1)} %refs_2_.2, ...), custom_call_target="tpu_custom_call" | custom-call | flops 1 | bytes 1 | tf_op jit(solution)/shard_map/pick_rows/pallas_call | solution.py:78
  6.7 3.3 %collective-permute-start.1 = (bf16[2,2,32,512]{3,2,1,0:T(8,128)(2,1)S(1)}, bf16[2,2,32,512]{3,2,1,0:T(8,128)(2,1)S(1)}, u32[]{:S(2)}, u32[]{:S(2)}) collective-permute-start(bf16[2,2,32,512]{3,2,1,0:T(8,128)(2,1)S(1)} %get-tuple-element.86), channel_id=1, source_target_pairs={{0,4},{1,5},{2,6},{3,7},{4,0},{5,1},{6,2},{7,3},{8,12},{9,13},{10,... | collective-permute-start | bytes 393224 | tf_op jit(solution)/shard_map/rows_z_2/ppermute | solution.py:37
  12.0 3.7 %collective-permute-done.1.refs_3_ = bf16[2,2,32,512]{3,2,1,0:T(8,128)(2,1)S(1)} collective-permute-done((bf16[2,2,32,512]{3,2,1,0:T(8,128)(2,1)S(1)}, bf16[2,2,32,512]{3,2,1,0:T(8,128)(2,1)S(1)}, u32[]{:S(2)}, u32[]{:S(2)}) %collective-permute-start.1) | collective-permute-done | bytes 131104 | tf_op jit(solution)/shard_map/rows_z_2/ppermute | solution.py:37
  24.9 2.8 %copy-done.1 = bf16[4096,2,3,128]{3,1,2,0:T(2,128)(2,1)S(1)} copy-done((bf16[4096,2,3,128]{3,1,2,0:T(2,128)(2,1)S(1)}, bf16[4096,2,3,128]{3,1,2,0:T(2,128)(2,1)}, u32[]{:S(2)}) %copy-start.1) | copy-done | bytes 6291480
  30.0 6.5 %collective-permute-done.5.refs_2_ = bf16[32,8320]{1,0:T(8,128)(2,1)S(1)} collective-permute-done((bf16[32,8320]{1,0:T(8,128)(2,1)S(1)}, bf16[32,8320]{1,0:T(8,128)(2,1)S(1)}, u32[]{:S(2)}, u32[]{:S(2)}) %collective-permute-start.5) | collective-permute-done | bytes 532512 | tf_op jit(solution)/shard_map/rows_first_2/ppermute | solution.py:31
  40.8 5.6 %collective-permute-done.10.refs_7_.refs_8_.refs_13_ = bf16[64,4224]{1,0:T(8,128)(2,1)S(1)} collective-permute-done((bf16[64,4224]{1,0:T(8,128)(2,1)S(1)}, bf16[64,4224]{1,0:T(8,128)(2,1)S(1)}, u32[]{:S(2)}, u32[]{:S(2)}) %collective-permute-start.10) | collective-permute-done | bytes 540704 | tf_op jit(solution)/shard_map/x_1_second_3/ppermute | solution.py:31
  49.0 2.8 %collective-permute-done.8.refs_5_.refs_3_.refs_4_.refs_9_ = bf16[64,4224]{1,0:T(8,128)(2,1)S(1)} collective-permute-done((bf16[64,4224]{1,0:T(8,128)(2,1)S(1)}, bf16[64,4224]{1,0:T(8,128)(2,1)S(1)}, u32[]{:S(2)}, u32[]{:S(2)}) %collective-permute-start.8) | collective-permute-done | bytes 540704 | tf_op jit(solution)/shard_map/x_2_second_1/ppermute | solution.py:31
  55.0 2.9 %collective-permute-done.11.refs_5_.refs_6_.refs_11_ = bf16[64,4224]{1,0:T(8,128)(2,1)S(1)} collective-permute-done((bf16[64,4224]{1,0:T(8,128)(2,1)S(1)}, bf16[64,4224]{1,0:T(8,128)(2,1)S(1)}, u32[]{:S(2)}, u32[]{:S(2)}) %collective-permute-start.11) | collective-permute-done | bytes 540704 | tf_op jit(solution)/shard_map/x_far_second_3/ppermute | solution.py:31
  57.9 5.3 %project.1 = (bf16[512,256]{1,0:T(8,128)(2,1)S(1)}, bf16[528,512]{1,0:T(8,128)(2,1)S(1)}, f32[512,384]{1,0:T(8,128)S(1)}) custom-call(bf16[64,4224]{1,0:T(8,128)(2,1)S(1)} %get-tuple-element.90.refs_4_.refs_0_.refs_1_.refs_6_, bf16[64,4224]{1,0:T(8,128)(2,1)S(1)} %get-tuple-element.91.refs_1_.refs_2_.refs_7_, ...), custom_call_target="tpu_custom_call" | custom-call | flops 1 | bytes 1 | tf_op jit(solution)/shard_map/project/pallas_call | solution.py:78
  67.1 3.6 %attention_near.1 = (bf16[2,512,1024]{2,1,0:T(8,128)(2,1)S(1)}, f32[512,256]{1,0:T(8,128)S(1)}, f32[512,256]{1,0:T(8,128)S(1)}, f32[512,256]{1,0:T(8,128)S(1)}) custom-call(bf16[512,256]{1,0:T(8,128)(2,1)S(1)} %get-tuple-element.92.refs_0_.refs_4_, bf16[528,512]{1,0:T(8,128)(2,1)S(1)} %get-tuple-element.93.refs_1_, ...), custom_call_target="tpu_custom_call" | custom-call | flops 1 | bytes 1 | tf_op jit(solution)/shard_map/attention_near/pallas_call | solution.py:78
  70.6 8.7 %collective-permute-done.14.refs_0_ = bf16[528,512]{1,0:T(8,128)(2,1)S(1)} collective-permute-done((bf16[528,512]{1,0:T(8,128)(2,1)S(1)}, bf16[528,512]{1,0:T(8,128)(2,1)S(1)}, u32[]{:S(2)}, u32[]{:S(2)}) %collective-permute-start.14) | collective-permute-done | bytes 540704 | tf_op jit(solution)/shard_map/pair_chip/ppermute | solution.py:47
  83.1 5.4 %attention_far.1 = (bf16[512,256]{1,0:T(8,128)(2,1)S(1)}, bf16[2,512,1024]{2,1,0:T(8,128)(2,1)S(1)}, f32[512,256]{1,0:T(8,128)S(1)}) custom-call(bf16[512,256]{1,0:T(8,128)(2,1)S(1)} %get-tuple-element.92.refs_0_.refs_4_, bf16[528,512]{1,0:T(8,128)(2,1)S(1)} %relay.1.refs_2_.refs_1_, bf16[528,512]{1,0:T(8,128)(2,1)S(1)} %collective-permute-done.15.refs_2_, ...), custom_call_target="tpu_custom_call" | custom-call | flops 1 | bytes 1 | tf_op jit(solution)/shard_map/attention_far/pallas_call | solution.py:78
  101.0 3.1 %attention_backward_near.1 = (bf16[512,256]{1,0:T(8,128)(2,1)S(1)}, bf16[512,512]{1,0:T(8,128)(2,1)S(1)}, bf16[256,512]{1,0:T(8,128)(2,1)S(1)}, bf16[256,512]{1,0:T(8,128)(2,1)S(1)}) custom-call(bf16[512,256]{1,0:T(8,128)(2,1)S(1)} %get-tuple-element.92.refs_0_.refs_4_, bf16[528,512]{1,0:T(8,128)(2,1)S(1)} %get-tuple-element.93.refs_1_, ...), custom_call_target="tpu_custom_call" | custom-call | flops 1 | bytes 1 | tf_op jit(solution)/shard_map/attention_backward_near/pallas_call | solution.py:78
  106.8 4.8 %query_weights.1 = (bf16[4,512,512]{2,1,0:T(8,128)(2,1)S(1)}, bf16[512,512]{1,0:T(8,128)(2,1)S(1)}, bf16[3,512,512]{2,1,0:T(8,128)(2,1)S(1)}) custom-call(s32[2]{0:T(128)S(1)} %pad_add_fusion.refs_0_.refs_5_, bf16[64,4224]{1,0:T(8,128)(2,1)S(1)} %get-tuple-element.90.refs_4_.refs_0_.refs_1_.refs_6_, ...), custom_call_target="tpu_custom_call" | custom-call | flops 1 | bytes 1 | tf_op jit(solution)/shard_map/query_weights/pallas_call | solution.py:78
  115.0 6.2 %feature_parts.1 = (bf16[512,768]{1,0:T(8,128)(2,1)}, bf16[512,512]{1,0:T(8,128)(2,1)S(1)}, bf16[128,4224]{1,0:T(8,128)(2,1)S(1)}, bf16[128,4224]{1,0:T(8,128)(2...) custom-call(bf16[512,512]{1,0:T(8,128)(2,1)S(1)} %get-tuple-element.109.refs_0_, ...), custom_call_target="tpu_custom_call" | custom-call | flops 30000001024 | bytes 1 | tf_op jit(solution)/shard_map/feature_parts/pallas_call | solution.py:78
  127.3 3.7 %collective-permute-done.33.refs_1_ = bf16[64,4224]{1,0:T(8,128)(2,1)S(1)} collective-permute-done((bf16[64,4224]{1,0:T(8,128)(2,1)S(1)}, bf16[64,4224]{1,0:T(8,128)(2,1)S(1)}, u32[]{:S(2)}, u32[]{:S(2)}) %collective-permute-start.33) | collective-permute-done | bytes 540704 | tf_op jit(solution)/shard_map/grad_second_3/ppermute | solution.py:31
  137.2 4.5 %key_weights.1 = (bf16[4,512,512]{2,1,0:T(8,128)(2,1)S(1)}, bf16[4,512,512]{2,1,0:T(8,128)(2,1)S(1)}) custom-call(s32[2]{0:T(128)S(1)} %pad_add_fusion.refs_0_.refs_5_, bf16[64,4224]{1,0:T(8,128)(2,1)S(1)} %get-tuple-element.90.refs_4_.refs_0_.refs_1_.refs_6_, bf16[64,4224]{1,0:T(8,128)(2,1)S(1)} %get-tuple-element.91.refs_1_.refs_2_.refs_7_, ...), custom_call_target="tpu_custom_call" | custom-call | flops 1 | bytes 1 | tf_op jit(solution)/shard_map/key_weights/pallas_call | solution.py:78
  141.7 3.5 %collective-permute-start.39 = (bf16[4,512,512]{2,1,0:T(8,128)(2,1)S(1)}, bf16[4,512,512]{2,1,0:T(8,128)(2,1)S(1)}, u32[]{:S(2)}, u32[]{:S(2)}) collective-permute-start(bf16[4,512,512]{2,1,0:T(8,128)(2,1)S(1)} %get-tuple-element.141), channel_id=1, source_target_pairs={{0,1},{1,0},{2,3},{3,2},{4,5},{5,4},{6,7},{7,6},{8,9},{9,8},{10,11... | collective-permute-start | bytes 6291464 | tf_op jit(solution)/shard_map/key_weights_core/ppermute | solution.py:42
  150.6 2.7 %collective-permute-start.38 = (bf16[16,8320]{1,0:T(8,128)(2,1)S(1)}, bf16[16,8320]{1,0:T(8,128)(2,1)S(1)}, u32[]{:S(2)}, u32[]{:S(2)}) collective-permute-start(bf16[16,8320]{1,0:T(8,128)(2,1)S(1)} %get-tuple-element.140), channel_id=1, source_target_pairs={{0,24},{1,97},{2,26},{3,99},{4,28},{5,101},{6,30},{7,103},{8,0},{9... | collective-permute-start | bytes 798728 | tf_op jit(solution)/shard_map/sum_far_first_1/ppermute | solution.py:31
  153.6 3.1 %collective-permute-done.38.refs_3_ = bf16[16,8320]{1,0:T(8,128)(2,1)S(1)} collective-permute-done((bf16[16,8320]{1,0:T(8,128)(2,1)S(1)}, bf16[16,8320]{1,0:T(8,128)(2,1)S(1)}, u32[]{:S(2)}, u32[]{:S(2)}) %collective-permute-start.38) | collective-permute-done | bytes 266272 | tf_op jit(solution)/shard_map/sum_far_first_1/ppermute | solution.py:31
  156.7 3.1 %collective-permute-done.37.refs_1_ = bf16[16,8320]{1,0:T(8,128)(2,1)S(1)} collective-permute-done((bf16[16,8320]{1,0:T(8,128)(2,1)S(1)}, bf16[16,8320]{1,0:T(8,128)(2,1)S(1)}, u32[]{:S(2)}, u32[]{:S(2)}) %collective-permute-start.37) | collective-permute-done | bytes 266272 | tf_op jit(solution)/shard_map/sum_far_first_3/ppermute | solution.py:31
  162.9 5.5 %collective-permute-done.43.refs_3_ = bf16[32,8320]{1,0:T(8,128)(2,1)S(1)} collective-permute-done((bf16[32,8320]{1,0:T(8,128)(2,1)S(1)}, bf16[32,8320]{1,0:T(8,128)(2,1)S(1)}, u32[]{:S(2)}, u32[]{:S(2)}) %collective-permute-start.43) | collective-permute-done | bytes 532512 | tf_op jit(solution)/shard_map/sum_first_1/ppermute | solution.py:31
  178.9 8.8 %collective-permute-start.49 = (bf16[4,32,1152]{2,1,0:T(8,128)(2,1)S(1)}, bf16[4,32,1152]{2,1,0:T(8,128)(2,1)S(1)}, u32[]{:S(2)}, u32[]{:S(2)}) collective-permute-start(bf16[4,32,1152]{2,1,0:T(8,128)(2,1)S(1)} %get-tuple-element.155), channel_id=1, source_target_pairs={{0,1},{1,0},{2,3},{3,2},{4,5},{5,4},{6,7},{7,6},{8,9},{9,8},{10,11... | collective-permute-start | bytes 884744 | tf_op jit(solution)/shard_map/final_core/ppermute | solution.py:42
  188.9 5.0 %place_rows.1 = (bf16[2048,512]{1,0:T(8,128)(2,1)}, bf16[2048,512]{1,0:T(8,128)(2,1)}) custom-call(bf16[2048,512]{1,0:T(8,128)(2,1)S(1)} %get-tuple-element.131.refs_6_.refs_0_, bf16[2048,512]{1,0:T(8,128)(2,1)S(1)} %get-tuple-element.132.refs_1_, s32[2,1,128]{2,1,0:T(1,128)S(1)} %copy-done.8, bf16[4,32,1024]{2,1,0:T(8,128)(2,1)S(1)} %get-tuple-element.154.refs_3_, ...), custom_call_target="tpu_custom_call" | custom-call | flops 1 | bytes 1 | tf_op jit(solution)/shard_map/place_rows/pallas_call | solution.py:78
  (141 shorter events, 90.2 us)
Async XLA Ops:
  21.2 15.3 %collective-permute-start.5 = (bf16[32,8320]{1,0:T(8,128)(2,1)S(1)}, bf16[32,8320]{1,0:T(8,128)(2,1)S(1)}, u32[]{:S(2)}, u32[]{:S(2)}) collective-permute-start(bf16[32,8320]{1,0:T(8,128)(2,1)S(1)} %get-tuple-element.88.refs_0_), channel_id=1, source_target_pairs={{0,16},{1,65},{2,18},{3,67},{4,20},{5,69},{6,22},{7,71},{8,24},{9,... | collective-permute-start | bytes 1597448 | tf_op jit(solution)/shard_map/rows_first_2/ppermute | solution.py:31
  23.8 12.7 %collective-permute-start.4 = (bf16[32,8320]{1,0:T(8,128)(2,1)S(1)}, bf16[32,8320]{1,0:T(8,128)(2,1)S(1)}, u32[]{:S(2)}, u32[]{:S(2)}) collective-permute-start(bf16[32,8320]{1,0:T(8,128)(2,1)S(1)} %get-tuple-element.88.refs_0_), channel_id=1, source_target_pairs={{0,24},{1,97},{2,26},{3,99},{4,28},{5,101},{6,30},{7,103},{8,0},{9... | collective-permute-start | bytes 1597448 | tf_op jit(solution)/shard_map/rows_first_1/ppermute | solution.py:31
  39.3 12.5 %collective-permute-start.8 = (bf16[64,4224]{1,0:T(8,128)(2,1)S(1)}, bf16[64,4224]{1,0:T(8,128)(2,1)S(1)}, u32[]{:S(2)}, u32[]{:S(2)}) collective-permute-start(bf16[64,4224]{1,0:T(8,128)(2,1)S(1)} %get-tuple-element.91.refs_1_.refs_2_.refs_7_), channel_id=1, source_target_pairs={{0,96},{1,25},{2,98},{3,27},{4,100},{5,29},{6,102},{7,31},{8,104},... | collective-permute-start | bytes 1622024 | tf_op jit(solution)/shard_map/x_2_second_1/ppermute | solution.py:31
  40.3 11.9 %collective-permute-start.12 = (bf16[64,4224]{1,0:T(8,128)(2,1)S(1)}, bf16[64,4224]{1,0:T(8,128)(2,1)S(1)}, u32[]{:S(2)}, u32[]{:S(2)}) collective-permute-start(bf16[64,4224]{1,0:T(8,128)(2,1)S(1)} %get-tuple-element.90.refs_4_.refs_0_.refs_1_.refs_6_), channel_id=1, source_target_pairs={{0,32},{1,9},{2,34},{3,11},{4,36},{5,13},{6,38},{7,15},{8,40},{9,1... | collective-permute-start | bytes 1622024 | tf_op jit(solution)/shard_map/x_2_second_3/ppermute | solution.py:31
  46.3 11.6 %collective-permute-start.11 = (bf16[64,4224]{1,0:T(8,128)(2,1)S(1)}, bf16[64,4224]{1,0:T(8,128)(2,1)S(1)}, u32[]{:S(2)}, u32[]{:S(2)}) collective-permute-start(bf16[64,4224]{1,0:T(8,128)(2,1)S(1)} %collective-permute-done.10.refs_7_.refs_8_.refs_13_), channel_id=1, source_target_pairs={{0,32},{1,9},{2,34},{3,11},{4,36},{5,13},{6,38},{7,15},{8,40},{9,1... | collective-permute-start | bytes 1622024 | tf_op jit(solution)/shard_map/x_far_second_3/ppermute | solution.py:31
  52.2 28.1 %collective-permute-start.17 = (bf16[128,4096]{1,0:T(8,128)(2,1)S(1)}, bf16[128,4096]{1,0:T(8,128)(2,1)S(1)}, u32[]{:S(2)}, u32[]{:S(2)}) collective-permute-start(bf16[128,4096]{1,0:T(8,128)(2,1)S(1)} %stack_g.1.refs_11_.refs_0_.refs_9_), channel_id=1, source_target_pairs={{0,32},{1,9},{2,34},{3,11},{4,36},{5,13},{6,38},{7,15},{8,40},{9,1... | collective-permute-start | bytes 3145736 | tf_op jit(solution)/shard_map/g_second_3/ppermute | solution.py:31
  53.2 27.1 %collective-permute-start.16 = (bf16[128,4096]{1,0:T(8,128)(2,1)S(1)}, bf16[128,4096]{1,0:T(8,128)(2,1)S(1)}, u32[]{:S(2)}, u32[]{:S(2)}) collective-permute-start(bf16[128,4096]{1,0:T(8,128)(2,1)S(1)} %stack_g.1.refs_11_.refs_0_.refs_9_), channel_id=1, source_target_pairs={{0,96},{1,25},{2,98},{3,27},{4,100},{5,29},{6,102},{7,31},{8,104},... | collective-permute-start | bytes 3145736 | tf_op jit(solution)/shard_map/g_second_1/ppermute | solution.py:31
  65.5 13.8 %collective-permute-start.14 = (bf16[528,512]{1,0:T(8,128)(2,1)S(1)}, bf16[528,512]{1,0:T(8,128)(2,1)S(1)}, u32[]{:S(2)}, u32[]{:S(2)}) collective-permute-start(bf16[528,512]{1,0:T(8,128)(2,1)S(1)} %get-tuple-element.93.refs_1_), channel_id=1, source_target_pairs={{0,2},{1,3},{2,0},{3,1},{4,6},{5,7},{6,4},{7,5},{8,10},{9,11},{10,... | collective-permute-start | bytes 1622024 | tf_op jit(solution)/shard_map/pair_chip/ppermute | solution.py:47
  80.4 12.1 %collective-permute-start.19 = (bf16[64,4096]{1,0:T(8,128)(2,1)S(1)}, bf16[64,4096]{1,0:T(8,128)(2,1)S(1)}, u32[]{:S(2)}, u32[]{:S(2)}) collective-permute-start(bf16[64,4096]{1,0:T(8,128)(2,1)S(1)} %get-tuple-element.101), channel_id=1, source_target_pairs={{0,32},{1,9},{2,34},{3,11},{4,36},{5,13},{6,38},{7,15},{8,40},{9,1... | collective-permute-start | bytes 1572872 | tf_op jit(solution)/shard_map/g_far_second_3/ppermute | solution.py:31
  90.9 14.0 %collective-permute-start.26 = (bf16[64,4096]{1,0:T(8,128)(2,1)S(1)}, bf16[64,4096]{1,0:T(8,128)(2,1)S(1)}, u32[]{:S(2)}, u32[]{:S(2)}) collective-permute-start(bf16[64,4096]{1,0:T(8,128)(2,1)S(1)} %get-tuple-element.115), channel_id=1, source_target_pairs={{0,96},{1,25},{2,98},{3,27},{4,100},{5,29},{6,102},{7,31},{8,104},... | collective-permute-start | bytes 1572872 | tf_op jit(solution)/shard_map/out_second_1/ppermute | solution.py:31
  92.1 12.9 %collective-permute-start.25 = (bf16[64,4096]{1,0:T(8,128)(2,1)S(1)}, bf16[64,4096]{1,0:T(8,128)(2,1)S(1)}, u32[]{:S(2)}, u32[]{:S(2)}) collective-permute-start(bf16[64,4096]{1,0:T(8,128)(2,1)S(1)} %get-tuple-element.103.refs_6_), channel_id=1, source_target_pairs={{0,32},{1,9},{2,34},{3,11},{4,36},{5,13},{6,38},{7,15},{8,40},{9,1... | collective-permute-start | bytes 1572872 | tf_op jit(solution)/shard_map/out_second_3/ppermute | solution.py:31
  100.0 15.0 %collective-permute-start.24 = (bf16[512,512]{1,0:T(8,128)(2,1)S(1)}, bf16[512,512]{1,0:T(8,128)(2,1)S(1)}, u32[]{:S(2)}, u32[]{:S(2)}) collective-permute-start(bf16[512,512]{1,0:T(8,128)(2,1)S(1)} %chip_sum.1.refs_9_), channel_id=1, source_target_pairs={{0,2},{1,3},{2,0},{3,1},{4,6},{5,7},{6,4},{7,5},{8,10},{9,11},{10,... | collective-permute-start | bytes 1572872 | tf_op jit(solution)/shard_map/key_grads_chip/ppermute | solution.py:47
  105.1 20.6 %collective-permute-start.29 = (bf16[128,4096]{1,0:T(8,128)(2,1)S(1)}, bf16[128,4096]{1,0:T(8,128)(2,1)S(1)}, u32[]{:S(2)}, u32[]{:S(2)}) collective-permute-start(bf16[128,4096]{1,0:T(8,128)(2,1)S(1)} %get-tuple-element.116.refs_16_), channel_id=1, source_target_pairs={{0,32},{1,9},{2,34},{3,11},{4,36},{5,13},{6,38},{7,15},{8,40},{9,1... | collective-permute-start | bytes 3145736 | tf_op jit(solution)/shard_map/out_second_3/ppermute | solution.py:31
  111.7 14.0 %collective-permute-start.30 = (bf16[128,4096]{1,0:T(8,128)(2,1)S(1)}, bf16[128,4096]{1,0:T(8,128)(2,1)S(1)}, u32[]{:S(2)}, u32[]{:S(2)}) collective-permute-start(bf16[128,4096]{1,0:T(8,128)(2,1)S(1)} %get-tuple-element.121), channel_id=1, source_target_pairs={{0,96},{1,25},{2,98},{3,27},{4,100},{5,29},{6,102},{7,31},{8,104},... | collective-permute-start | bytes 3145736 | tf_op jit(solution)/shard_map/out_second_1/ppermute | solution.py:31
  113.3 20.9 %collective-permute-start.27 = (bf16[3,512,512]{2,1,0:T(8,128)(2,1)S(1)}, bf16[3,512,512]{2,1,0:T(8,128)(2,1)S(1)}, u32[]{:S(2)}, u32[]{:S(2)}) collective-permute-start(bf16[3,512,512]{2,1,0:T(8,128)(2,1)S(1)} %get-tuple-element.120), channel_id=1, source_target_pairs={{0,1},{1,0},{2,3},{3,2},{4,5},{5,4},{6,7},{7,6},{8,9},{9,8},{10,11... | collective-permute-start | bytes 4718600 | tf_op jit(solution)/shard_map/query_weights_core/ppermute | solution.py:42
  131.7 15.8 %collective-permute-start.36 = (bf16[128,4224]{1,0:T(8,128)(2,1)S(1)}, bf16[128,4224]{1,0:T(8,128)(2,1)S(1)}, u32[]{:S(2)}, u32[]{:S(2)}) collective-permute-start(bf16[128,4224]{1,0:T(8,128)(2,1)S(1)} %get-tuple-element.134), channel_id=1, source_target_pairs={{0,96},{1,25},{2,98},{3,27},{4,100},{5,29},{6,102},{7,31},{8,104},... | collective-permute-start | bytes 3244040 | tf_op jit(solution)/shard_map/grad_second_1/ppermute | solution.py:31
  134.2 15.5 %collective-permute-start.35 = (bf16[128,4224]{1,0:T(8,128)(2,1)S(1)}, bf16[128,4224]{1,0:T(8,128)(2,1)S(1)}, u32[]{:S(2)}, u32[]{:S(2)}) collective-permute-start(bf16[128,4224]{1,0:T(8,128)(2,1)S(1)} %get-tuple-element.128.refs_4_), channel_id=1, source_target_pairs={{0,32},{1,9},{2,34},{3,11},{4,36},{5,13},{6,38},{7,15},{8,40},{9,1... | collective-permute-start | bytes 3244040 | tf_op jit(solution)/shard_map/grad_second_3/ppermute | solution.py:31
  134.4 18.9 %collective-permute-start.40 = (bf16[512,512]{1,0:T(8,128)(2,1)S(1)}, bf16[512,512]{1,0:T(8,128)(2,1)S(1)}, u32[]{:S(2)}, u32[]{:S(2)}) collective-permute-start(bf16[512,512]{1,0:T(8,128)(2,1)S(1)} %get-tuple-element.142), channel_id=1, source_target_pairs={{0,2},{1,3},{2,4},{3,5},{4,6},{5,7},{6,0},{7,1},{8,10},{9,11},{10,... | collective-permute-start | bytes 1572872 | tf_op jit(solution)/shard_map/query_weights_z_1/ppermute | solution.py:37
  135.0 18.3 %collective-permute-start.41 = (bf16[512,512]{1,0:T(8,128)(2,1)S(1)}, bf16[512,512]{1,0:T(8,128)(2,1)S(1)}, u32[]{:S(2)}, u32[]{:S(2)}) collective-permute-start(bf16[512,512]{1,0:T(8,128)(2,1)S(1)} %get-tuple-element.143), channel_id=1, source_target_pairs={{0,6},{1,7},{2,0},{3,1},{4,2},{5,3},{6,4},{7,5},{8,14},{9,15},{10,... | collective-permute-start | bytes 1572872 | tf_op jit(solution)/shard_map/query_weights_z_3/ppermute | solution.py:37
  141.7 11.6 %collective-permute-start.39 = (bf16[4,512,512]{2,1,0:T(8,128)(2,1)S(1)}, bf16[4,512,512]{2,1,0:T(8,128)(2,1)S(1)}, u32[]{:S(2)}, u32[]{:S(2)}) collective-permute-start(bf16[4,512,512]{2,1,0:T(8,128)(2,1)S(1)} %get-tuple-element.141), channel_id=1, source_target_pairs={{0,1},{1,0},{2,3},{3,2},{4,5},{5,4},{6,7},{7,6},{8,9},{9,8},{10,11... | collective-permute-start | bytes 6291464 | tf_op jit(solution)/shard_map/key_weights_core/ppermute | solution.py:42
  161.4 13.8 %collective-permute-start.48 = (bf16[256,512]{1,0:T(8,128)(2,1)S(1)}, bf16[256,512]{1,0:T(8,128)(2,1)S(1)}, u32[]{:S(2)}, u32[]{:S(2)}) collective-permute-start(bf16[256,512]{1,0:T(8,128)(2,1)S(1)} %get-tuple-element.152), channel_id=1, source_target_pairs={{0,6},{1,7},{2,0},{3,1},{4,2},{5,3},{6,4},{7,5},{8,14},{9,15},{10,... | collective-permute-start | bytes 786440 | tf_op jit(solution)/shard_map/key_weights_far_z_3/ppermute | solution.py:37
  162.7 12.6 %collective-permute-start.47 = (bf16[256,512]{1,0:T(8,128)(2,1)S(1)}, bf16[256,512]{1,0:T(8,128)(2,1)S(1)}, u32[]{:S(2)}, u32[]{:S(2)}) collective-permute-start(bf16[256,512]{1,0:T(8,128)(2,1)S(1)} %get-tuple-element.144.refs_4_), channel_id=1, source_target_pairs={{0,2},{1,3},{2,4},{3,5},{4,6},{5,7},{6,0},{7,1},{8,10},{9,11},{10,... | collective-permute-start | bytes 786440 | tf_op jit(solution)/shard_map/key_weights_far_z_1/ppermute | solution.py:37
  175.4 19.0 %collective-permute-start.50 = (bf16[512,512]{1,0:T(8,128)(2,1)S(1)}, bf16[512,512]{1,0:T(8,128)(2,1)S(1)}, u32[]{:S(2)}, u32[]{:S(2)}) collective-permute-start(bf16[512,512]{1,0:T(8,128)(2,1)S(1)} %get-tuple-element.159), channel_id=1, source_target_pairs={{0,2},{1,3},{2,4},{3,5},{4,6},{5,7},{6,0},{7,1},{8,10},{9,11},{10,... | collective-permute-start | bytes 1572872 | tf_op jit(solution)/shard_map/key_weights_z_1/ppermute | solution.py:37
  175.5 19.0 %collective-permute-start.51 = (bf16[512,512]{1,0:T(8,128)(2,1)S(1)}, bf16[512,512]{1,0:T(8,128)(2,1)S(1)}, u32[]{:S(2)}, u32[]{:S(2)}) collective-permute-start(bf16[512,512]{1,0:T(8,128)(2,1)S(1)} %get-tuple-element.160), channel_id=1, source_target_pairs={{0,6},{1,7},{2,0},{3,1},{4,2},{5,3},{6,4},{7,5},{8,14},{9,15},{10,... | collective-permute-start | bytes 1572872 | tf_op jit(solution)/shard_map/key_weights_z_3/ppermute | solution.py:37
  (38 other events, 312.9 us)

commit v7 on v5

--- a/solution.py
+++ b/solution.py
@@ -927,6 +927,7 @@
     mine, other, gain_part = other_columns(where, final)
 
     hidden_out, grad_in = place_rows(where, *bases, route_index, mine, other)
+    ORDER.pop()
     grad_w_qkv, grad_w_out = sum_weights(terms_a, terms_b)
     grad_gain = gain_part + other[0, :, 1024:].astype(F32) + other[1, :, 1024:].astype(F32)
     return (

time: 197 us -> 195 us (0.990)
    unnamed x20 -> x18, local copies, waits for them, and re-layouts: 5.08 us -> 3.49 us
  transfers between devices with their start and end apart: 52 -> 52, of which waited for: 21 -> 21; matrix products, arithmetic and copies ran while one was open for 0% -> 0% of each run, Pallas kernels for 25% -> 26%
where the time goes in v7:
time: 195 us
  starting transfers between devices  75.7 us (39%)
  waiting for transfers between devices  57.6 us (30%)
  Pallas kernels  55.4 us (28%)
  local copies, waits for them, and re-layouts  4.66 us (2%)
    pallas_call x30, Pallas kernels, invoke(): pl.pallas_call(body, out_shape=out_shape, compiler_params=pltpu.CompilerP...  55.4 us
    ppermute x25, waiting for transfers between devices, ring(): return lax.ppermute(values, BOTH, ring_pairs(second, shift))  40.5 us
    ppermute x25, starting transfers between devices, ring(): return lax.ppermute(values, BOTH, ring_pairs(second, shift))  33 us
    ppermute x11, starting transfers between devices, swap_core(): return lax.ppermute(values, 'cmp', [(k, k ^ 1) for k in range(8)])  21.4 us
    ppermute x14, starting transfers between devices, send_z(): return lax.ppermute(values, 'cmp', pairs)  19.3 us
    ppermute x2, waiting for transfers between devices, swap_chip(): return lax.ppermute(values, 'cmp', [(k, k ^ 2) for k in range(8)])  8.17 us
    ppermute x14, waiting for transfers between devices, send_z(): return lax.ppermute(values, 'cmp', pairs)  5.18 us
  transfers between devices with their start and end apart: 52, of which 21 were waited for; matrix products, arithmetic and copies ran while one was open for 0% of the time, Pallas kernels for 26%

profile of v7, /device:TPU:1, one launch (start us, length us, event | category | flops | bytes accessed | tf_op | source)
XLA Modules:
  0.0 195.1 jit_solution(16655235291661819243)
XLA Ops:
  6.7 3.3 %collective-permute-start.1 = (bf16[2,2,32,512]{3,2,1,0:T(8,128)(2,1)S(1)}, bf16[2,2,32,512]{3,2,1,0:T(8,128)(2,1)S(1)}, u32[]{:S(2)}, u32[]{:S(2)}) collective-permute-start(bf16[2,2,32,512]{3,2,1,0:T(8,128)(2,1)S(1)} %get-tuple-element.81), channel_id=1, source_target_pairs={{0,4},{1,5},{2,6},{3,7},{4,0},{5,1},{6,2},{7,3},{8,12},{9,13},{10,... | collective-permute-start | bytes 393224 | tf_op jit(solution)/shard_map/rows_z_2/ppermute | solution.py:37
  12.0 3.7 %collective-permute-done.1.refs_3_ = bf16[2,2,32,512]{3,2,1,0:T(8,128)(2,1)S(1)} collective-permute-done((bf16[2,2,32,512]{3,2,1,0:T(8,128)(2,1)S(1)}, bf16[2,2,32,512]{3,2,1,0:T(8,128)(2,1)S(1)}, u32[]{:S(2)}, u32[]{:S(2)}) %collective-permute-start.1) | collective-permute-done | bytes 131104 | tf_op jit(solution)/shard_map/rows_z_2/ppermute | solution.py:37
  24.9 2.8 %copy-done.1 = bf16[4096,2,3,128]{3,1,2,0:T(2,128)(2,1)S(1)} copy-done((bf16[4096,2,3,128]{3,1,2,0:T(2,128)(2,1)S(1)}, bf16[4096,2,3,128]{3,1,2,0:T(2,128)(2,1)}, u32[]{:S(2)}) %copy-start.1) | copy-done | bytes 6291480
  30.0 6.5 %collective-permute-done.5.refs_2_ = bf16[32,8320]{1,0:T(8,128)(2,1)S(1)} collective-permute-done((bf16[32,8320]{1,0:T(8,128)(2,1)S(1)}, bf16[32,8320]{1,0:T(8,128)(2,1)S(1)}, u32[]{:S(2)}, u32[]{:S(2)}) %collective-permute-start.5) | collective-permute-done | bytes 532512 | tf_op jit(solution)/shard_map/rows_first_2/ppermute | solution.py:31
  40.8 5.6 %collective-permute-done.10.refs_7_.refs_8_.refs_13_ = bf16[64,4224]{1,0:T(8,128)(2,1)S(1)} collective-permute-done((bf16[64,4224]{1,0:T(8,128)(2,1)S(1)}, bf16[64,4224]{1,0:T(8,128)(2,1)S(1)}, u32[]{:S(2)}, u32[]{:S(2)}) %collective-permute-start.10) | collective-permute-done | bytes 540704 | tf_op jit(solution)/shard_map/x_1_second_3/ppermute | solution.py:31
  49.0 2.8 %collective-permute-done.8.refs_5_.refs_3_.refs_4_.refs_9_ = bf16[64,4224]{1,0:T(8,128)(2,1)S(1)} collective-permute-done((bf16[64,4224]{1,0:T(8,128)(2,1)S(1)}, bf16[64,4224]{1,0:T(8,128)(2,1)S(1)}, u32[]{:S(2)}, u32[]{:S(2)}) %collective-permute-start.8) | collective-permute-done | bytes 540704 | tf_op jit(solution)/shard_map/x_2_second_1/ppermute | solution.py:31
  55.0 2.9 %collective-permute-done.11.refs_5_.refs_6_.refs_11_ = bf16[64,4224]{1,0:T(8,128)(2,1)S(1)} collective-permute-done((bf16[64,4224]{1,0:T(8,128)(2,1)S(1)}, bf16[64,4224]{1,0:T(8,128)(2,1)S(1)}, u32[]{:S(2)}, u32[]{:S(2)}) %collective-permute-start.11) | collective-permute-done | bytes 540704 | tf_op jit(solution)/shard_map/x_far_second_3/ppermute | solution.py:31
  57.9 5.3 %project.1 = (bf16[512,256]{1,0:T(8,128)(2,1)S(1)}, bf16[528,512]{1,0:T(8,128)(2,1)S(1)}, f32[512,384]{1,0:T(8,128)S(1)}) custom-call(bf16[64,4224]{1,0:T(8,128)(2,1)S(1)} %get-tuple-element.85.refs_4_.refs_0_.refs_1_.refs_6_, bf16[64,4224]{1,0:T(8,128)(2,1)S(1)} %get-tuple-element.86.refs_1_.refs_2_.refs_7_, ...), custom_call_target="tpu_custom_call" | custom-call | flops 1 | bytes 1 | tf_op jit(solution)/shard_map/project/pallas_call | solution.py:78
  66.7 8.2 %collective-permute-done.14.refs_3_.refs_1_ = bf16[528,512]{1,0:T(8,128)(2,1)S(1)} collective-permute-done((bf16[528,512]{1,0:T(8,128)(2,1)S(1)}, bf16[528,512]{1,0:T(8,128)(2,1)S(1)}, u32[]{:S(2)}, u32[]{:S(2)}) %collective-permute-start.14) | collective-permute-done | bytes 540704 | tf_op jit(solution)/shard_map/pair_chip/ppermute | solution.py:47
  74.9 3.1 %collective-permute-start.15 = (bf16[528,512]{1,0:T(8,128)(2,1)S(1)}, bf16[528,512]{1,0:T(8,128)(2,1)S(1)}, u32[]{:S(2)}, u32[]{:S(2)}) collective-permute-start(bf16[528,512]{1,0:T(8,128)(2,1)S(1)} %collective-permute-done.14.refs_3_.refs_1_), channel_id=1, source_target_pairs={{0,1},{1,0},{2,3},{3,2},{4,5},{5,4},{6,7},{7,6},{8,9},{9,8},{10,11... | collective-permute-start | bytes 1622024 | tf_op jit(solution)/shard_map/far_pair_core/ppermute | solution.py:42
  81.1 6.4 %attention_forward.1 = (bf16[512,256]{1,0:T(8,128)(2,1)S(1)}, bf16[2,512,2048]{2,1,0:T(8,128)(2,1)S(1)}) custom-call(bf16[512,256]{1,0:T(8,128)(2,1)S(1)} %get-tuple-element.87.refs_2_.refs_0_, bf16[528,512]{1,0:T(8,128)(2,1)S(1)} %get-tuple-element.88.refs_1_, bf16[528,512]{1,0:T(8,128)(2,1)S(1)} %collective-permute-done.13.refs_2_, ...), custom_call_target="tpu_custom_call" | custom-call | flops 1 | bytes 1 | tf_op jit(solution)/shard_map/attention_forward/pallas_call | solution.py:78
  104.3 4.8 %query_weights.1 = (bf16[4,512,512]{2,1,0:T(8,128)(2,1)S(1)}, bf16[512,512]{1,0:T(8,128)(2,1)S(1)}, bf16[3,512,512]{2,1,0:T(8,128)(2,1)S(1)}) custom-call(s32[2]{0:T(128)S(1)} %pad_add_fusion.refs_0_.refs_5_, bf16[64,4224]{1,0:T(8,128)(2,1)S(1)} %get-tuple-element.85.refs_4_.refs_0_.refs_1_.refs_6_, ...), custom_call_target="tpu_custom_call" | custom-call | flops 1 | bytes 1 | tf_op jit(solution)/shard_map/query_weights/pallas_call | solution.py:78
  112.0 6.2 %feature_parts.1 = (bf16[512,768]{1,0:T(8,128)(2,1)}, bf16[512,512]{1,0:T(8,128)(2,1)S(1)}, bf16[128,4224]{1,0:T(8,128)(2,1)S(1)}, bf16[128,4224]{1,0:T(8,128)(2...) custom-call(bf16[512,512]{1,0:T(8,128)(2,1)S(1)} %get-tuple-element.99.refs_0_, ...), custom_call_target="tpu_custom_call" | custom-call | flops 30000001024 | bytes 1 | tf_op jit(solution)/shard_map/feature_parts/pallas_call | solution.py:78
  124.7 3.1 %collective-permute-done.33.refs_1_ = bf16[64,4224]{1,0:T(8,128)(2,1)S(1)} collective-permute-done((bf16[64,4224]{1,0:T(8,128)(2,1)S(1)}, bf16[64,4224]{1,0:T(8,128)(2,1)S(1)}, u32[]{:S(2)}, u32[]{:S(2)}) %collective-permute-start.33) | collective-permute-done | bytes 540704 | tf_op jit(solution)/shard_map/grad_second_3/ppermute | solution.py:31
  129.1 3.2 %collective-permute-start.36 = (bf16[128,4224]{1,0:T(8,128)(2,1)S(1)}, bf16[128,4224]{1,0:T(8,128)(2,1)S(1)}, u32[]{:S(2)}, u32[]{:S(2)}) collective-permute-start(bf16[128,4224]{1,0:T(8,128)(2,1)S(1)} %get-tuple-element.124), channel_id=1, source_target_pairs={{0,96},{1,25},{2,98},{3,27},{4,100},{5,29},{6,102},{7,31},{8,104},... | collective-permute-start | bytes 3244040 | tf_op jit(solution)/shard_map/grad_second_1/ppermute | solution.py:31
  135.3 4.5 %key_weights.1 = (bf16[4,512,512]{2,1,0:T(8,128)(2,1)S(1)}, bf16[4,512,512]{2,1,0:T(8,128)(2,1)S(1)}) custom-call(s32[2]{0:T(128)S(1)} %pad_add_fusion.refs_0_.refs_5_, bf16[64,4224]{1,0:T(8,128)(2,1)S(1)} %get-tuple-element.85.refs_4_.refs_0_.refs_1_.refs_6_, bf16[64,4224]{1,0:T(8,128)(2,1)S(1)} %get-tuple-element.86.refs_1_.refs_2_.refs_7_, ...), custom_call_target="tpu_custom_call" | custom-call | flops 1 | bytes 1 | tf_op jit(solution)/shard_map/key_weights/pallas_call | solution.py:78
  139.8 2.8 %collective-permute-start.39 = (bf16[4,512,512]{2,1,0:T(8,128)(2,1)S(1)}, bf16[4,512,512]{2,1,0:T(8,128)(2,1)S(1)}, u32[]{:S(2)}, u32[]{:S(2)}) collective-permute-start(bf16[4,512,512]{2,1,0:T(8,128)(2,1)S(1)} %get-tuple-element.131), channel_id=1, source_target_pairs={{0,1},{1,0},{2,3},{3,2},{4,5},{5,4},{6,7},{7,6},{8,9},{9,8},{10,11... | collective-permute-start | bytes 6291464 | tf_op jit(solution)/shard_map/key_weights_core/ppermute | solution.py:42
  144.9 3.0 %collective-permute-done.35.refs_1_ = bf16[128,4224]{1,0:T(8,128)(2,1)S(1)} collective-permute-done((bf16[128,4224]{1,0:T(8,128)(2,1)S(1)}, bf16[128,4224]{1,0:T(8,128)(2,1)S(1)}, u32[]{:S(2)}, u32[]{:S(2)}) %collective-permute-start.35) | collective-permute-done | bytes 1081376 | tf_op jit(solution)/shard_map/grad_second_3/ppermute | solution.py:31
  148.6 3.1 %collective-permute-start.38 = (bf16[16,8320]{1,0:T(8,128)(2,1)S(1)}, bf16[16,8320]{1,0:T(8,128)(2,1)S(1)}, u32[]{:S(2)}, u32[]{:S(2)}) collective-permute-start(bf16[16,8320]{1,0:T(8,128)(2,1)S(1)} %get-tuple-element.130), channel_id=1, source_target_pairs={{0,24},{1,97},{2,26},{3,99},{4,28},{5,101},{6,30},{7,103},{8,0},{9... | collective-permute-start | bytes 798728 | tf_op jit(solution)/shard_map/sum_far_first_1/ppermute | solution.py:31
  152.0 3.1 %collective-permute-done.38.refs_3_ = bf16[16,8320]{1,0:T(8,128)(2,1)S(1)} collective-permute-done((bf16[16,8320]{1,0:T(8,128)(2,1)S(1)}, bf16[16,8320]{1,0:T(8,128)(2,1)S(1)}, u32[]{:S(2)}, u32[]{:S(2)}) %collective-permute-start.38) | collective-permute-done | bytes 266272 | tf_op jit(solution)/shard_map/sum_far_first_1/ppermute | solution.py:31
  155.1 3.1 %collective-permute-done.37.refs_1_ = bf16[16,8320]{1,0:T(8,128)(2,1)S(1)} collective-permute-done((bf16[16,8320]{1,0:T(8,128)(2,1)S(1)}, bf16[16,8320]{1,0:T(8,128)(2,1)S(1)}, u32[]{:S(2)}, u32[]{:S(2)}) %collective-permute-start.37) | collective-permute-done | bytes 266272 | tf_op jit(solution)/shard_map/sum_far_first_3/ppermute | solution.py:31
  161.5 5.3 %collective-permute-done.43.refs_3_ = bf16[32,8320]{1,0:T(8,128)(2,1)S(1)} collective-permute-done((bf16[32,8320]{1,0:T(8,128)(2,1)S(1)}, bf16[32,8320]{1,0:T(8,128)(2,1)S(1)}, u32[]{:S(2)}, u32[]{:S(2)}) %collective-permute-start.43) | collective-permute-done | bytes 532512 | tf_op jit(solution)/shard_map/sum_first_1/ppermute | solution.py:31
  177.3 8.8 %collective-permute-start.49 = (bf16[4,32,1152]{2,1,0:T(8,128)(2,1)S(1)}, bf16[4,32,1152]{2,1,0:T(8,128)(2,1)S(1)}, u32[]{:S(2)}, u32[]{:S(2)}) collective-permute-start(bf16[4,32,1152]{2,1,0:T(8,128)(2,1)S(1)} %get-tuple-element.145), channel_id=1, source_target_pairs={{0,1},{1,0},{2,3},{3,2},{4,5},{5,4},{6,7},{7,6},{8,9},{9,8},{10,11... | collective-permute-start | bytes 884744 | tf_op jit(solution)/shard_map/final_core/ppermute | solution.py:42
  187.3 5.0 %place_rows.1 = (bf16[2048,512]{1,0:T(8,128)(2,1)}, bf16[2048,512]{1,0:T(8,128)(2,1)}) custom-call(bf16[2048,512]{1,0:T(8,128)(2,1)S(1)} %get-tuple-element.121.refs_6_.refs_0_, bf16[2048,512]{1,0:T(8,128)(2,1)S(1)} %get-tuple-element.122.refs_1_, s32[2,1,128]{2,1,0:T(1,128)S(1)} %copy-done.7, bf16[4,32,1024]{2,1,0:T(8,128)(2,1)S(1)} %get-tuple-element.144.refs_3_, ...), custom_call_target="tpu_custom_call" | custom-call | flops 1 | bytes 1 | tf_op jit(solution)/shard_map/place_rows/pallas_call | solution.py:78
  (137 shorter events, 87.8 us)
Async XLA Ops:
  21.2 15.3 %collective-permute-start.5 = (bf16[32,8320]{1,0:T(8,128)(2,1)S(1)}, bf16[32,8320]{1,0:T(8,128)(2,1)S(1)}, u32[]{:S(2)}, u32[]{:S(2)}) collective-permute-start(bf16[32,8320]{1,0:T(8,128)(2,1)S(1)} %get-tuple-element.83.refs_0_), channel_id=1, source_target_pairs={{0,16},{1,65},{2,18},{3,67},{4,20},{5,69},{6,22},{7,71},{8,24},{9,... | collective-permute-start | bytes 1597448 | tf_op jit(solution)/shard_map/rows_first_2/ppermute | solution.py:31
  23.8 12.7 %collective-permute-start.4 = (bf16[32,8320]{1,0:T(8,128)(2,1)S(1)}, bf16[32,8320]{1,0:T(8,128)(2,1)S(1)}, u32[]{:S(2)}, u32[]{:S(2)}) collective-permute-start(bf16[32,8320]{1,0:T(8,128)(2,1)S(1)} %get-tuple-element.83.refs_0_), channel_id=1, source_target_pairs={{0,24},{1,97},{2,26},{3,99},{4,28},{5,101},{6,30},{7,103},{8,0},{9... | collective-permute-start | bytes 1597448 | tf_op jit(solution)/shard_map/rows_first_1/ppermute | solution.py:31
  39.3 12.5 %collective-permute-start.8 = (bf16[64,4224]{1,0:T(8,128)(2,1)S(1)}, bf16[64,4224]{1,0:T(8,128)(2,1)S(1)}, u32[]{:S(2)}, u32[]{:S(2)}) collective-permute-start(bf16[64,4224]{1,0:T(8,128)(2,1)S(1)} %get-tuple-element.86.refs_1_.refs_2_.refs_7_), channel_id=1, source_target_pairs={{0,96},{1,25},{2,98},{3,27},{4,100},{5,29},{6,102},{7,31},{8,104},... | collective-permute-start | bytes 1622024 | tf_op jit(solution)/shard_map/x_2_second_1/ppermute | solution.py:31
  40.3 11.9 %collective-permute-start.12 = (bf16[64,4224]{1,0:T(8,128)(2,1)S(1)}, bf16[64,4224]{1,0:T(8,128)(2,1)S(1)}, u32[]{:S(2)}, u32[]{:S(2)}) collective-permute-start(bf16[64,4224]{1,0:T(8,128)(2,1)S(1)} %get-tuple-element.85.refs_4_.refs_0_.refs_1_.refs_6_), channel_id=1, source_target_pairs={{0,32},{1,9},{2,34},{3,11},{4,36},{5,13},{6,38},{7,15},{8,40},{9,1... | collective-permute-start | bytes 1622024 | tf_op jit(solution)/shard_map/x_2_second_3/ppermute | solution.py:31
  52.2 25.8 %collective-permute-start.17 = (bf16[128,4096]{1,0:T(8,128)(2,1)S(1)}, bf16[128,4096]{1,0:T(8,128)(2,1)S(1)}, u32[]{:S(2)}, u32[]{:S(2)}) collective-permute-start(bf16[128,4096]{1,0:T(8,128)(2,1)S(1)} %stack_g.1.refs_11_.refs_0_.refs_9_), channel_id=1, source_target_pairs={{0,32},{1,9},{2,34},{3,11},{4,36},{5,13},{6,38},{7,15},{8,40},{9,1... | collective-permute-start | bytes 3145736 | tf_op jit(solution)/shard_map/g_second_3/ppermute | solution.py:31
  53.2 24.8 %collective-permute-start.16 = (bf16[128,4096]{1,0:T(8,128)(2,1)S(1)}, bf16[128,4096]{1,0:T(8,128)(2,1)S(1)}, u32[]{:S(2)}, u32[]{:S(2)}) collective-permute-start(bf16[128,4096]{1,0:T(8,128)(2,1)S(1)} %stack_g.1.refs_11_.refs_0_.refs_9_), channel_id=1, source_target_pairs={{0,96},{1,25},{2,98},{3,27},{4,100},{5,29},{6,102},{7,31},{8,104},... | collective-permute-start | bytes 3145736 | tf_op jit(solution)/shard_map/g_second_1/ppermute | solution.py:31
  64.2 16.8 %collective-permute-start.13 = (bf16[528,512]{1,0:T(8,128)(2,1)S(1)}, bf16[528,512]{1,0:T(8,128)(2,1)S(1)}, u32[]{:S(2)}, u32[]{:S(2)}) collective-permute-start(bf16[528,512]{1,0:T(8,128)(2,1)S(1)} %get-tuple-element.88.refs_1_), channel_id=1, source_target_pairs={{0,1},{1,0},{2,3},{3,2},{4,5},{5,4},{6,7},{7,6},{8,9},{9,8},{10,11... | collective-permute-start | bytes 1622024 | tf_op jit(solution)/shard_map/pair_core/ppermute | solution.py:42
  78.1 13.3 %collective-permute-start.19 = (bf16[64,4096]{1,0:T(8,128)(2,1)S(1)}, bf16[64,4096]{1,0:T(8,128)(2,1)S(1)}, u32[]{:S(2)}, u32[]{:S(2)}) collective-permute-start(bf16[64,4096]{1,0:T(8,128)(2,1)S(1)} %get-tuple-element.92), channel_id=1, source_target_pairs={{0,32},{1,9},{2,34},{3,11},{4,36},{5,13},{6,38},{7,15},{8,40},{9,1... | collective-permute-start | bytes 1572872 | tf_op jit(solution)/shard_map/g_far_second_3/ppermute | solution.py:31
  79.0 12.4 %collective-permute-start.18 = (bf16[64,4096]{1,0:T(8,128)(2,1)S(1)}, bf16[64,4096]{1,0:T(8,128)(2,1)S(1)}, u32[]{:S(2)}, u32[]{:S(2)}) collective-permute-start(bf16[64,4096]{1,0:T(8,128)(2,1)S(1)} %get-tuple-element.90.refs_6_), channel_id=1, source_target_pairs={{0,96},{1,25},{2,98},{3,27},{4,100},{5,29},{6,102},{7,31},{8,104},... | collective-permute-start | bytes 1572872 | tf_op jit(solution)/shard_map/g_far_second_1/ppermute | solution.py:31
  89.9 13.2 %collective-permute-start.26 = (bf16[64,4096]{1,0:T(8,128)(2,1)S(1)}, bf16[64,4096]{1,0:T(8,128)(2,1)S(1)}, u32[]{:S(2)}, u32[]{:S(2)}) collective-permute-start(bf16[64,4096]{1,0:T(8,128)(2,1)S(1)} %get-tuple-element.105), channel_id=1, source_target_pairs={{0,96},{1,25},{2,98},{3,27},{4,100},{5,29},{6,102},{7,31},{8,104},... | collective-permute-start | bytes 1572872 | tf_op jit(solution)/shard_map/out_second_1/ppermute | solution.py:31
  91.2 12.0 %collective-permute-start.25 = (bf16[64,4096]{1,0:T(8,128)(2,1)S(1)}, bf16[64,4096]{1,0:T(8,128)(2,1)S(1)}, u32[]{:S(2)}, u32[]{:S(2)}) collective-permute-start(bf16[64,4096]{1,0:T(8,128)(2,1)S(1)} %get-tuple-element.94.refs_6_), channel_id=1, source_target_pairs={{0,32},{1,9},{2,34},{3,11},{4,36},{5,13},{6,38},{7,15},{8,40},{9,1... | collective-permute-start | bytes 1572872 | tf_op jit(solution)/shard_map/out_second_3/ppermute | solution.py:31
  98.6 13.3 %collective-permute-start.24 = (bf16[512,512]{1,0:T(8,128)(2,1)S(1)}, bf16[512,512]{1,0:T(8,128)(2,1)S(1)}, u32[]{:S(2)}, u32[]{:S(2)}) collective-permute-start(bf16[512,512]{1,0:T(8,128)(2,1)S(1)} %chip_sum.1.refs_8_), channel_id=1, source_target_pairs={{0,2},{1,3},{2,0},{3,1},{4,6},{5,7},{6,4},{7,5},{8,10},{9,11},{10,... | collective-permute-start | bytes 1572872 | tf_op jit(solution)/shard_map/key_grads_chip/ppermute | solution.py:47
  103.3 19.9 %collective-permute-start.29 = (bf16[128,4096]{1,0:T(8,128)(2,1)S(1)}, bf16[128,4096]{1,0:T(8,128)(2,1)S(1)}, u32[]{:S(2)}, u32[]{:S(2)}) collective-permute-start(bf16[128,4096]{1,0:T(8,128)(2,1)S(1)} %get-tuple-element.106.refs_16_), channel_id=1, source_target_pairs={{0,32},{1,9},{2,34},{3,11},{4,36},{5,13},{6,38},{7,15},{8,40},{9,1... | collective-permute-start | bytes 3145736 | tf_op jit(solution)/shard_map/out_second_3/ppermute | solution.py:31
  109.1 14.0 %collective-permute-start.30 = (bf16[128,4096]{1,0:T(8,128)(2,1)S(1)}, bf16[128,4096]{1,0:T(8,128)(2,1)S(1)}, u32[]{:S(2)}, u32[]{:S(2)}) collective-permute-start(bf16[128,4096]{1,0:T(8,128)(2,1)S(1)} %get-tuple-element.111), channel_id=1, source_target_pairs={{0,96},{1,25},{2,98},{3,27},{4,100},{5,29},{6,102},{7,31},{8,104},... | collective-permute-start | bytes 3145736 | tf_op jit(solution)/shard_map/out_second_1/ppermute | solution.py:31
  111.3 21.0 %collective-permute-start.27 = (bf16[3,512,512]{2,1,0:T(8,128)(2,1)S(1)}, bf16[3,512,512]{2,1,0:T(8,128)(2,1)S(1)}, u32[]{:S(2)}, u32[]{:S(2)}) collective-permute-start(bf16[3,512,512]{2,1,0:T(8,128)(2,1)S(1)} %get-tuple-element.110), channel_id=1, source_target_pairs={{0,1},{1,0},{2,3},{3,2},{4,5},{5,4},{6,7},{7,6},{8,9},{9,8},{10,11... | collective-permute-start | bytes 4718600 | tf_op jit(solution)/shard_map/query_weights_core/ppermute | solution.py:42
  129.1 15.7 %collective-permute-start.36 = (bf16[128,4224]{1,0:T(8,128)(2,1)S(1)}, bf16[128,4224]{1,0:T(8,128)(2,1)S(1)}, u32[]{:S(2)}, u32[]{:S(2)}) collective-permute-start(bf16[128,4224]{1,0:T(8,128)(2,1)S(1)} %get-tuple-element.124), channel_id=1, source_target_pairs={{0,96},{1,25},{2,98},{3,27},{4,100},{5,29},{6,102},{7,31},{8,104},... | collective-permute-start | bytes 3244040 | tf_op jit(solution)/shard_map/grad_second_1/ppermute | solution.py:31
  132.4 15.5 %collective-permute-start.35 = (bf16[128,4224]{1,0:T(8,128)(2,1)S(1)}, bf16[128,4224]{1,0:T(8,128)(2,1)S(1)}, u32[]{:S(2)}, u32[]{:S(2)}) collective-permute-start(bf16[128,4224]{1,0:T(8,128)(2,1)S(1)} %get-tuple-element.118.refs_4_), channel_id=1, source_target_pairs={{0,32},{1,9},{2,34},{3,11},{4,36},{5,13},{6,38},{7,15},{8,40},{9,1... | collective-permute-start | bytes 3244040 | tf_op jit(solution)/shard_map/grad_second_3/ppermute | solution.py:31
  132.6 19.2 %collective-permute-start.40 = (bf16[512,512]{1,0:T(8,128)(2,1)S(1)}, bf16[512,512]{1,0:T(8,128)(2,1)S(1)}, u32[]{:S(2)}, u32[]{:S(2)}) collective-permute-start(bf16[512,512]{1,0:T(8,128)(2,1)S(1)} %get-tuple-element.132), channel_id=1, source_target_pairs={{0,2},{1,3},{2,4},{3,5},{4,6},{5,7},{6,0},{7,1},{8,10},{9,11},{10,... | collective-permute-start | bytes 1572872 | tf_op jit(solution)/shard_map/query_weights_z_1/ppermute | solution.py:37
  133.3 18.4 %collective-permute-start.41 = (bf16[512,512]{1,0:T(8,128)(2,1)S(1)}, bf16[512,512]{1,0:T(8,128)(2,1)S(1)}, u32[]{:S(2)}, u32[]{:S(2)}) collective-permute-start(bf16[512,512]{1,0:T(8,128)(2,1)S(1)} %get-tuple-element.133), channel_id=1, source_target_pairs={{0,6},{1,7},{2,0},{3,1},{4,2},{5,3},{6,4},{7,5},{8,14},{9,15},{10,... | collective-permute-start | bytes 1572872 | tf_op jit(solution)/shard_map/query_weights_z_3/ppermute | solution.py:37
  139.8 11.9 %collective-permute-start.39 = (bf16[4,512,512]{2,1,0:T(8,128)(2,1)S(1)}, bf16[4,512,512]{2,1,0:T(8,128)(2,1)S(1)}, u32[]{:S(2)}, u32[]{:S(2)}) collective-permute-start(bf16[4,512,512]{2,1,0:T(8,128)(2,1)S(1)} %get-tuple-element.131), channel_id=1, source_target_pairs={{0,1},{1,0},{2,3},{3,2},{4,5},{5,4},{6,7},{7,6},{8,9},{9,8},{10,11... | collective-permute-start | bytes 6291464 | tf_op jit(solution)/shard_map/key_weights_core/ppermute | solution.py:42
  159.8 13.6 %collective-permute-start.48 = (bf16[256,512]{1,0:T(8,128)(2,1)S(1)}, bf16[256,512]{1,0:T(8,128)(2,1)S(1)}, u32[]{:S(2)}, u32[]{:S(2)}) collective-permute-start(bf16[256,512]{1,0:T(8,128)(2,1)S(1)} %get-tuple-element.142), channel_id=1, source_target_pairs={{0,6},{1,7},{2,0},{3,1},{4,2},{5,3},{6,4},{7,5},{8,14},{9,15},{10,... | collective-permute-start | bytes 786440 | tf_op jit(solution)/shard_map/key_weights_far_z_3/ppermute | solution.py:37
  161.5 12.0 %collective-permute-start.47 = (bf16[256,512]{1,0:T(8,128)(2,1)S(1)}, bf16[256,512]{1,0:T(8,128)(2,1)S(1)}, u32[]{:S(2)}, u32[]{:S(2)}) collective-permute-start(bf16[256,512]{1,0:T(8,128)(2,1)S(1)} %get-tuple-element.134.refs_4_), channel_id=1, source_target_pairs={{0,2},{1,3},{2,4},{3,5},{4,6},{5,7},{6,0},{7,1},{8,10},{9,11},{10,... | collective-permute-start | bytes 786440 | tf_op jit(solution)/shard_map/key_weights_far_z_1/ppermute | solution.py:37
  173.6 19.2 %collective-permute-start.50 = (bf16[512,512]{1,0:T(8,128)(2,1)S(1)}, bf16[512,512]{1,0:T(8,128)(2,1)S(1)}, u32[]{:S(2)}, u32[]{:S(2)}) collective-permute-start(bf16[512,512]{1,0:T(8,128)(2,1)S(1)} %get-tuple-element.149), channel_id=1, source_target_pairs={{0,2},{1,3},{2,4},{3,5},{4,6},{5,7},{6,0},{7,1},{8,10},{9,11},{10,... | collective-permute-start | bytes 1572872 | tf_op jit(solution)/shard_map/key_weights_z_1/ppermute | solution.py:37
  173.8 19.0 %collective-permute-start.51 = (bf16[512,512]{1,0:T(8,128)(2,1)S(1)}, bf16[512,512]{1,0:T(8,128)(2,1)S(1)}, u32[]{:S(2)}, u32[]{:S(2)}) collective-permute-start(bf16[512,512]{1,0:T(8,128)(2,1)S(1)} %get-tuple-element.150), channel_id=1, source_target_pairs={{0,6},{1,7},{2,0},{3,1},{4,2},{5,3},{6,4},{7,5},{8,14},{9,15},{10,... | collective-permute-start | bytes 1572872 | tf_op jit(solution)/shard_map/key_weights_z_3/ppermute | solution.py:37
  (37 other events, 327.0 us)
